TPU v7x, 32 devices: a whole 2x2x4 slice. The times are simulated.
32 devices in a mesh: expert: 16 (over z, x, core), tensor: 2 (over y).
Axes of the slice: x: 2, y: 2, z: 4, core: 2. Of those that a mesh axis runs over, the one named last changes fastest.
Arguments:
- hidden: bfloat16 [16, 128, 2048], P('expert'), may hold values from -6 to 6
- down_weight: bfloat16 [16, 2048, 7168], P('expert', None, 'tensor'), may hold values from -0.125 to 0.125
- expert_ids: int32 [256, 8], P('expert'), may hold values from 0 to 15, as said below
- gate_weights: float32 [256, 8], P('expert'), may hold values from 0.1 to 0.6
- residual: bfloat16 [256, 7168], P('expert', 'tensor'), may hold values from -36 to 36
- norm_gain: float32 [7168], replicated, may hold values from 0.1 to 1.9
- proj_weight: bfloat16 [7168, 2112], P(None, 'tensor'), may hold values from -0.0625 to 0.0625
Outputs:
- stream: bfloat16 [256, 7168], P('expert', 'tensor')
- latents: bfloat16 [256, 2112], P('expert', 'tensor')
Inputs may be any that keep to these rules, and one draw needn't show every extreme that they name: `expert_ids`: experts 4 g to 4 g + 3 form node group g. Each token names 8 different experts, two in each of exactly 4 node groups. Within each aligned block of 16 tokens no expert is named by more than 8 tokens and no node group is used by more than 16 tokens; in every block some node group is used by exactly 16 tokens and each of its experts is named by exactly 8.
All inputs are finite; a program needn't handle non-finite values.
Results may differ from a plain program's by a relative error of at most 0.014.
Values may be sent and summed in bfloat16 or wider, within the bound.
No kernel may reach another device: no remote copies, remote signals or barrier semaphores. Data moves between devices by JAX's collectives and lax.ppermute only.
A program may use at most 64 MiB of HBM per device.

v0:
```python
import jax
import jax.numpy as jnp
from jax import lax
from jax.sharding import PartitionSpec as P

D = 7168
NODE_SIZE = 4


epsilon = 1e-06


def on_device(hidden, down_weight, expert_ids, gate_weights, residual, norm_gain, proj_weight):
    devices = lax.axis_size("expert")
    local_experts = hidden.shape[0]
    capacity = hidden.shape[1] // devices
    columns = down_weight.shape[2]
    experts = local_experts * devices
    group_count = experts // NODE_SIZE
    outputs = jnp.einsum(
        "xsf,xfd->xsd", hidden, down_weight, preferred_element_type=jnp.float32
    ).astype(jnp.bfloat16)
    grouped = outputs.reshape(local_experts, devices, capacity, columns)
    returned = lax.all_to_all(grouped, "expert", split_axis=1, concat_axis=0, tiled=True)
    returned = returned.reshape(experts * capacity, columns)
    expert_range = jnp.arange(experts, dtype=jnp.int32)
    counts = jnp.sum((expert_ids[:, :, None] == expert_range).astype(jnp.int32), axis=1)
    before = jnp.cumsum(counts, axis=0) - counts
    slot_index = jnp.take_along_axis(before, expert_ids, axis=1)
    flat_rows = expert_ids * capacity + slot_index
    picked = returned[flat_rows]
    gated = gate_weights[:, :, None] * picked.astype(jnp.float32)
    membership = (
        expert_ids[:, :, None] // NODE_SIZE == jnp.arange(group_count, dtype=jnp.int32)
    ).astype(jnp.float32)
    group_sums = jnp.einsum("tkg,tkd->tgd", membership, gated, precision=lax.Precision.HIGHEST)
    group_parts = lax.optimization_barrier(group_sums.astype(jnp.bfloat16))
    summed = residual.astype(jnp.float32) + jnp.sum(group_parts.astype(jnp.float32), axis=1)
    stream = summed.astype(jnp.bfloat16)
    section_wide = lax.all_gather(stream, "tensor", axis=1, tiled=True).astype(jnp.float32)
    normed_part = (section_wide * norm_gain).astype(jnp.bfloat16)
    added = jnp.dot(normed_part, proj_weight, preferred_element_type=jnp.float32)
    energy = jnp.sum(section_wide * section_wide, axis=1)
    inverse = lax.rsqrt(energy / D + epsilon)
    latents = (added * inverse[:, None]).astype(jnp.bfloat16)
    return (stream, latents)


def solution(mesh):
    return jax.shard_map(
        on_device,
        mesh=mesh,
        in_specs=(
            P("expert", None, None),
            P("expert", None, "tensor"),
            P("expert", None),
            P("expert", None),
            P("expert", "tensor"),
            P(),
            P(None, "tensor"),
        ),
        out_specs=(P("expert", "tensor"), P("expert", "tensor")),
        check_vma=False,
    )
```

profile of v0, /device:TPU:0, one launch (start us, length us, event | category | flops | bytes accessed | tf_op | source)
XLA Modules:
  0.0 57.4 jit_solution(2573537923528756667)
XLA Ops:
  0.6 0.0 copy-start
  0.6 0.0 copy-start.3
  0.7 0.0 copy-start.5
  0.7 1.0 %copy-done = bf16[1,128,2048]{2,1,0:T(8,128)(2,1)S(1)} copy-done((bf16[1,128,2048]{2,1,0:T(8,128)(2,1)S(1)}, bf16[1,128,2048]{2,1,0:T(8,128)(2,1)}, u32[]{:S(2)}) %copy-start) | copy-done | bytes 524312
  1.7 8.2 %fusion.5 = bf16[1,16,8,3584]{3,2,0,1:T(8,128)(2,1)} fusion(bf16[1,2048,3584]{2,1,0:T(8,128)(2,1)} %param.8, bf16[1,128,2048]{2,1,0:T(8,128)(2,1)S(1)} %copy-done), kind=kOutput, calls=%fused_computation.5 | convolution fusion | flops 1879506944 | bytes 16121856 | tf_op jit(solution)/shard_map/xsf,xfd->xsd/dot_general | solution.py:20
  9.9 0.0 copy-start.2
  9.9 0.0 copy-start.4
  9.9 7.5 %all-to-all-start = ((bf16[1,16,8,3584]{3,2,0,1:T(8,128)(2,1)}), bf16[1,16,8,3584]{3,2,0,1:T(8,128)(2,1)S(1)}, u32[]{:S(2)}, u32[]{:S(2)}) async-start(bf16[1,16,8,3584]{3,2,0,1:T(8,128)(2,1)} %fusion.5), calls=%async_computation | async-start | bytes 1835008 | tf_op jit(solution)/shard_map/all_to_all | solution.py:24
  17.4 0.0 copy-done.3
  17.4 0.1 copy.31
  17.4 0.1 convert_reduce_fusion.1
  17.6 0.1 copy.32
  17.7 0.1 reshape.72
  17.8 1.3 %gather_fusion.1 = s32[128]{0:T(128)S(1)} fusion(s32[16,16]{1,0:T(8,128)S(1)} %sub.10, s32[128]{0:T(128)S(1)} %reshape.72), kind=kCustom, calls=%fused_computation.1 | custom fusion | bytes 2048 | tf_op jit(solution)/shard_map/jit(take_along_axis)/gather | solution.py:29
  19.0 0.1 reshape.75
  19.1 0.1 copy.33
  19.2 0.1 copy.34
  19.3 0.1 reshape.66
  19.4 0.0 copy-done.5
  19.4 0.1 copy.29
  19.5 0.1 copy.28
  19.5 18.6 %all-to-all-done = bf16[1,16,8,3584]{3,2,0,1:T(8,128)(2,1)S(1)} async-done(((bf16[1,16,8,3584]{3,2,0,1:T(8,128)(2,1)}), bf16[1,16,8,3584]{3,2,0,1:T(8,128)(2,1)S(1)}, u32[]{:S(2)}, u32[]{:S(2)}) %all-to-all-start) | async-done | bytes 917536 | tf_op jit(solution)/shard_map/all_to_all | solution.py:24
  38.2 1.1 %gather_fusion = bf16[128,3584]{1,0:T(8,128)(2,1)S(1)} fusion(bf16[128,3584]{1,0:T(8,128)(2,1)S(1)} %bitcast.26, s32[1024]{0:T(1024)S(1)} %pad_clamp_fusion), kind=kCustom, calls=%fused_computation | custom fusion | bytes 1835520 | tf_op jit(solution)/shard_map/gather | solution.py:31
  39.3 1.1 %convolution_convert_fusion = bf16[16,4,3584]{2,1,0:T(4,128)(2,1)S(1)} fusion(bf16[128,3584]{1,0:T(8,128)(2,1)S(1)} %gather_fusion, f32[16,8]{1,0:T(8,128)S(1)} %copy.29, s32[16,8]{1,0:T(8,128)S(1)} %copy.28), kind=kOutput, calls=%fused_computation.6 | convolution fusion | flops 23167488 | bytes 1377280 | tf_op jit(solution)/shard_map/tkg,tkd->tgd/dot_general | solution.py:36
  40.4 0.6 %convert_reduce_fusion = f32[16,3584]{1,0:T(8,128)S(1)} fusion(bf16[16,4,3584]{2,1,0:T(4,128)(2,1)S(1)} %convolution_convert_fusion), kind=kLoop, calls=%fused_computation.11 | loop fusion | flops 401408 | bytes 688128 | tf_op jit(solution)/shard_map/reduce_sum | solution.py:38
  41.0 0.0 copy-done.2
  41.1 0.0 copy-start.1
  41.1 6.2 %all_gather.3 = bf16[16,7168]{1,0:T(8,128)(2,1)S(1)} all-gather(bf16[16,3584]{1,0:T(8,128)(2,1)S(1)} %add_convert_fusion), channel_id=1, replica_groups=mesh['expert'=16,'tensor'=2] {'tensor'}, dimensions={1}, use_global_device_ids=true | all-gather | bytes 344064 | tf_op jit(solution)/shard_map/all_gather | solution.py:40
  47.3 0.2 fusion.13
  47.4 0.0 copy-done.4
  47.4 10.0 %fusion.8 = bf16[16,1056]{1,0:T(8,128)(2,1)} fusion(bf16[7168,1056]{0,1:T(8,128)(2,1)} %param.13, bf16[16,7168]{1,0:T(8,128)(2,1)S(1)} %all_gather.3, f32[7168]{0:T(1024)S(1)} %copy-done.4, f32[16]{0:T(128)S(1)} %add_rsqrt_fusion), kind=kOutput, calls=%fused_computation.8 | convolution fusion | flops 242598912 | bytes 15430720 | tf_op jit(solution)/shard_map/dot_general | solution.py:42
  57.4 0.0 copy-done.1
  (7 shorter events, 0.1 us)
Async XLA Ops:
  0.6 1.0 %copy-start = (bf16[1,128,2048]{2,1,0:T(8,128)(2,1)S(1)}, bf16[1,128,2048]{2,1,0:T(8,128)(2,1)}, u32[]{:S(2)}) copy-start(bf16[1,128,2048]{2,1,0:T(8,128)(2,1)} %param.7) | copy-start | bytes 1572868
  0.6 16.7 %copy-start.3 = (s32[16,8]{0,1:T(8,128)S(1)}, s32[16,8]{0,1:T(8,128)}, u32[]{:S(2)}) copy-start(s32[16,8]{0,1:T(8,128)} %param.9) | copy-start | bytes 1540
  0.7 18.7 %copy-start.5 = (f32[16,8]{0,1:T(8,128)S(1)}, f32[16,8]{0,1:T(8,128)}, u32[]{:S(2)}) copy-start(f32[16,8]{0,1:T(8,128)} %param.10) | copy-start | bytes 1540
  9.9 31.2 %copy-start.2 = (bf16[16,3584]{1,0:T(8,128)(2,1)S(1)}, bf16[16,3584]{1,0:T(8,128)(2,1)}, u32[]{:S(2)}) copy-start(bf16[16,3584]{1,0:T(8,128)(2,1)} %param.11) | copy-start | bytes 344068
  9.9 37.6 %copy-start.4 = (f32[7168]{0:T(1024)S(1)}, f32[7168]{0:T(1024)}, u32[]{:S(2)}) copy-start(f32[7168]{0:T(1024)} %param.12) | copy-start | bytes 86020
  9.9 28.3 %all-to-all-start = ((bf16[1,16,8,3584]{3,2,0,1:T(8,128)(2,1)}), bf16[1,16,8,3584]{3,2,0,1:T(8,128)(2,1)S(1)}, u32[]{:S(2)}, u32[]{:S(2)}) async-start(bf16[1,16,8,3584]{3,2,0,1:T(8,128)(2,1)} %fusion.5), calls=%async_computation | async-start | bytes 1835008 | tf_op jit(solution)/shard_map/all_to_all | solution.py:24
  41.1 16.3 %copy-start.1 = (bf16[16,3584]{1,0:T(8,128)(2,1)}, bf16[16,3584]{1,0:T(8,128)(2,1)S(1)}, u32[]{:S(2)}) copy-start(bf16[16,3584]{1,0:T(8,128)(2,1)S(1)} %add_convert_fusion) | copy-start | bytes 344068
where the time goes:
time: 57.8 us; the launch traced here: 57.4 us
  matrix products  19.3 us (33%)
  waiting for transfers between devices  18.6 us (32%)
  starting transfers between devices  7.49 us (13%)
  blocking collectives  6.16 us (11%)
  local copies, waits for them, and re-layouts  4.11 us (7%)
  other arithmetic  0.97 us (2%)
  between operations  0.77 us (1%)
    all_to_all x1, waiting for transfers between devices, on_device(): lax.all_to_all(grouped, 'expert', split_axis=1, concat_axis=0, tiled=True)  18.6 us
    dot_general x1, matrix products, on_device(): jnp.dot(normed_part, proj_weight, preferred_element_type=jnp.float32)  9.95 us
    dot_general x1, matrix products, on_device(): jnp.einsum('xsf,xfd->xsd', hidden, down_weight, preferred_element_type=jn...  8.18 us
    all_to_all x1, starting transfers between devices, on_device(): lax.all_to_all(grouped, 'expert', split_axis=1, concat_axis=0, tiled=True)  7.49 us
    all_gather x1, blocking collectives, on_device(): lax.all_gather(stream, 'tensor', axis=1, tiled=True).astype(jnp.float32)  6.16 us
    gather x5, local copies, waits for them, and re-layouts, on_device(): slot_index = jnp.take_along_axis(before, expert_ids, axis=1)  1.58 us
    unnamed x14, local copies, waits for them, and re-layouts  1.19 us
  transfers between devices with their start and end apart: 1, of which 1 were waited for; matrix products, arithmetic and copies ran while one was open for 4% of the time, Pallas kernels for 0%

commit v1 on v0

v1 whole, which is shorter than its diff:
```python
import functools

import jax
import jax.numpy as jnp
from jax import lax
from jax.experimental import pallas as pl
from jax.experimental.pallas import tpu as pltpu
from jax.sharding import PartitionSpec as P

NODE_SIZE = 4
LANES = 128
MIB = 1 << 20


epsilon = 1e-06

VMEM = pl.BlockSpec(memory_space=pltpu.VMEM)
SMEM = pl.BlockSpec(memory_space=pltpu.SMEM)
ANY = pl.BlockSpec(memory_space=pl.ANY)
HBM = pl.BlockSpec(memory_space=pltpu.HBM)


def shape_of(shape, dtype):
    return jax.ShapeDtypeStruct(shape, dtype)


def cut(columns):
    tiles = columns // LANES
    if columns % LANES or tiles < 8:
        return [(0, columns)]
    first = tiles // 2 * LANES
    return [(0, first), (first, columns - first)]


def block_width(width):
    for tiles in (2, 3, 1):
        if width % (tiles * LANES) == 0:
            return tiles * LANES
    return width


def routing(index, experts, capacity, ids, gates):
    groups = experts // NODE_SIZE
    slots = experts * capacity
    tokens = ids.shape[1]
    row = lax.broadcasted_iota(jnp.int32, (slots, tokens), 0)
    slot = row % capacity
    group = row // capacity % groups
    member = row // (capacity * groups)
    expert = index ^ (group * NODE_SIZE + member)
    named = jnp.zeros((slots, tokens), jnp.float32)
    gate = jnp.zeros((slots, tokens), jnp.float32)
    for k in range(ids.shape[0]):
        hit = ids[k : k + 1, :] == expert
        named = named + jnp.where(hit, 1.0, 0.0)
        gate = gate + jnp.where(hit, gates[k : k + 1, :], 0.0)
    earlier = lax.broadcasted_iota(jnp.int32, (tokens, tokens), 0) < lax.broadcasted_iota(
        jnp.int32, (tokens, tokens), 1
    )
    before = jnp.dot(named, jnp.where(earlier, 1.0, 0.0), preferred_element_type=jnp.float32)
    full = jnp.where(before == slot.astype(jnp.float32), gate, 0.0)
    return [jnp.where(group == d, full, 0.0).T for d in range(groups)]


def down_kernel(experts, first, width, block, with_routing, *refs):
    if with_routing:
        index_ref, hidden_ref, weight_ref, ids_ref, gates_ref = refs[:5]
        rest = refs[5:]
    else:
        index_ref, hidden_ref, weight_ref = refs[:3]
        rest = refs[3:]
    out_refs, rest = rest[:NODE_SIZE], rest[NODE_SIZE:]
    groups = experts // NODE_SIZE
    if with_routing:
        gate_refs, rest = rest[:groups], rest[groups:]
    weights, wide, ordered, sems = rest
    index = index_ref[0]
    blocks = width // block
    copies = [
        pltpu.make_async_copy(
            weight_ref.at[0, :, pl.ds(first + i * block, block)], weights.at[i], sems.at[i]
        )
        for i in range(blocks)
    ]
    for copy in copies:
        copy.start()
    rows = wide.shape[0]
    capacity = rows // experts
    wide[...] = hidden_ref[0].astype(jnp.float32)
    for j in range(NODE_SIZE):
        for d in range(0, groups, 2):
            pair = []
            for other in (d, d + 1):
                owner = index ^ (other * NODE_SIZE + j)
                pair.append(wide[pl.ds(pl.multiple_of(owner * capacity, capacity), capacity), :])
            start = (j * groups + d) * capacity
            ordered[start : start + 2 * capacity, :] = jnp.concatenate(pair, axis=0).astype(
                jnp.bfloat16
            )
    if with_routing:
        parts = routing(index, experts, capacity, ids_ref[...], gates_ref[...])
        for ref, part in zip(gate_refs, parts):
            ref[...] = part
    share = rows // NODE_SIZE
    for i, copy in enumerate(copies):
        copy.wait()
        product = jnp.dot(
            ordered[...], weights[i], preferred_element_type=jnp.float32
        ).astype(jnp.bfloat16)
        for j in range(NODE_SIZE):
            out_refs[j][:, i * block : (i + 1) * block] = product[j * share : (j + 1) * share, :]


def down(index, hidden, down_weight, first, width, experts, ids=None, gates=None):
    block = block_width(width)
    rows, depth = hidden.shape[1:]
    share = rows // NODE_SIZE
    groups = experts // NODE_SIZE
    out_shape = [shape_of((share, width), jnp.bfloat16)] * NODE_SIZE
    in_specs = [SMEM, VMEM, HBM]
    args = [index, hidden, down_weight]
    if ids is not None:
        out_shape += [shape_of((ids.shape[1], rows), jnp.float32)] * groups
        in_specs += [VMEM, VMEM]
        args += [ids, gates]
    return pl.pallas_call(
        functools.partial(down_kernel, experts, first, width, block, ids is not None),
        out_shape=out_shape,
        in_specs=in_specs,
        out_specs=[VMEM] * len(out_shape),
        scratch_shapes=[
            pltpu.VMEM((width // block, depth, block), jnp.bfloat16),
            pltpu.VMEM((rows, depth), jnp.float32),
            pltpu.VMEM((rows, depth), jnp.bfloat16),
            pltpu.SemaphoreType.DMA((width // block,)),
        ],
        name="down",
        compiler_params=pltpu.CompilerParams(vmem_limit_bytes=48 * MIB if rows > 512 else 24 * MIB),
    )(*args)


def combine_kernel(groups, *refs):
    gate_refs = refs[:groups]
    row_refs = refs[groups : groups + NODE_SIZE]
    out_refs = refs[groups + NODE_SIZE :]
    tokens = gate_refs[0].shape[0]
    rows = jnp.concatenate([ref[...] for ref in row_refs], axis=0)
    together = groups if groups * tokens <= LANES else 1
    for base in range(0, groups, together):
        gate = jnp.concatenate([ref[...] for ref in gate_refs[base : base + together]], axis=0)
        high = gate.astype(jnp.bfloat16)
        low = (gate - high.astype(jnp.float32)).astype(jnp.bfloat16)
        both = jnp.dot(
            jnp.concatenate([high, low], axis=0), rows, preferred_element_type=jnp.float32
        )
        half = together * tokens
        part = (both[:half] + both[half:]).astype(jnp.bfloat16)
        for d in range(together):
            out_refs[base + d][...] = part[d * tokens : (d + 1) * tokens]


def combine(gates, rows):
    groups = len(gates)
    tokens = gates[0].shape[0]
    width = rows[0].shape[1]
    return pl.pallas_call(
        functools.partial(combine_kernel, groups),
        out_shape=[shape_of((tokens, width), jnp.bfloat16)] * groups,
        in_specs=[VMEM] * (groups + NODE_SIZE),
        out_specs=[VMEM] * groups,
        name="combine",
        compiler_params=pltpu.CompilerParams(vmem_limit_bytes=(40 if tokens > 16 else 8) * MIB),
    )(*gates, *rows)


def project_kernel(spans, columns, final, *refs):
    base_ref, gain_ref, weight_ref, refs = refs[0], refs[1], refs[2], refs[3:]
    section_refs, refs = refs[: len(spans)], refs[len(spans) :]
    carried = len(refs) - (1 if final else 2) == 2
    total = energy = None
    if carried:
        total, energy = refs[0][...], refs[1][...]
        refs = refs[2:]
    for n, (first, width) in enumerate(spans):
        start = pl.multiple_of(base_ref[n] * columns + first, LANES)
        wide = section_refs[n][...].astype(jnp.float32)
        square = jnp.sum(wide * wide, axis=1, keepdims=True)
        normed = (wide * gain_ref[:, pl.ds(start, width)]).astype(jnp.bfloat16)
        product = lax.dot_general(
            normed,
            weight_ref[:, pl.ds(start, width)],
            (((1,), (1,)), ((), ())),
            preferred_element_type=jnp.float32,
        )
        total = product if total is None else total + product
        energy = square if energy is None else energy + square
    if final:
        scale = lax.rsqrt(energy / final + epsilon)
        refs[0][...] = (total * scale).astype(jnp.bfloat16)
    else:
        refs[0][...] = total
        refs[1][...] = energy


def project(bases, gain, weight, sections, spans, columns, carried=(), final=0):
    tokens = sections[0].shape[0]
    latents = weight.shape[0]
    if final:
        out_shape = [shape_of((tokens, latents), jnp.bfloat16)]
    else:
        out_shape = [shape_of((tokens, latents), jnp.float32), shape_of((tokens, 1), jnp.float32)]
    return pl.pallas_call(
        functools.partial(project_kernel, spans, columns, final),
        out_shape=out_shape,
        in_specs=[SMEM] + [VMEM] * (2 + len(sections) + len(carried)),
        out_specs=[VMEM] * len(out_shape),
        name="project",
        compiler_params=pltpu.CompilerParams(vmem_limit_bytes=8 * MIB),
    )(bases, gain, weight, *sections, *carried)


def on_device(hidden, down_weight, expert_ids, gate_weights, residual, norm_gain, proj_weight):
    experts = lax.axis_size("expert")
    tensors = lax.axis_size("tensor")
    groups = experts // NODE_SIZE
    columns = down_weight.shape[2]
    index = lax.axis_index("expert").astype(jnp.int32)
    column_index = lax.axis_index("tensor").astype(jnp.int32)

    def swap(value, bits):
        return lax.ppermute(value, "expert", [(i, i ^ bits) for i in range(experts)])

    def swap_columns(value, bits):
        return lax.ppermute(value, "tensor", [(i, i ^ bits) for i in range(tensors)])

    spans = cut(columns)
    ids, gates = expert_ids.T, gate_weights.T
    place = index.reshape(1)
    arrived = []
    routed = None
    for first, width in spans:
        if routed is None:
            results = down(place, hidden, down_weight, first, width, experts, ids, gates)
            rows, own_routed = results[:NODE_SIZE], results[NODE_SIZE:]
        else:
            rows = down(place, hidden, down_weight, first, width, experts)
        arrived.append([rows[0]] + [swap(rows[j], j) for j in range(1, NODE_SIZE)])
        if routed is None:
            routed = [own_routed[0]] + [
                swap(own_routed[d], d * NODE_SIZE) for d in range(1, groups)
            ]
    streams = []
    for (first, width), rows in zip(spans, arrived):
        parts = combine(routed, rows)
        received = [parts[0]] + [swap(parts[d], d * NODE_SIZE) for d in range(1, groups)]
        summed = residual[:, first : first + width].astype(jnp.float32)
        for part in received:
            summed = summed + part.astype(jnp.float32)
        streams.append(summed.astype(jnp.bfloat16))
    stream = jnp.concatenate(streams, axis=1) if len(streams) > 1 else streams[0]
    features = columns * tensors
    if columns % LANES or len(spans) < 2 or tensors != 2:
        wide = lax.all_gather(stream, "tensor", axis=1, tiled=True).astype(jnp.float32)
        normed = (wide * norm_gain).astype(jnp.bfloat16)
        added = jnp.dot(normed, proj_weight, preferred_element_type=jnp.float32)
        energy = jnp.sum(wide * wide, axis=1)
        inverse = lax.rsqrt(energy / features + epsilon)
        return (stream, (added * inverse[:, None]).astype(jnp.bfloat16))
    others = [swap_columns(section, 1) for section in streams]
    gain = norm_gain.reshape(1, features)
    weight = proj_weight.T
    near, far = column_index, column_index ^ 1
    carried = project(near.reshape(1), gain, weight, streams[:1], spans[:1], columns)
    for n in range(1, len(spans)):
        carried = project(
            jnp.stack([near, far]),
            gain,
            weight,
            [streams[n], others[n - 1]],
            [spans[n], spans[n - 1]],
            columns,
            carried,
        )
    (latents,) = project(
        far.reshape(1), gain, weight, others[-1:], spans[-1:], columns, carried, features
    )
    return (stream, latents)


def solution(mesh):
    return jax.shard_map(
        on_device,
        mesh=mesh,
        in_specs=(
            P("expert", None, None),
            P("expert", None, "tensor"),
            P("expert", None),
            P("expert", None),
            P("expert", "tensor"),
            P(),
            P(None, "tensor"),
        ),
        out_specs=(P("expert", "tensor"), P("expert", "tensor")),
        check_vma=False,
    )
```

time: 57.8 us -> 61.4 us (1.062)
  matrix products: 19.3 us -> 0 us
  starting transfers between devices: 7.49 us -> 23.1 us
  local copies, waits for them, and re-layouts: 4.11 us -> 18.2 us
  waiting for transfers between devices: 18.6 us -> 5 us
  Pallas kernels: 0 us -> 13.2 us
  blocking collectives: 6.16 us -> 0 us
    ppermute x0 -> x17, starting transfers between devices: none -> 23.1 us  [the longest x15 21 us: swap(): lax.ppermute(value, 'expert', [(i, i ^ bits) for i in range(experts)])]
    dot_general x3 -> x0, matrix products: 19.3 us -> none  [the longest x1 9.95 us: on_device(): jnp.dot(normed_part, proj_weight, preferred_element_type=jnp.float32)]
    all_to_all x1 -> x0, waiting for transfers between devices: 18.6 us -> none  [on_device(): lax.all_to_all(grouped, 'expert', split_axis=1, concat_axis=0, tiled=True)]
    unnamed x14 -> x16, local copies, waits for them, and re-layouts: 1.19 us -> 18.2 us
    pallas_call x0 -> x7, Pallas kernels: none -> 13.2 us  [the longest x2 7.24 us: down(): pl.pallas_call(functools.partial(down_kernel, experts, first, width, bloc...]
    all_to_all x1 -> x0, starting transfers between devices: 7.49 us -> none  [on_device(): lax.all_to_all(grouped, 'expert', split_axis=1, concat_axis=0, tiled=True)]
    all_gather x1 -> x0, blocking collectives: 6.16 us -> none  [on_device(): lax.all_gather(stream, 'tensor', axis=1, tiled=True).astype(jnp.float32)]
    ppermute x0 -> x17, waiting for transfers between devices: none -> 5 us  [the longest x15 4.99 us: swap(): lax.ppermute(value, 'expert', [(i, i ^ bits) for i in range(experts)])]
  transfers between devices with their start and end apart: 1 -> 17, of which waited for: 1 -> 4; matrix products, arithmetic and copies ran while one was open for 4% -> 1% of each run, Pallas kernels for 0% -> 13%
where the time goes in v1:
time: 61.4 us; the launch traced here: 61.1 us
  starting transfers between devices  23.1 us (38%)
  local copies, waits for them, and re-layouts  18.2 us (30%)
  Pallas kernels  13.2 us (21%)
  waiting for transfers between devices  5 us (8%)
  other arithmetic  0.8 us (1%)
  between operations  0.75 us (1%)
    ppermute x15, starting transfers between devices, swap(): lax.ppermute(value, 'expert', [(i, i ^ bits) for i in range(experts)])  21 us
    unnamed x16, local copies, waits for them, and re-layouts  18.2 us
    pallas_call x2, Pallas kernels, down(): pl.pallas_call(functools.partial(down_kernel, experts, first, width, bloc...  7.24 us
    pallas_call x3, Pallas kernels, project(): pl.pallas_call(functools.partial(project_kernel, spans, columns, final),...  5.41 us
    ppermute x15, waiting for transfers between devices, swap(): lax.ppermute(value, 'expert', [(i, i ^ bits) for i in range(experts)])  4.99 us
    ppermute x2, starting transfers between devices, swap_columns(): lax.ppermute(value, 'tensor', [(i, i ^ bits) for i in range(tensors)])  2.09 us
  transfers between devices with their start and end apart: 17, of which 4 were waited for; matrix products, arithmetic and copies ran while one was open for 1% of the time, Pallas kernels for 13%

profile of v1, /device:TPU:0, one launch (start us, length us, event | category | flops | bytes accessed | tf_op | source)
XLA Modules:
  0.0 61.1 jit_solution(11117259259891792006)
XLA Ops:
  0.6 5.2 %copy-done.2 = bf16[1,2048,3584]{2,1,0:T(8,128)(2,1)S(1)} copy-done((bf16[1,2048,3584]{2,1,0:T(8,128)(2,1)S(1)}, bf16[1,2048,3584]{2,1,0:T(8,128)(2,1)}, u32[]{:S(2)}) %copy-start.2) | copy-done | bytes 14680088
  5.8 1.0 %copy-done.3 = bf16[1,128,2048]{2,1,0:T(8,128)(2,1)S(1)} copy-done((bf16[1,128,2048]{2,1,0:T(8,128)(2,1)S(1)}, bf16[1,128,2048]{2,1,0:T(8,128)(2,1)}, u32[]{:S(2)}) %copy-start.3) | copy-done | bytes 524312
  6.9 0.7 %copy-done.5 = s32[16,8]{0,1:T(8,128)S(1)} copy-done((s32[16,8]{0,1:T(8,128)S(1)}, s32[16,8]{0,1:T(8,128)}, u32[]{:S(2)}) %copy-start.5) | copy-done | bytes 536
  7.5 0.7 %copy-done.6 = f32[16,8]{0,1:T(8,128)S(1)} copy-done((f32[16,8]{0,1:T(8,128)S(1)}, f32[16,8]{0,1:T(8,128)}, u32[]{:S(2)}) %copy-start.6) | copy-done | bytes 536
  8.2 3.7 %down.2 = (bf16[32,1792]{1,0:T(8,128)(2,1)S(1)}, bf16[32,1792]{1,0:T(8,128)(2,1)S(1)}, bf16[32,1792]{1,0:T(8,128)(2,1)S(1)}, bf16[32,1792]{1,0:T(8,128)(2,1)S(1)...) custom-call(s32[1]{0:T(128)} %bitcast.refs_0_, ...), custom_call_target="tpu_custom_call" | custom-call | tf_op jit(solution)/shard_map/down/pallas_call | solution.py:126
  12.0 0.5 collective-permute-start.3
  12.5 2.6 %collective-permute-start.4 = (bf16[32,1792]{1,0:T(8,128)(2,1)S(1)}, bf16[32,1792]{1,0:T(8,128)(2,1)S(1)}, u32[]{:S(2)}, u32[]{:S(2)}) collective-permute-start(bf16[32,1792]{1,0:T(8,128)(2,1)S(1)} %get-tuple-element.32), channel_id=1, source_target_pairs={{0,4},{2,6},{4,0},{6,2},{8,12},{10,14},{12,8},{14,10},{16,20},{18,... | collective-permute-start | bytes 344072 | tf_op jit(solution)/shard_map/ppermute | solution.py:231
  15.1 0.1 collective-permute-start.5
  15.1 1.8 %collective-permute-start = (f32[16,128]{1,0:T(8,128)S(1)}, f32[16,128]{1,0:T(8,128)S(1)}, u32[]{:S(2)}, u32[]{:S(2)}) collective-permute-start(f32[16,128]{1,0:T(8,128)S(1)} %get-tuple-element.27), channel_id=1, source_target_pairs={{0,8},{2,10},{4,12},{6,14},{8,0},{10,2},{12,4},{14,6},{16,24},{18,... | collective-permute-start | bytes 24584 | tf_op jit(solution)/shard_map/ppermute | solution.py:231
  16.9 2.6 %collective-permute-start.1 = (f32[16,128]{1,0:T(8,128)S(1)}, f32[16,128]{1,0:T(8,128)S(1)}, u32[]{:S(2)}, u32[]{:S(2)}) collective-permute-start(f32[16,128]{1,0:T(8,128)S(1)} %get-tuple-element.28), channel_id=1, source_target_pairs={{0,16},{2,18},{4,20},{6,22},{8,24},{10,26},{12,28},{14,30},{16,0},... | collective-permute-start | bytes 24584 | tf_op jit(solution)/shard_map/ppermute | solution.py:231
  19.5 0.0 collective-permute-done.refs_1_
  19.5 3.1 %collective-permute-start.2 = (f32[16,128]{1,0:T(8,128)S(1)}, f32[16,128]{1,0:T(8,128)S(1)}, u32[]{:S(2)}, u32[]{:S(2)}) collective-permute-start(f32[16,128]{1,0:T(8,128)S(1)} %get-tuple-element.29), channel_id=1, source_target_pairs={{0,24},{2,26},{4,28},{6,30},{8,16},{10,18},{12,20},{14,22},{16,8},... | collective-permute-start | bytes 24584 | tf_op jit(solution)/shard_map/ppermute | solution.py:231
  22.6 3.5 %down.3 = (bf16[32,1792]{1,0:T(8,128)(2,1)S(1)}, bf16[32,1792]{1,0:T(8,128)(2,1)S(1)}, bf16[32,1792]{1,0:T(8,128)(2,1)S(1)}, bf16[32,1792]{1,0:T(8,128)(2,1)S(1)}) custom-call(s32[1]{0:T(128)} %bitcast.refs_0_, bf16[1,128,2048]{2,1,0:T(8,128)(2,1)S(1)} %copy-done.3, bf16[1,2048,3584]{2,1,0:T(8,128)(2,1)S(1)} %copy-done.2), custom_call_target="tpu_custom_call" | custom-call | tf_op jit(solution)/shard_map/down/pallas_call | solution.py:126
  26.1 0.0 collective-permute-done.1.refs_2_
  26.1 1.6 %collective-permute-start.10 = (bf16[32,1792]{1,0:T(8,128)(2,1)S(1)}, bf16[32,1792]{1,0:T(8,128)(2,1)S(1)}, u32[]{:S(2)}, u32[]{:S(2)}) collective-permute-start(bf16[32,1792]{1,0:T(8,128)(2,1)S(1)} %get-tuple-element.40), channel_id=1, source_target_pairs={{0,4},{2,6},{4,0},{6,2},{8,12},{10,14},{12,8},{14,10},{16,20},{18,... | collective-permute-start | bytes 344072 | tf_op jit(solution)/shard_map/ppermute | solution.py:231
  27.7 0.0 collective-permute-done.2.refs_3_
  27.7 0.0 collective-permute-start.11
  27.7 0.0 collective-permute-done.3.refs_5_
  27.7 0.6 %collective-permute-start.9 = (bf16[32,1792]{1,0:T(8,128)(2,1)S(1)}, bf16[32,1792]{1,0:T(8,128)(2,1)S(1)}, u32[]{:S(2)}, u32[]{:S(2)}) collective-permute-start(bf16[32,1792]{1,0:T(8,128)(2,1)S(1)} %get-tuple-element.39), channel_id=1, source_target_pairs={{0,2},{2,0},{4,6},{6,4},{8,10},{10,8},{12,14},{14,12},{16,18},{18,... | collective-permute-start | bytes 344072 | tf_op jit(solution)/shard_map/ppermute | solution.py:231
  28.4 0.0 collective-permute-done.4.refs_6_
  28.4 0.0 collective-permute-done.5.refs_7_
  28.4 0.3 combine.2
  28.7 0.1 collective-permute-start.6
  28.7 1.9 %collective-permute-start.7 = (bf16[16,1792]{1,0:T(8,128)(2,1)S(1)}, bf16[16,1792]{1,0:T(8,128)(2,1)S(1)}, u32[]{:S(2)}, u32[]{:S(2)}) collective-permute-start(bf16[16,1792]{1,0:T(8,128)(2,1)S(1)} %get-tuple-element.36), channel_id=1, source_target_pairs={{0,16},{2,18},{4,20},{6,22},{8,24},{10,26},{12,28},{14,30},{16,0},... | collective-permute-start | bytes 172040 | tf_op jit(solution)/shard_map/ppermute | solution.py:231
  30.6 0.7 %collective-permute-done.10.refs_6_ = bf16[32,1792]{1,0:T(8,128)(2,1)S(1)} collective-permute-done((bf16[32,1792]{1,0:T(8,128)(2,1)S(1)}, bf16[32,1792]{1,0:T(8,128)(2,1)S(1)}, u32[]{:S(2)}, u32[]{:S(2)}) %collective-permute-start.10) | collective-permute-done | bytes 114720 | tf_op jit(solution)/shard_map/ppermute | solution.py:231
  31.3 1.8 %collective-permute-start.8 = (bf16[16,1792]{1,0:T(8,128)(2,1)S(1)}, bf16[16,1792]{1,0:T(8,128)(2,1)S(1)}, u32[]{:S(2)}, u32[]{:S(2)}) collective-permute-start(bf16[16,1792]{1,0:T(8,128)(2,1)S(1)} %get-tuple-element.37), channel_id=1, source_target_pairs={{0,24},{2,26},{4,28},{6,30},{8,16},{10,18},{12,20},{14,22},{16,8},... | collective-permute-start | bytes 172040 | tf_op jit(solution)/shard_map/ppermute | solution.py:231
  33.1 0.0 collective-permute-done.11.refs_7_
  33.1 0.3 combine.3
  33.4 0.1 collective-permute-start.12
  33.5 2.6 %collective-permute-start.13 = (bf16[16,1792]{1,0:T(8,128)(2,1)S(1)}, bf16[16,1792]{1,0:T(8,128)(2,1)S(1)}, u32[]{:S(2)}, u32[]{:S(2)}) collective-permute-start(bf16[16,1792]{1,0:T(8,128)(2,1)S(1)} %get-tuple-element.44), channel_id=1, source_target_pairs={{0,16},{2,18},{4,20},{6,22},{8,24},{10,26},{12,28},{14,30},{16,0},... | collective-permute-start | bytes 172040 | tf_op jit(solution)/shard_map/ppermute | solution.py:231
  36.1 1.8 %collective-permute-start.14 = (bf16[16,1792]{1,0:T(8,128)(2,1)S(1)}, bf16[16,1792]{1,0:T(8,128)(2,1)S(1)}, u32[]{:S(2)}, u32[]{:S(2)}) collective-permute-start(bf16[16,1792]{1,0:T(8,128)(2,1)S(1)} %get-tuple-element.45), channel_id=1, source_target_pairs={{0,24},{2,26},{4,28},{6,30},{8,16},{10,18},{12,20},{14,22},{16,8},... | collective-permute-start | bytes 172040 | tf_op jit(solution)/shard_map/ppermute | solution.py:231
  37.9 0.1 pad_add_fusion.refs_0_
  37.9 0.0 collective-permute-done.7
  38.0 0.0 collective-permute-done.8
  38.0 1.4 %collective-permute-done.12 = bf16[16,1792]{1,0:T(8,128)(2,1)S(1)} collective-permute-done((bf16[16,1792]{1,0:T(8,128)(2,1)S(1)}, bf16[16,1792]{1,0:T(8,128)(2,1)S(1)}, u32[]{:S(2)}, u32[]{:S(2)}) %collective-permute-start.12) | collective-permute-done | bytes 57376 | tf_op jit(solution)/shard_map/ppermute | solution.py:231
  39.4 1.7 %collective-permute-done.13 = bf16[16,1792]{1,0:T(8,128)(2,1)S(1)} collective-permute-done((bf16[16,1792]{1,0:T(8,128)(2,1)S(1)}, bf16[16,1792]{1,0:T(8,128)(2,1)S(1)}, u32[]{:S(2)}, u32[]{:S(2)}) %collective-permute-start.13) | collective-permute-done | bytes 57376 | tf_op jit(solution)/shard_map/ppermute | solution.py:231
  41.0 1.1 %collective-permute-done.14 = bf16[16,1792]{1,0:T(8,128)(2,1)S(1)} collective-permute-done((bf16[16,1792]{1,0:T(8,128)(2,1)S(1)}, bf16[16,1792]{1,0:T(8,128)(2,1)S(1)}, u32[]{:S(2)}, u32[]{:S(2)}) %collective-permute-start.14) | collective-permute-done | bytes 57376 | tf_op jit(solution)/shard_map/ppermute | solution.py:231
  42.2 0.1 add_convert_fusion.1
  42.2 1.6 %collective-permute-start.16 = (bf16[16,1792]{1,0:T(8,128)(2,1)S(1)}, bf16[16,1792]{1,0:T(8,128)(2,1)S(1)}, u32[]{:S(2)}, u32[]{:S(2)}) collective-permute-start(bf16[16,1792]{1,0:T(8,128)(2,1)S(1)} %get-tuple-element.50.refs_3_), channel_id=1, source_target_pairs={{0,1},{1,0},{2,3},{3,2},{4,5},{5,4},{6,7},{7,6},{8,9},{9,8},{10,11... | collective-permute-start | bytes 172040 | tf_op jit(solution)/shard_map/ppermute | solution.py:234
  43.8 0.5 collective-permute-start.15
  44.3 0.7 %pad_maximum_fusion = bf16[16,3584]{1,0:T(8,128)(2,1)} fusion(bf16[16,1792]{1,0:T(8,128)(2,1)S(1)} %get-tuple-element.51.refs_3_, bf16[16,1792]{1,0:T(8,128)(2,1)S(1)} %get-tuple-element.50.refs_3_), kind=kLoop, calls=%fused_computation | loop fusion | flops 229376 | bytes 229376 | tf_op jit(solution)/shard_map/concatenate | solution.py:260
  45.0 5.3 %copy-done = bf16[7168,1056]{0,1:T(8,128)(2,1)S(1)} copy-done((bf16[7168,1056]{0,1:T(8,128)(2,1)S(1)}, bf16[7168,1056]{0,1:T(8,128)(2,1)}, u32[]{:S(2)}) %copy-start) | copy-done | bytes 15138840
  50.3 1.1 %project.3 = (f32[16,1056]{1,0:T(8,128)S(1)}, f32[16,1]{1,0:T(8,128)S(1)}) custom-call(s32[1]{0:T(128)} %bitcast.6.refs_0_, f32[1,7168]{1,0:T(1,128)S(1)} %bitcast.10, bf16[1056,7168]{1,0:T(8,128)(2,1)S(1)} %bitcast.7, bf16[16,1792]{1,0:T(8,128)(2,1)S(1)} %get-tuple-element.50.refs_3_), custom_call_target="tpu_custom_call" | custom-call | tf_op jit(solution)/shard_map/project/pallas_call | solution.py:212
  51.4 0.0 copy-start.1
  51.4 5.3 %copy-done.1 = bf16[7168,1056]{0,1:T(8,128)(2,1)S(1)} copy-done((bf16[7168,1056]{0,1:T(8,128)(2,1)S(1)}, bf16[7168,1056]{0,1:T(8,128)(2,1)}, u32[]{:S(2)}) %copy-start.1) | copy-done | bytes 15138840
  56.7 2.6 %project.4 = (f32[16,1056]{1,0:T(8,128)S(1)}, f32[16,1]{1,0:T(8,128)S(1)}) custom-call(s32[2]{0:T(128)S(1)} %pad_add_fusion.refs_0_, f32[1,7168]{1,0:T(1,128)S(1)} %bitcast.11, bf16[1056,7168]{1,0:T(8,128)(2,1)S(1)} %bitcast.8, bf16[16,1792]{1,0:T(8,128)(2,1)S(1)} %get-tuple-element.51.refs_3_, bf16[16,1792]{1,0:T(8,128)(2,1)S(1)} %collective-permute-done.16.refs_4_, ...), custom_call_target="tpu_custom_call" | custom-call | tf_op jit(solution)/shard_map/project/pallas_call | solution.py:212
  59.3 0.0 collective-permute-done.15.refs_3_
  59.3 1.7 %project.5 = bf16[16,1056]{1,0:T(8,128)(2,1)} custom-call(s32[1]{0:T(128)} %bitcast.3.refs_0_, f32[1,7168]{1,0:T(1,128)S(1)} %bitcast.12, bf16[1056,7168]{1,0:T(8,128)(2,1)S(1)} %bitcast.9, bf16[16,1792]{1,0:T(8,128)(2,1)S(1)} %collective-permute-done.15.refs_3_, f32[16,1056]{1,0:T(8,128)S(1)} %get-tuple-element.48.refs_4_, ...), custom_call_target="tpu_custom_call" | custom-call | tf_op jit(solution)/shard_map/project/pallas_call | solution.py:212
  (12 shorter events, 0.0 us)
Async XLA Ops:
  0.6 5.2 %copy-start.2 = (bf16[1,2048,3584]{2,1,0:T(8,128)(2,1)S(1)}, bf16[1,2048,3584]{2,1,0:T(8,128)(2,1)}, u32[]{:S(2)}) copy-start(bf16[1,2048,3584]{2,1,0:T(8,128)(2,1)} %refs_2_.3) | copy-start | bytes 44040196
  5.8 1.0 %copy-start.3 = (bf16[1,128,2048]{2,1,0:T(8,128)(2,1)S(1)}, bf16[1,128,2048]{2,1,0:T(8,128)(2,1)}, u32[]{:S(2)}) copy-start(bf16[1,128,2048]{2,1,0:T(8,128)(2,1)} %refs_1_.3) | copy-start | bytes 1572868
  6.9 0.7 %copy-start.5 = (s32[16,8]{0,1:T(8,128)S(1)}, s32[16,8]{0,1:T(8,128)}, u32[]{:S(2)}) copy-start(s32[16,8]{0,1:T(8,128)} %param.9) | copy-start | bytes 1540
  7.5 0.7 %copy-start.6 = (f32[16,8]{0,1:T(8,128)S(1)}, f32[16,8]{0,1:T(8,128)}, u32[]{:S(2)}) copy-start(f32[16,8]{0,1:T(8,128)} %param.10) | copy-start | bytes 1540
  8.2 33.9 %copy-start.7 = (bf16[16,3584]{1,0:T(8,128)(2,1)S(1)}, bf16[16,3584]{1,0:T(8,128)(2,1)}, u32[]{:S(2)}) copy-start(bf16[16,3584]{1,0:T(8,128)(2,1)} %param.11) | copy-start | bytes 344068
  8.2 36.8 %copy-start.4 = (f32[7168]{0:T(1024)S(1)}, f32[7168]{0:T(1024)}, u32[]{:S(2)}) copy-start(f32[7168]{0:T(1024)} %param.12) | copy-start | bytes 86020
  12.0 15.7 %collective-permute-start.3 = (bf16[32,1792]{1,0:T(8,128)(2,1)S(1)}, bf16[32,1792]{1,0:T(8,128)(2,1)S(1)}, u32[]{:S(2)}, u32[]{:S(2)}) collective-permute-start(bf16[32,1792]{1,0:T(8,128)(2,1)S(1)} %get-tuple-element.31), channel_id=1, source_target_pairs={{0,2},{2,0},{4,6},{6,4},{8,10},{10,8},{12,14},{14,12},{16,18},{18,... | collective-permute-start | bytes 344072 | tf_op jit(solution)/shard_map/ppermute | solution.py:231
  12.5 15.9 %collective-permute-start.4 = (bf16[32,1792]{1,0:T(8,128)(2,1)S(1)}, bf16[32,1792]{1,0:T(8,128)(2,1)S(1)}, u32[]{:S(2)}, u32[]{:S(2)}) collective-permute-start(bf16[32,1792]{1,0:T(8,128)(2,1)S(1)} %get-tuple-element.32), channel_id=1, source_target_pairs={{0,4},{2,6},{4,0},{6,2},{8,12},{10,14},{12,8},{14,10},{16,20},{18,... | collective-permute-start | bytes 344072 | tf_op jit(solution)/shard_map/ppermute | solution.py:231
  15.1 13.3 %collective-permute-start.5 = (bf16[32,1792]{1,0:T(8,128)(2,1)S(1)}, bf16[32,1792]{1,0:T(8,128)(2,1)S(1)}, u32[]{:S(2)}, u32[]{:S(2)}) collective-permute-start(bf16[32,1792]{1,0:T(8,128)(2,1)S(1)} %get-tuple-element.33), channel_id=1, source_target_pairs={{0,6},{2,4},{4,2},{6,0},{8,14},{10,12},{12,10},{14,8},{16,22},{18,... | collective-permute-start | bytes 344072 | tf_op jit(solution)/shard_map/ppermute | solution.py:231
  15.1 4.4 %collective-permute-start = (f32[16,128]{1,0:T(8,128)S(1)}, f32[16,128]{1,0:T(8,128)S(1)}, u32[]{:S(2)}, u32[]{:S(2)}) collective-permute-start(f32[16,128]{1,0:T(8,128)S(1)} %get-tuple-element.27), channel_id=1, source_target_pairs={{0,8},{2,10},{4,12},{6,14},{8,0},{10,2},{12,4},{14,6},{16,24},{18,... | collective-permute-start | bytes 24584 | tf_op jit(solution)/shard_map/ppermute | solution.py:231
  16.9 9.2 %collective-permute-start.1 = (f32[16,128]{1,0:T(8,128)S(1)}, f32[16,128]{1,0:T(8,128)S(1)}, u32[]{:S(2)}, u32[]{:S(2)}) collective-permute-start(f32[16,128]{1,0:T(8,128)S(1)} %get-tuple-element.28), channel_id=1, source_target_pairs={{0,16},{2,18},{4,20},{6,22},{8,24},{10,26},{12,28},{14,30},{16,0},... | collective-permute-start | bytes 24584 | tf_op jit(solution)/shard_map/ppermute | solution.py:231
  19.5 8.2 %collective-permute-start.2 = (f32[16,128]{1,0:T(8,128)S(1)}, f32[16,128]{1,0:T(8,128)S(1)}, u32[]{:S(2)}, u32[]{:S(2)}) collective-permute-start(f32[16,128]{1,0:T(8,128)S(1)} %get-tuple-element.29), channel_id=1, source_target_pairs={{0,24},{2,26},{4,28},{6,30},{8,16},{10,18},{12,20},{14,22},{16,8},... | collective-permute-start | bytes 24584 | tf_op jit(solution)/shard_map/ppermute | solution.py:231
  26.1 5.2 %collective-permute-start.10 = (bf16[32,1792]{1,0:T(8,128)(2,1)S(1)}, bf16[32,1792]{1,0:T(8,128)(2,1)S(1)}, u32[]{:S(2)}, u32[]{:S(2)}) collective-permute-start(bf16[32,1792]{1,0:T(8,128)(2,1)S(1)} %get-tuple-element.40), channel_id=1, source_target_pairs={{0,4},{2,6},{4,0},{6,2},{8,12},{10,14},{12,8},{14,10},{16,20},{18,... | collective-permute-start | bytes 344072 | tf_op jit(solution)/shard_map/ppermute | solution.py:231
  27.7 5.4 %collective-permute-start.11 = (bf16[32,1792]{1,0:T(8,128)(2,1)S(1)}, bf16[32,1792]{1,0:T(8,128)(2,1)S(1)}, u32[]{:S(2)}, u32[]{:S(2)}) collective-permute-start(bf16[32,1792]{1,0:T(8,128)(2,1)S(1)} %get-tuple-element.41), channel_id=1, source_target_pairs={{0,6},{2,4},{4,2},{6,0},{8,14},{10,12},{12,10},{14,8},{16,22},{18,... | collective-permute-start | bytes 344072 | tf_op jit(solution)/shard_map/ppermute | solution.py:231
  27.7 5.4 %collective-permute-start.9 = (bf16[32,1792]{1,0:T(8,128)(2,1)S(1)}, bf16[32,1792]{1,0:T(8,128)(2,1)S(1)}, u32[]{:S(2)}, u32[]{:S(2)}) collective-permute-start(bf16[32,1792]{1,0:T(8,128)(2,1)S(1)} %get-tuple-element.39), channel_id=1, source_target_pairs={{0,2},{2,0},{4,6},{6,4},{8,10},{10,8},{12,14},{14,12},{16,18},{18,... | collective-permute-start | bytes 344072 | tf_op jit(solution)/shard_map/ppermute | solution.py:231
  28.7 7.4 %collective-permute-start.6 = (bf16[16,1792]{1,0:T(8,128)(2,1)S(1)}, bf16[16,1792]{1,0:T(8,128)(2,1)S(1)}, u32[]{:S(2)}, u32[]{:S(2)}) collective-permute-start(bf16[16,1792]{1,0:T(8,128)(2,1)S(1)} %get-tuple-element.35), channel_id=1, source_target_pairs={{0,8},{2,10},{4,12},{6,14},{8,0},{10,2},{12,4},{14,6},{16,24},{18,... | collective-permute-start | bytes 172040 | tf_op jit(solution)/shard_map/ppermute | solution.py:231
  28.7 9.2 %collective-permute-start.7 = (bf16[16,1792]{1,0:T(8,128)(2,1)S(1)}, bf16[16,1792]{1,0:T(8,128)(2,1)S(1)}, u32[]{:S(2)}, u32[]{:S(2)}) collective-permute-start(bf16[16,1792]{1,0:T(8,128)(2,1)S(1)} %get-tuple-element.36), channel_id=1, source_target_pairs={{0,16},{2,18},{4,20},{6,22},{8,24},{10,26},{12,28},{14,30},{16,0},... | collective-permute-start | bytes 172040 | tf_op jit(solution)/shard_map/ppermute | solution.py:231
  31.3 6.6 %collective-permute-start.8 = (bf16[16,1792]{1,0:T(8,128)(2,1)S(1)}, bf16[16,1792]{1,0:T(8,128)(2,1)S(1)}, u32[]{:S(2)}, u32[]{:S(2)}) collective-permute-start(bf16[16,1792]{1,0:T(8,128)(2,1)S(1)} %get-tuple-element.37), channel_id=1, source_target_pairs={{0,24},{2,26},{4,28},{6,30},{8,16},{10,18},{12,20},{14,22},{16,8},... | collective-permute-start | bytes 172040 | tf_op jit(solution)/shard_map/ppermute | solution.py:231
  33.4 6.0 %collective-permute-start.12 = (bf16[16,1792]{1,0:T(8,128)(2,1)S(1)}, bf16[16,1792]{1,0:T(8,128)(2,1)S(1)}, u32[]{:S(2)}, u32[]{:S(2)}) collective-permute-start(bf16[16,1792]{1,0:T(8,128)(2,1)S(1)} %get-tuple-element.43), channel_id=1, source_target_pairs={{0,8},{2,10},{4,12},{6,14},{8,0},{10,2},{12,4},{14,6},{16,24},{18,... | collective-permute-start | bytes 172040 | tf_op jit(solution)/shard_map/ppermute | solution.py:231
  33.5 7.5 %collective-permute-start.13 = (bf16[16,1792]{1,0:T(8,128)(2,1)S(1)}, bf16[16,1792]{1,0:T(8,128)(2,1)S(1)}, u32[]{:S(2)}, u32[]{:S(2)}) collective-permute-start(bf16[16,1792]{1,0:T(8,128)(2,1)S(1)} %get-tuple-element.44), channel_id=1, source_target_pairs={{0,16},{2,18},{4,20},{6,22},{8,24},{10,26},{12,28},{14,30},{16,0},... | collective-permute-start | bytes 172040 | tf_op jit(solution)/shard_map/ppermute | solution.py:231
  36.1 6.1 %collective-permute-start.14 = (bf16[16,1792]{1,0:T(8,128)(2,1)S(1)}, bf16[16,1792]{1,0:T(8,128)(2,1)S(1)}, u32[]{:S(2)}, u32[]{:S(2)}) collective-permute-start(bf16[16,1792]{1,0:T(8,128)(2,1)S(1)} %get-tuple-element.45), channel_id=1, source_target_pairs={{0,24},{2,26},{4,28},{6,30},{8,16},{10,18},{12,20},{14,22},{16,8},... | collective-permute-start | bytes 172040 | tf_op jit(solution)/shard_map/ppermute | solution.py:231
  42.2 9.1 %collective-permute-start.16 = (bf16[16,1792]{1,0:T(8,128)(2,1)S(1)}, bf16[16,1792]{1,0:T(8,128)(2,1)S(1)}, u32[]{:S(2)}, u32[]{:S(2)}) collective-permute-start(bf16[16,1792]{1,0:T(8,128)(2,1)S(1)} %get-tuple-element.50.refs_3_), channel_id=1, source_target_pairs={{0,1},{1,0},{2,3},{3,2},{4,5},{5,4},{6,7},{7,6},{8,9},{9,8},{10,11... | collective-permute-start | bytes 172040 | tf_op jit(solution)/shard_map/ppermute | solution.py:234
  43.8 15.5 %collective-permute-start.15 = (bf16[16,1792]{1,0:T(8,128)(2,1)S(1)}, bf16[16,1792]{1,0:T(8,128)(2,1)S(1)}, u32[]{:S(2)}, u32[]{:S(2)}) collective-permute-start(bf16[16,1792]{1,0:T(8,128)(2,1)S(1)} %get-tuple-element.51.refs_3_), channel_id=1, source_target_pairs={{0,1},{1,0},{2,3},{3,2},{4,5},{5,4},{6,7},{7,6},{8,9},{9,8},{10,11... | collective-permute-start | bytes 172040 | tf_op jit(solution)/shard_map/ppermute | solution.py:234
  45.0 5.3 %copy-start = (bf16[7168,1056]{0,1:T(8,128)(2,1)S(1)}, bf16[7168,1056]{0,1:T(8,128)(2,1)}, u32[]{:S(2)}) copy-start(bf16[7168,1056]{0,1:T(8,128)(2,1)} %param.13) | copy-start | bytes 45416452
  51.4 5.3 %copy-start.1 = (bf16[7168,1056]{0,1:T(8,128)(2,1)S(1)}, bf16[7168,1056]{0,1:T(8,128)(2,1)}, u32[]{:S(2)}) copy-start(bf16[7168,1056]{0,1:T(8,128)(2,1)} %param.13) | copy-start | bytes 45416452

commit v2 on v0

v2 whole, which is shorter than its diff:
```python
import functools

import jax
import jax.numpy as jnp
from jax import lax
from jax.experimental import pallas as pl
from jax.experimental.pallas import tpu as pltpu
from jax.sharding import PartitionSpec as P

NODE_SIZE = 4
LANES = 128
MIB = 1 << 20
ADD_COST = 64 * MIB


epsilon = 1e-06

VMEM = pl.BlockSpec(memory_space=pltpu.VMEM)
SMEM = pl.BlockSpec(memory_space=pltpu.SMEM)
ANY = pl.BlockSpec(memory_space=pl.ANY)
HBM = pl.BlockSpec(memory_space=pltpu.HBM)


def shape_of(shape, dtype):
    return jax.ShapeDtypeStruct(shape, dtype)


def block_width(width):
    for tiles in (4, 2, 3, 1):
        if width % (tiles * LANES) == 0:
            return tiles * LANES
    return width


def halves(groups):
    if groups < 4 or groups % 4:
        return [(0, groups)]
    return [(groups // 2, groups // 2), (0, groups // 2)]


def pieces_of(spans):
    outputs = [[(j, low, count) for low, count in spans] for j in (0, 1)]
    low, count = spans[0]
    outputs.append([(2, low, count), (3, low, count)])
    for low, count in spans[1:]:
        outputs += [[(2, low, count)], [(3, low, count)]]
    return outputs


def down_kernel(experts, outputs, block, hidden_hbm, weight_hbm, *refs):
    out_refs = refs[: len(outputs)]
    hidden, wide, ordered, weights, hidden_sem, weight_sems = refs[len(outputs) :]
    index = lax.axis_index("expert")
    first_copy = pltpu.make_async_copy(hidden_hbm.at[0], hidden, hidden_sem)
    copies = [
        pltpu.make_async_copy(
            weight_hbm.at[0, :, pl.ds(i * block, block)], weights.at[i], weight_sems.at[i]
        )
        for i in range(weights.shape[0])
    ]
    first_copy.start()
    for copy in copies:
        copy.start()
    rows = hidden.shape[0]
    capacity = rows // experts
    first_copy.wait()
    wide[...] = hidden[...].astype(jnp.float32)
    start = 0
    starts = []
    for pieces in outputs:
        starts.append(start)
        for j, low, count in pieces:
            for d in range(low, low + count, 2):
                pair = []
                for other in (d, d + 1):
                    owner = index ^ (other * NODE_SIZE + j)
                    pair.append(
                        wide[pl.ds(pl.multiple_of(owner * capacity, capacity), capacity), :]
                    )
                ordered[start : start + 2 * capacity, :] = jnp.concatenate(pair, axis=0).astype(
                    jnp.bfloat16
                )
                start += 2 * capacity
    starts.append(start)
    for i, copy in enumerate(copies):
        copy.wait()
        product = jnp.dot(
            ordered[...], weights[i], preferred_element_type=jnp.float32
        ).astype(jnp.bfloat16)
        for ref, begin, end in zip(out_refs, starts[:-1], starts[1:]):
            ref[:, i * block : (i + 1) * block] = product[begin:end, :]


def down(hidden, down_weight, experts, spans):
    rows, depth = hidden.shape[1:]
    columns = down_weight.shape[2]
    capacity = rows // experts
    block = block_width(columns)
    outputs = pieces_of(spans)
    out_shape = [
        shape_of((sum(count for _, _, count in pieces) * capacity, columns), jnp.bfloat16)
        for pieces in outputs
    ]
    return pl.pallas_call(
        functools.partial(down_kernel, experts, outputs, block),
        out_shape=out_shape,
        in_specs=[ANY, ANY],
        out_specs=[VMEM] * len(out_shape),
        scratch_shapes=[
            pltpu.VMEM((rows, depth), jnp.bfloat16),
            pltpu.VMEM((rows, depth), jnp.float32),
            pltpu.VMEM((rows, depth), jnp.bfloat16),
            pltpu.VMEM((columns // block, depth, block), jnp.bfloat16),
            pltpu.SemaphoreType.DMA(()),
            pltpu.SemaphoreType.DMA((columns // block,)),
        ],
        name="down",
        cost_estimate=pl.CostEstimate(
            flops=2 * rows * depth * columns, bytes_accessed=2 * depth * columns, transcendentals=0
        ),
        compiler_params=pltpu.CompilerParams(vmem_limit_bytes=50 * MIB),
    )(hidden, down_weight)


def gates_of(index, low, count, capacity, tokens, chosen):
    shape = (NODE_SIZE * count * capacity, tokens)
    row = lax.broadcasted_iota(jnp.int32, shape, 0)
    slot = (row % capacity).astype(jnp.float32)
    group = row // capacity % count + low
    expert = (index ^ (row // (capacity * count))).astype(jnp.float32)
    earlier = lax.broadcasted_iota(jnp.int32, (tokens, tokens), 0) < lax.broadcasted_iota(
        jnp.int32, (tokens, tokens), 1
    )
    earlier = jnp.where(earlier, 1.0, 0.0)
    found = []
    for d in range(low, low + count):
        picks = chosen[d - low].shape[0] // 2
        ids, gates = chosen[d - low][:picks], chosen[d - low][picks:]
        named = jnp.zeros(shape, jnp.float32)
        gate = jnp.zeros(shape, jnp.float32)
        for k in range(picks):
            hit = ids[k : k + 1, :] == expert
            named = named + jnp.where(hit, 1.0, 0.0)
            gate = gate + jnp.where(hit, gates[k : k + 1, :], 0.0)
        before = jnp.dot(named, earlier, preferred_element_type=jnp.float32)
        found.append(jnp.where((before == slot) & (group == d), gate, 0.0).T)
    return found


def combine_kernel(low, count, capacity, begins, *refs):
    chosen_refs = refs[:count]
    row_refs = refs[count : count + NODE_SIZE]
    out_refs = refs[len(refs) - count :]
    tokens = chosen_refs[0].shape[1]
    index = lax.axis_index("expert")
    found = gates_of(index, low, count, capacity, tokens, [ref[...] for ref in chosen_refs])
    rows = jnp.concatenate(
        [ref[begin : begin + count * capacity] for ref, begin in zip(row_refs, begins)], axis=0
    )
    together = count if count * tokens <= LANES else 1
    for base in range(0, count, together):
        gate = jnp.concatenate(found[base : base + together], axis=0)
        high = gate.astype(jnp.bfloat16)
        rest = (gate - high.astype(jnp.float32)).astype(jnp.bfloat16)
        both = jnp.dot(
            jnp.concatenate([high, rest], axis=0), rows, preferred_element_type=jnp.float32
        )
        half = together * tokens
        part = (both[:half] + both[half:]).astype(jnp.bfloat16)
        for d in range(together):
            out_refs[base + d][...] = part[d * tokens : (d + 1) * tokens]


def combine(chosen, rows, begins, low, capacity, after):
    count = len(chosen)
    tokens = chosen[0].shape[1]
    columns = rows[0].shape[1]
    return pl.pallas_call(
        functools.partial(combine_kernel, low, count, capacity, begins),
        out_shape=[shape_of((tokens, columns), jnp.bfloat16)] * count,
        in_specs=[VMEM] * (count + NODE_SIZE) + [ANY] * len(after),
        out_specs=[VMEM] * count,
        name="combine",
        cost_estimate=pl.CostEstimate(
            flops=4 * count * tokens * LANES * columns,
            bytes_accessed=4 * count * tokens * columns,
            transcendentals=0,
        ),
        compiler_params=pltpu.CompilerParams(vmem_limit_bytes=(40 if tokens > 16 else 8) * MIB),
    )(*chosen, *rows, *after)


def add_kernel(base_ref, *refs):
    total = base_ref[...].astype(jnp.float32)
    for ref in refs[:-1]:
        total = total + ref[...].astype(jnp.float32)
    refs[-1][...] = total


def add(base, parts):
    return pl.pallas_call(
        add_kernel,
        out_shape=shape_of(base.shape, jnp.float32),
        in_specs=[VMEM] * (1 + len(parts)),
        out_specs=VMEM,
        name="add",
        cost_estimate=pl.CostEstimate(
            flops=0, bytes_accessed=ADD_COST, transcendentals=0
        ),
        compiler_params=pltpu.CompilerParams(vmem_limit_bytes=(40 if base.shape[0] > 16 else 8) * MIB),
    )(base, *parts)


def fetch_kernel(columns, flip, pieces, source_hbm, after_ref, out_ref, sems):
    width = columns // pieces
    base = (lax.axis_index("tensor") ^ flip) * columns
    copies = [
        pltpu.make_async_copy(
            source_hbm.at[:, pl.ds(pl.multiple_of(base + i * width, LANES), width)],
            out_ref.at[:, pl.ds(i * width, width)],
            sems.at[i],
        )
        for i in range(pieces)
    ]
    for copy in copies:
        copy.start()
    for copy in copies:
        copy.wait()


def fetch(source, columns, flip, after):
    pieces = 4 if columns // 4 % LANES == 0 else 1
    return pl.pallas_call(
        functools.partial(fetch_kernel, columns, flip, pieces),
        out_shape=pltpu.VMEM((source.shape[0], columns), source.dtype),
        in_specs=[ANY, ANY],
        out_specs=VMEM,
        scratch_shapes=[pltpu.SemaphoreType.DMA((pieces,))],
        name="fetch",
        cost_estimate=pl.CostEstimate(
            flops=0, bytes_accessed=2 * source.shape[0] * columns, transcendentals=0
        ),
        compiler_params=pltpu.CompilerParams(vmem_limit_bytes=40 * MIB),
    )(source, after)


def project_kernel(block, features, *refs):
    gain_ref, weight_ref, section_ref = refs[:3]
    refs = refs[3:]
    columns = section_ref.shape[1]
    base = lax.axis_index("tensor")
    total = energy = None
    if features:
        base = base ^ 1
        total, energy = refs[0][...], refs[1][...]
    for i in range(0, columns, block):
        wide = section_ref[:, i : i + block].astype(jnp.float32)
        square = jnp.sum(wide * wide, axis=1, keepdims=True)
        begin = pl.multiple_of(base * columns + i, LANES)
        normed = (wide * gain_ref[:, pl.ds(begin, block)]).astype(jnp.bfloat16)
        product = lax.dot_general(
            normed,
            weight_ref[:, i : i + block],
            (((1,), (1,)), ((), ())),
            preferred_element_type=jnp.float32,
        )
        total = product if total is None else total + product
        energy = square if energy is None else energy + square
    if features:
        scale = lax.rsqrt(energy / features + epsilon)
        refs[2][...] = (total * scale).astype(jnp.bfloat16)
    else:
        refs[0][...] = total
        refs[1][...] = energy


def project(gain, weight, section, carried=(), features=0):
    tokens, columns = section.shape
    latents = weight.shape[0]
    block = columns // 4 if columns // 4 % LANES == 0 else columns
    if features:
        out_shape = [shape_of((tokens, latents), jnp.bfloat16)]
    else:
        out_shape = [shape_of((tokens, latents), jnp.float32), shape_of((tokens, 1), jnp.float32)]
    return pl.pallas_call(
        functools.partial(project_kernel, block, features),
        out_shape=out_shape,
        in_specs=[VMEM] * (3 + len(carried)),
        out_specs=[VMEM] * len(out_shape),
        name="project",
        cost_estimate=pl.CostEstimate(
            flops=64 * tokens * latents * columns, bytes_accessed=0, transcendentals=0
        ),
        compiler_params=pltpu.CompilerParams(vmem_limit_bytes=8 * MIB),
    )(gain, weight, section, *carried)


def on_device(hidden, down_weight, expert_ids, gate_weights, residual, norm_gain, proj_weight):
    experts = lax.axis_size("expert")
    tensors = lax.axis_size("tensor")
    groups = experts // NODE_SIZE
    columns = down_weight.shape[2]
    capacity = hidden.shape[1] // experts
    features = columns * tensors
    spans = halves(groups)

    def swap(value, bits):
        return lax.ppermute(value, "expert", [(i, i ^ bits) for i in range(experts)])

    results = down(hidden, down_weight, experts, spans)
    results, expert_ids, gate_weights = lax.optimization_barrier(
        (results, expert_ids, gate_weights)
    )
    own, near, first, *rest = results
    first = swap(first, 2)
    near = swap(near, 1)
    rest = [swap(rows, 2 + n % 2) for n, rows in enumerate(rest)]
    chosen = [jnp.concatenate([expert_ids.T.astype(jnp.float32), gate_weights.T], axis=0)]
    while len(chosen) < groups:
        sent = jnp.concatenate(chosen, axis=0)
        got = swap(sent, len(chosen) * NODE_SIZE)
        chosen += jnp.split(got, len(chosen), axis=0)
    weight = proj_weight.T
    summed = residual
    begin = 0
    after = ()
    paired = columns % LANES == 0 and tensors == 2 and len(spans) == 2
    for n, (low, count) in enumerate(spans):
        height = count * capacity
        if n:
            far = rest[2 * n - 2 : 2 * n]
        else:
            far = [first, swap(first[height:], 1)]
        parts = combine(
            chosen[low : low + count],
            [own, near, *far],
            [begin, begin, 0, 0],
            low,
            capacity,
            after,
        )
        begin += height
        after = parts[:1]
        moved = [swap(part, d * NODE_SIZE) if d else part for d, part in enumerate(parts, low)]
        if low:
            summed = add(summed, moved)
        else:
            for part in moved:
                summed = summed.astype(jnp.float32) + part.astype(jnp.float32)
    stream = summed.astype(jnp.bfloat16)
    if not paired:
        wide = lax.all_gather(stream, "tensor", axis=1, tiled=True).astype(jnp.float32)
        normed = (wide * norm_gain).astype(jnp.bfloat16)
        added = jnp.dot(normed, proj_weight, preferred_element_type=jnp.float32)
        energy = jnp.sum(wide * wide, axis=1)
        inverse = lax.rsqrt(energy / features + epsilon)
        return (stream, (added * inverse[:, None]).astype(jnp.bfloat16))
    held = [fetch(weight, columns, flip, *after) for flip in range(2)]
    stream, held = lax.optimization_barrier((stream, held))
    other = lax.ppermute(stream, "tensor", [(i, i ^ 1) for i in range(tensors)])
    gain = norm_gain.reshape(1, features)
    carried = project(gain, held[0], stream)
    (latents,) = project(gain, held[1], other, carried, features)
    return (stream, latents)


def solution(mesh):
    return jax.shard_map(
        on_device,
        mesh=mesh,
        in_specs=(
            P("expert", None, None),
            P("expert", None, "tensor"),
            P("expert", None),
            P("expert", None),
            P("expert", "tensor"),
            P(),
            P(None, "tensor"),
        ),
        out_specs=(P("expert", "tensor"), P("expert", "tensor")),
        check_vma=False,
    )
```

time: 57.8 us -> 42.3 us (0.73)
  matrix products: 19.3 us -> 0 us
  Pallas kernels: 0 us -> 18.2 us
  waiting for transfers between devices: 18.6 us -> 6.48 us
  starting transfers between devices: 7.49 us -> 15.6 us
  blocking collectives: 6.16 us -> 0 us
  local copies, waits for them, and re-layouts: 4.11 us -> 1.07 us
  other arithmetic: 0.97 us -> 0.06 us
    dot_general x3 -> x0, matrix products: 19.3 us -> none  [the longest x1 9.95 us: on_device(): jnp.dot(normed_part, proj_weight, preferred_element_type=jnp.float32)]
    all_to_all x1 -> x0, waiting for transfers between devices: 18.6 us -> none  [on_device(): lax.all_to_all(grouped, 'expert', split_axis=1, concat_axis=0, tiled=True)]
    pallas_call x0 -> x8, Pallas kernels: none -> 18.2 us  [the longest x2 6.6 us: fetch(): pl.pallas_call(functools.partial(fetch_kernel, columns, flip, pieces), ou...]
    ppermute x0 -> x11, starting transfers between devices: none -> 15.6 us  [the longest x10 14 us: swap(): lax.ppermute(value, 'expert', [(i, i ^ bits) for i in range(experts)])]
    all_to_all x1 -> x0, starting transfers between devices: 7.49 us -> none  [on_device(): lax.all_to_all(grouped, 'expert', split_axis=1, concat_axis=0, tiled=True)]
    ppermute x0 -> x11, waiting for transfers between devices: none -> 6.48 us  [the longest x10 5.25 us: swap(): lax.ppermute(value, 'expert', [(i, i ^ bits) for i in range(experts)])]
    all_gather x1 -> x0, blocking collectives: 6.16 us -> none  [on_device(): lax.all_gather(stream, 'tensor', axis=1, tiled=True).astype(jnp.float32)]
    gather x6 -> x0, local copies, waits for them, and re-layouts: 2.7 us -> none  [the longest x5 1.58 us: on_device(): slot_index = jnp.take_along_axis(before, expert_ids, axis=1)]
  transfers between devices with their start and end apart: 1 -> 11, of which waited for: 1 -> 4; matrix products, arithmetic and copies ran while one was open for 4% -> 0% of each run, Pallas kernels for 0% -> 23%
where the time goes in v2:
time: 42.3 us; the launch traced here: 42.1 us
  Pallas kernels  18.2 us (43%)
  starting transfers between devices  15.6 us (37%)
  waiting for transfers between devices  6.48 us (15%)
  local copies, waits for them, and re-layouts  1.07 us (3%)
  between operations  0.75 us (2%)
    ppermute x10, starting transfers between devices, swap(): lax.ppermute(value, 'expert', [(i, i ^ bits) for i in range(experts)])  14 us
    pallas_call x2, Pallas kernels, fetch(): pl.pallas_call(functools.partial(fetch_kernel, columns, flip, pieces), ou...  6.6 us
    pallas_call x1, Pallas kernels, down(): pl.pallas_call(functools.partial(down_kernel, experts, outputs, block), o...  5.9 us
    ppermute x10, waiting for transfers between devices, swap(): lax.ppermute(value, 'expert', [(i, i ^ bits) for i in range(experts)])  5.25 us
    pallas_call x2, Pallas kernels, project(): pl.pallas_call(functools.partial(project_kernel, block, features), out_sh...  4.74 us
    ppermute x1, starting transfers between devices, on_device(): other = lax.ppermute(stream, 'tensor', [(i, i ^ 1) for i in range(tensors)])  1.58 us
    ppermute x1, waiting for transfers between devices, on_device(): other = lax.ppermute(stream, 'tensor', [(i, i ^ 1) for i in range(tensors)])  1.23 us
    unnamed x12, local copies, waits for them, and re-layouts  1.06 us
  transfers between devices with their start and end apart: 11, of which 4 were waited for; matrix products, arithmetic and copies ran while one was open for 0% of the time, Pallas kernels for 23%

profile of v2, /device:TPU:0, one launch (start us, length us, event | category | flops | bytes accessed | tf_op | source)
XLA Modules:
  0.0 42.1 jit_solution(9247361967661811361)
XLA Ops:
  0.6 0.0 copy-start
  0.6 1.0 %copy-done = bf16[1,128,2048]{2,1,0:T(8,128)(2,1)S(1)} copy-done((bf16[1,128,2048]{2,1,0:T(8,128)(2,1)S(1)}, bf16[1,128,2048]{2,1,0:T(8,128)(2,1)}, u32[]{:S(2)}) %copy-start) | copy-done | bytes 524312
  1.7 0.0 copy-start.5
  1.7 0.0 copy-start.4
  1.7 5.9 %down.1 = (bf16[32,3584]{1,0:T(8,128)(2,1)S(1)}, bf16[32,3584]{1,0:T(8,128)(2,1)S(1)}, bf16[32,3584]{1,0:T(8,128)(2,1)S(1)}, bf16[16,3584]{1,0:T(8,128)(2,1)S(1)}, bf16[16,3584]{1,0:T(8,128)(2,1)S(1)}) custom-call(bf16[1,128,2048]{2,1,0:T(8,128)(2,1)S(1)} %copy-done, bf16[1,2048,3584]{2,1,0:T(8,128)(2,1)} %weight_hbm.1), custom_call_target="tpu_custom_call" | custom-call | flops 1879048192 | bytes 14680064 | tf_op jit(solution)/shard_map/down/pallas_call | solution.py:104
  7.6 3.0 %collective-permute-start.3 = (bf16[32,3584]{1,0:T(8,128)(2,1)S(1)}, bf16[32,3584]{1,0:T(8,128)(2,1)S(1)}, u32[]{:S(2)}, u32[]{:S(2)}) collective-permute-start(bf16[32,3584]{1,0:T(8,128)(2,1)S(1)} %get-tuple-element.32), channel_id=1, source_target_pairs={{0,4},{2,6},{4,0},{6,2},{8,12},{10,14},{12,8},{14,10},{16,20},{18,... | collective-permute-start | bytes 688136 | tf_op jit(solution)/shard_map/ppermute | solution.py:308
  10.6 0.0 copy-done.5
  10.6 0.0 copy-done.4
  10.6 1.6 %collective-permute-start = (f32[16,16]{1,0:T(8,128)S(1)}, f32[16,16]{1,0:T(8,128)S(1)}, u32[]{:S(2)}, u32[]{:S(2)}) collective-permute-start(f32[16,16]{1,0:T(8,128)S(1)} %pad_maximum_fusion.1.refs_0_), channel_id=1, source_target_pairs={{0,8},{2,10},{4,12},{6,14},{8,0},{10,2},{12,4},{14,6},{16,24},{18,... | collective-permute-start | bytes 3080 | tf_op jit(solution)/shard_map/ppermute | solution.py:308
  12.2 0.0 collective-permute-start.2
  12.2 2.1 %collective-permute-done.refs_1_ = f32[16,16]{1,0:T(8,128)S(1)} collective-permute-done((f32[16,16]{1,0:T(8,128)S(1)}, f32[16,16]{1,0:T(8,128)S(1)}, u32[]{:S(2)}, u32[]{:S(2)}) %collective-permute-start) | collective-permute-done | bytes 1056 | tf_op jit(solution)/shard_map/ppermute | solution.py:308
  14.3 2.6 %collective-permute-start.1 = (f32[32,16]{1,0:T(8,128)S(1)}, f32[32,16]{1,0:T(8,128)S(1)}, u32[]{:S(2)}, u32[]{:S(2)}) collective-permute-start(f32[32,16]{1,0:T(8,128)S(1)} %pad_maximum_fusion), channel_id=1, source_target_pairs={{0,16},{2,18},{4,20},{6,22},{8,24},{10,26},{12,28},{14,30},{16,0},... | collective-permute-start | bytes 6152 | tf_op jit(solution)/shard_map/ppermute | solution.py:308
  16.9 0.5 %collective-permute-start.7 = (bf16[16,3584]{1,0:T(8,128)(2,1)S(1)}, bf16[16,3584]{1,0:T(8,128)(2,1)S(1)}, u32[]{:S(2)}, u32[]{:S(2)}) collective-permute-start(bf16[16,3584]{1,0:T(8,128)(2,1)S(1)} %get-tuple-element.35), channel_id=1, source_target_pairs={{0,4},{2,6},{4,0},{6,2},{8,12},{10,14},{12,8},{14,10},{16,20},{18,... | collective-permute-start | bytes 344072 | tf_op jit(solution)/shard_map/ppermute | solution.py:308
  17.5 0.0 collective-permute-start.8
  17.5 0.0 collective-permute-done.3.refs_4_
  17.5 1.7 %collective-permute-start.4 = (bf16[16,3584]{1,0:T(8,128)(2,1)S(1)}, bf16[16,3584]{1,0:T(8,128)(2,1)S(1)}, u32[]{:S(2)}, u32[]{:S(2)}) collective-permute-start(bf16[16,3584]{1,0:T(8,128)(2,1)S(1)} %slice.4), channel_id=1, source_target_pairs={{0,2},{2,0},{4,6},{6,4},{8,10},{10,8},{12,14},{14,12},{16,18},{18,... | collective-permute-start | bytes 344072 | tf_op jit(solution)/shard_map/ppermute | solution.py:308
  19.1 0.0 collective-permute-done.1
  19.1 0.0 collective-permute-done.2.refs_3_
  19.2 1.0 %collective-permute-done.4.refs_5_ = bf16[16,3584]{1,0:T(8,128)(2,1)S(1)} collective-permute-done((bf16[16,3584]{1,0:T(8,128)(2,1)S(1)}, bf16[16,3584]{1,0:T(8,128)(2,1)S(1)}, u32[]{:S(2)}, u32[]{:S(2)}) %collective-permute-start.4) | collective-permute-done | bytes 114720 | tf_op jit(solution)/shard_map/ppermute | solution.py:308
  20.1 0.5 %combine.2 = (bf16[16,3584]{1,0:T(8,128)(2,1)S(1)}, bf16[16,3584]{1,0:T(8,128)(2,1)S(1)}) custom-call(f32[16,16]{1,0:T(8,128)S(1)} %get-tuple-element.45.refs_0_, f32[16,16]{1,0:T(8,128)S(1)} %get-tuple-element.44.refs_1_, bf16[32,3584]{1,0:T(8,128)(2,1)S(1)} %get-tuple-element.30.refs_2_, bf16[32,3584]{1,0:T(8,128)(2,1)S(1)} %collective-permute-done.2.refs_3_, ...), custom_call_target="tpu_custom_call" | custom-call | flops 58720256 | bytes 458752 | tf_op jit(solution)/shard_map/combine/pallas_call | solution.py:178
  20.6 2.6 %collective-permute-start.6 = (bf16[16,3584]{1,0:T(8,128)(2,1)S(1)}, bf16[16,3584]{1,0:T(8,128)(2,1)S(1)}, u32[]{:S(2)}, u32[]{:S(2)}) collective-permute-start(bf16[16,3584]{1,0:T(8,128)(2,1)S(1)} %get-tuple-element.34), channel_id=1, source_target_pairs={{0,24},{2,26},{4,28},{6,30},{8,16},{10,18},{12,20},{14,22},{16,8},... | collective-permute-start | bytes 344072 | tf_op jit(solution)/shard_map/ppermute | solution.py:308
  23.2 0.5 %collective-permute-start.5 = (bf16[16,3584]{1,0:T(8,128)(2,1)S(1)}, bf16[16,3584]{1,0:T(8,128)(2,1)S(1)}, u32[]{:S(2)}, u32[]{:S(2)}) collective-permute-start(bf16[16,3584]{1,0:T(8,128)(2,1)S(1)} %get-tuple-element.33.refs_6_), channel_id=1, source_target_pairs={{0,16},{2,18},{4,20},{6,22},{8,24},{10,26},{12,28},{14,30},{16,0},... | collective-permute-start | bytes 344072 | tf_op jit(solution)/shard_map/ppermute | solution.py:308
  23.7 0.0 collective-permute-done.7.refs_4_
  23.7 0.0 collective-permute-done.8.refs_5_
  23.7 0.5 %combine.3 = (bf16[16,3584]{1,0:T(8,128)(2,1)S(1)}, bf16[16,3584]{1,0:T(8,128)(2,1)S(1)}) custom-call(f32[16,16]{1,0:T(8,128)S(1)} %pad_maximum_fusion.1.refs_0_, f32[16,16]{1,0:T(8,128)S(1)} %collective-permute-done.refs_1_, bf16[32,3584]{1,0:T(8,128)(2,1)S(1)} %get-tuple-element.30.refs_2_, bf16[32,3584]{1,0:T(8,128)(2,1)S(1)} %collective-permute-done.2.refs_3_, ...), custom_call_target="tpu_custom_call" | custom-call | flops 58720256 | bytes 458752 | tf_op jit(solution)/shard_map/combine/pallas_call | solution.py:178
  24.2 1.4 %collective-permute-start.9 = (bf16[16,3584]{1,0:T(8,128)(2,1)S(1)}, bf16[16,3584]{1,0:T(8,128)(2,1)S(1)}, u32[]{:S(2)}, u32[]{:S(2)}) collective-permute-start(bf16[16,3584]{1,0:T(8,128)(2,1)S(1)} %get-tuple-element.38), channel_id=1, source_target_pairs={{0,8},{2,10},{4,12},{6,14},{8,0},{10,2},{12,4},{14,6},{16,24},{18,... | collective-permute-start | bytes 344072 | tf_op jit(solution)/shard_map/ppermute | solution.py:308
  25.6 3.3 %fetch.3.refs_1_ = bf16[1056,3584]{1,0:T(8,128)(2,1)S(1)} custom-call(bf16[1056,7168]{1,0:T(8,128)(2,1)} %bitcast.7, bf16[16,3584]{1,0:T(8,128)(2,1)S(1)} %get-tuple-element.37.after_ref), custom_call_target="tpu_custom_call" | custom-call | bytes 7569408 | tf_op jit(solution)/shard_map/fetch/pallas_call | solution.py:233
  28.9 0.0 copy-start.1
  28.9 0.0 copy-start.3
  28.9 3.3 %fetch.2.refs_1_ = bf16[1056,3584]{1,0:T(8,128)(2,1)S(1)} custom-call(bf16[1056,7168]{1,0:T(8,128)(2,1)} %bitcast.8, bf16[16,3584]{1,0:T(8,128)(2,1)S(1)} %get-tuple-element.37.after_ref), custom_call_target="tpu_custom_call" | custom-call | bytes 7569408 | tf_op jit(solution)/shard_map/fetch/pallas_call | solution.py:233
  32.2 0.0 collective-permute-done.6.refs_1_
  32.2 2.2 %collective-permute-done.5.refs_0_ = bf16[16,3584]{1,0:T(8,128)(2,1)S(1)} collective-permute-done((bf16[16,3584]{1,0:T(8,128)(2,1)S(1)}, bf16[16,3584]{1,0:T(8,128)(2,1)S(1)}, u32[]{:S(2)}, u32[]{:S(2)}) %collective-permute-start.5) | collective-permute-done | bytes 114720 | tf_op jit(solution)/shard_map/ppermute | solution.py:308
  34.4 0.0 copy-done.1
  34.5 0.0 collective-permute-done.9
  34.6 0.0 copy-start.2
  34.6 1.6 %collective-permute-start.10 = (bf16[16,3584]{1,0:T(8,128)(2,1)S(1)}, bf16[16,3584]{1,0:T(8,128)(2,1)S(1)}, u32[]{:S(2)}, u32[]{:S(2)}) collective-permute-start(bf16[16,3584]{1,0:T(8,128)(2,1)S(1)} %add_convert_fusion.refs_2_), channel_id=1, source_target_pairs={{0,1},{1,0},{2,3},{3,2},{4,5},{5,4},{6,7},{7,6},{8,9},{9,8},{10,11... | collective-permute-start | bytes 344072 | tf_op jit(solution)/shard_map/ppermute | solution.py:360
  36.1 0.0 copy-done.3
  36.1 2.0 %project.2 = (f32[16,1056]{1,0:T(8,128)S(1)}, f32[16,1]{1,0:T(8,128)S(1)}) custom-call(f32[1,7168]{1,0:T(1,128)S(1)} %bitcast.5, bf16[1056,3584]{1,0:T(8,128)(2,1)S(1)} %fetch.2.refs_1_, bf16[16,3584]{1,0:T(8,128)(2,1)S(1)} %add_convert_fusion.refs_2_), custom_call_target="tpu_custom_call" | custom-call | flops 3875536896 | tf_op jit(solution)/shard_map/project/pallas_call | solution.py:285
  38.2 1.2 %collective-permute-done.10.refs_2_ = bf16[16,3584]{1,0:T(8,128)(2,1)S(1)} collective-permute-done((bf16[16,3584]{1,0:T(8,128)(2,1)S(1)}, bf16[16,3584]{1,0:T(8,128)(2,1)S(1)}, u32[]{:S(2)}, u32[]{:S(2)}) %collective-permute-start.10) | collective-permute-done | bytes 114720 | tf_op jit(solution)/shard_map/ppermute | solution.py:360
  39.4 2.7 %project.3 = bf16[16,1056]{1,0:T(8,128)(2,1)} custom-call(f32[1,7168]{1,0:T(1,128)S(1)} %bitcast.6, bf16[1056,3584]{1,0:T(8,128)(2,1)S(1)} %fetch.3.refs_1_, bf16[16,3584]{1,0:T(8,128)(2,1)S(1)} %collective-permute-done.10.refs_2_, f32[16,1056]{1,0:T(8,128)S(1)} %get-tuple-element.42.refs_3_, f32[16,1]{1,0:T(8,128)S(1)} %get-tuple-element.43.refs_4_), custom_call_target="tpu_custom_call" | custom-call | flops 3875536896 | tf_op jit(solution)/shard_map/project/pallas_call | solution.py:285
  42.1 0.0 copy-done.2
  (7 shorter events, 0.1 us)
Async XLA Ops:
  0.6 1.0 %copy-start = (bf16[1,128,2048]{2,1,0:T(8,128)(2,1)S(1)}, bf16[1,128,2048]{2,1,0:T(8,128)(2,1)}, u32[]{:S(2)}) copy-start(bf16[1,128,2048]{2,1,0:T(8,128)(2,1)} %hidden_hbm.1) | copy-start | bytes 1572868
  1.7 8.9 %copy-start.5 = (s32[16,8]{0,1:T(8,128)S(1)}, s32[16,8]{0,1:T(8,128)}, u32[]{:S(2)}) copy-start(s32[16,8]{0,1:T(8,128)} %param.9) | copy-start | bytes 1540
  1.7 8.9 %copy-start.4 = (f32[16,8]{0,1:T(8,128)S(1)}, f32[16,8]{0,1:T(8,128)}, u32[]{:S(2)}) copy-start(f32[16,8]{0,1:T(8,128)} %param.10) | copy-start | bytes 1540
  7.6 9.9 %collective-permute-start.3 = (bf16[32,3584]{1,0:T(8,128)(2,1)S(1)}, bf16[32,3584]{1,0:T(8,128)(2,1)S(1)}, u32[]{:S(2)}, u32[]{:S(2)}) collective-permute-start(bf16[32,3584]{1,0:T(8,128)(2,1)S(1)} %get-tuple-element.32), channel_id=1, source_target_pairs={{0,4},{2,6},{4,0},{6,2},{8,12},{10,14},{12,8},{14,10},{16,20},{18,... | collective-permute-start | bytes 688136 | tf_op jit(solution)/shard_map/ppermute | solution.py:308
  10.6 3.7 %collective-permute-start = (f32[16,16]{1,0:T(8,128)S(1)}, f32[16,16]{1,0:T(8,128)S(1)}, u32[]{:S(2)}, u32[]{:S(2)}) collective-permute-start(f32[16,16]{1,0:T(8,128)S(1)} %pad_maximum_fusion.1.refs_0_), channel_id=1, source_target_pairs={{0,8},{2,10},{4,12},{6,14},{8,0},{10,2},{12,4},{14,6},{16,24},{18,... | collective-permute-start | bytes 3080 | tf_op jit(solution)/shard_map/ppermute | solution.py:308
  12.2 6.9 %collective-permute-start.2 = (bf16[32,3584]{1,0:T(8,128)(2,1)S(1)}, bf16[32,3584]{1,0:T(8,128)(2,1)S(1)}, u32[]{:S(2)}, u32[]{:S(2)}) collective-permute-start(bf16[32,3584]{1,0:T(8,128)(2,1)S(1)} %get-tuple-element.31), channel_id=1, source_target_pairs={{0,2},{2,0},{4,6},{6,4},{8,10},{10,8},{12,14},{14,12},{16,18},{18,... | collective-permute-start | bytes 688136 | tf_op jit(solution)/shard_map/ppermute | solution.py:308
  14.3 4.8 %collective-permute-start.1 = (f32[32,16]{1,0:T(8,128)S(1)}, f32[32,16]{1,0:T(8,128)S(1)}, u32[]{:S(2)}, u32[]{:S(2)}) collective-permute-start(f32[32,16]{1,0:T(8,128)S(1)} %pad_maximum_fusion), channel_id=1, source_target_pairs={{0,16},{2,18},{4,20},{6,22},{8,24},{10,26},{12,28},{14,30},{16,0},... | collective-permute-start | bytes 6152 | tf_op jit(solution)/shard_map/ppermute | solution.py:308
  16.9 6.8 %collective-permute-start.7 = (bf16[16,3584]{1,0:T(8,128)(2,1)S(1)}, bf16[16,3584]{1,0:T(8,128)(2,1)S(1)}, u32[]{:S(2)}, u32[]{:S(2)}) collective-permute-start(bf16[16,3584]{1,0:T(8,128)(2,1)S(1)} %get-tuple-element.35), channel_id=1, source_target_pairs={{0,4},{2,6},{4,0},{6,2},{8,12},{10,14},{12,8},{14,10},{16,20},{18,... | collective-permute-start | bytes 344072 | tf_op jit(solution)/shard_map/ppermute | solution.py:308
  17.5 6.3 %collective-permute-start.8 = (bf16[16,3584]{1,0:T(8,128)(2,1)S(1)}, bf16[16,3584]{1,0:T(8,128)(2,1)S(1)}, u32[]{:S(2)}, u32[]{:S(2)}) collective-permute-start(bf16[16,3584]{1,0:T(8,128)(2,1)S(1)} %get-tuple-element.36), channel_id=1, source_target_pairs={{0,6},{2,4},{4,2},{6,0},{8,14},{10,12},{12,10},{14,8},{16,22},{18,... | collective-permute-start | bytes 344072 | tf_op jit(solution)/shard_map/ppermute | solution.py:308
  17.5 2.6 %collective-permute-start.4 = (bf16[16,3584]{1,0:T(8,128)(2,1)S(1)}, bf16[16,3584]{1,0:T(8,128)(2,1)S(1)}, u32[]{:S(2)}, u32[]{:S(2)}) collective-permute-start(bf16[16,3584]{1,0:T(8,128)(2,1)S(1)} %slice.4), channel_id=1, source_target_pairs={{0,2},{2,0},{4,6},{6,4},{8,10},{10,8},{12,14},{14,12},{16,18},{18,... | collective-permute-start | bytes 344072 | tf_op jit(solution)/shard_map/ppermute | solution.py:308
  20.6 11.7 %collective-permute-start.6 = (bf16[16,3584]{1,0:T(8,128)(2,1)S(1)}, bf16[16,3584]{1,0:T(8,128)(2,1)S(1)}, u32[]{:S(2)}, u32[]{:S(2)}) collective-permute-start(bf16[16,3584]{1,0:T(8,128)(2,1)S(1)} %get-tuple-element.34), channel_id=1, source_target_pairs={{0,24},{2,26},{4,28},{6,30},{8,16},{10,18},{12,20},{14,22},{16,8},... | collective-permute-start | bytes 344072 | tf_op jit(solution)/shard_map/ppermute | solution.py:308
  23.2 11.3 %collective-permute-start.5 = (bf16[16,3584]{1,0:T(8,128)(2,1)S(1)}, bf16[16,3584]{1,0:T(8,128)(2,1)S(1)}, u32[]{:S(2)}, u32[]{:S(2)}) collective-permute-start(bf16[16,3584]{1,0:T(8,128)(2,1)S(1)} %get-tuple-element.33.refs_6_), channel_id=1, source_target_pairs={{0,16},{2,18},{4,20},{6,22},{8,24},{10,26},{12,28},{14,30},{16,0},... | collective-permute-start | bytes 344072 | tf_op jit(solution)/shard_map/ppermute | solution.py:308
  24.2 10.3 %collective-permute-start.9 = (bf16[16,3584]{1,0:T(8,128)(2,1)S(1)}, bf16[16,3584]{1,0:T(8,128)(2,1)S(1)}, u32[]{:S(2)}, u32[]{:S(2)}) collective-permute-start(bf16[16,3584]{1,0:T(8,128)(2,1)S(1)} %get-tuple-element.38), channel_id=1, source_target_pairs={{0,8},{2,10},{4,12},{6,14},{8,0},{10,2},{12,4},{14,6},{16,24},{18,... | collective-permute-start | bytes 344072 | tf_op jit(solution)/shard_map/ppermute | solution.py:308
  28.9 5.6 %copy-start.1 = (bf16[16,3584]{1,0:T(8,128)(2,1)S(1)}, bf16[16,3584]{1,0:T(8,128)(2,1)}, u32[]{:S(2)}) copy-start(bf16[16,3584]{1,0:T(8,128)(2,1)} %base_ref.1) | copy-start | bytes 344068
  28.9 7.3 %copy-start.3 = (f32[7168]{0:T(1024)S(1)}, f32[7168]{0:T(1024)}, u32[]{:S(2)}) copy-start(f32[7168]{0:T(1024)} %param.12) | copy-start | bytes 86020
  34.6 7.6 %copy-start.2 = (bf16[16,3584]{1,0:T(8,128)(2,1)}, bf16[16,3584]{1,0:T(8,128)(2,1)S(1)}, u32[]{:S(2)}) copy-start(bf16[16,3584]{1,0:T(8,128)(2,1)S(1)} %add_convert_fusion.refs_2_) | copy-start | bytes 344068
  34.6 4.9 %collective-permute-start.10 = (bf16[16,3584]{1,0:T(8,128)(2,1)S(1)}, bf16[16,3584]{1,0:T(8,128)(2,1)S(1)}, u32[]{:S(2)}, u32[]{:S(2)}) collective-permute-start(bf16[16,3584]{1,0:T(8,128)(2,1)S(1)} %add_convert_fusion.refs_2_), channel_id=1, source_target_pairs={{0,1},{1,0},{2,3},{3,2},{4,5},{5,4},{6,7},{7,6},{8,9},{9,8},{10,11... | collective-permute-start | bytes 344072 | tf_op jit(solution)/shard_map/ppermute | solution.py:360

commit v3 on v2

--- a/solution.py
+++ b/solution.py
@@ -10,6 +10,8 @@
 NODE_SIZE = 4
 LANES = 128
 MIB = 1 << 20
+AHEAD = 3
+DEPTH_STEPS = 8
 ADD_COST = 64 * MIB
 
 
@@ -47,19 +49,20 @@
     return outputs
 
 
-def down_kernel(experts, outputs, block, hidden_hbm, weight_hbm, *refs):
+def down_kernel(experts, outputs, hidden_hbm, weight_hbm, *refs):
     out_refs = refs[: len(outputs)]
-    hidden, wide, ordered, weights, hidden_sem, weight_sems = refs[len(outputs) :]
+    hidden, wide, ordered, weights, total, hidden_sem, weight_sems = refs[len(outputs) :]
     index = lax.axis_index("expert")
+    steps, depth = weights.shape[:2]
     first_copy = pltpu.make_async_copy(hidden_hbm.at[0], hidden, hidden_sem)
     copies = [
         pltpu.make_async_copy(
-            weight_hbm.at[0, :, pl.ds(i * block, block)], weights.at[i], weight_sems.at[i]
+            weight_hbm.at[0, pl.ds(i * depth, depth)], weights.at[i], weight_sems.at[i]
         )
-        for i in range(weights.shape[0])
+        for i in range(steps)
     ]
     first_copy.start()
-    for copy in copies:
+    for copy in copies[:AHEAD]:
         copy.start()
     rows = hidden.shape[0]
     capacity = rows // experts
@@ -82,27 +85,39 @@
                 )
                 start += 2 * capacity
     starts.append(start)
+    columns = total.shape[1]
+    block = block_width(columns)
     for i, copy in enumerate(copies):
         copy.wait()
-        product = jnp.dot(
-            ordered[...], weights[i], preferred_element_type=jnp.float32
-        ).astype(jnp.bfloat16)
-        for ref, begin, end in zip(out_refs, starts[:-1], starts[1:]):
-            ref[:, i * block : (i + 1) * block] = product[begin:end, :]
+        if i + AHEAD < steps:
+            copies[i + AHEAD].start()
+        for first in range(0, columns, block):
+            product = jnp.dot(
+                ordered[:, i * depth : (i + 1) * depth],
+                weights[i, :, first : first + block],
+                preferred_element_type=jnp.float32,
+            )
+            if i:
+                product = total[:, first : first + block] + product
+            if i < steps - 1:
+                total[:, first : first + block] = product
+            else:
+                rounded = product.astype(jnp.bfloat16)
+                for ref, begin, end in zip(out_refs, starts[:-1], starts[1:]):
+                    ref[:, first : first + block] = rounded[begin:end, :]
 
 
 def down(hidden, down_weight, experts, spans):
     rows, depth = hidden.shape[1:]
     columns = down_weight.shape[2]
     capacity = rows // experts
-    block = block_width(columns)
     outputs = pieces_of(spans)
     out_shape = [
         shape_of((sum(count for _, _, count in pieces) * capacity, columns), jnp.bfloat16)
         for pieces in outputs
     ]
     return pl.pallas_call(
-        functools.partial(down_kernel, experts, outputs, block),
+        functools.partial(down_kernel, experts, outputs),
         out_shape=out_shape,
         in_specs=[ANY, ANY],
         out_specs=[VMEM] * len(out_shape),
@@ -110,15 +125,16 @@
             pltpu.VMEM((rows, depth), jnp.bfloat16),
             pltpu.VMEM((rows, depth), jnp.float32),
             pltpu.VMEM((rows, depth), jnp.bfloat16),
-            pltpu.VMEM((columns // block, depth, block), jnp.bfloat16),
+            pltpu.VMEM((DEPTH_STEPS, depth // DEPTH_STEPS, columns), jnp.bfloat16),
+            pltpu.VMEM((rows, columns), jnp.float32),
             pltpu.SemaphoreType.DMA(()),
-            pltpu.SemaphoreType.DMA((columns // block,)),
+            pltpu.SemaphoreType.DMA((DEPTH_STEPS,)),
         ],
         name="down",
         cost_estimate=pl.CostEstimate(
             flops=2 * rows * depth * columns, bytes_accessed=2 * depth * columns, transcendentals=0
         ),
-        compiler_params=pltpu.CompilerParams(vmem_limit_bytes=50 * MIB),
+        compiler_params=pltpu.CompilerParams(vmem_limit_bytes=53 * MIB),
     )(hidden, down_weight)
 
 
@@ -211,31 +227,35 @@
     )(base, *parts)
 
 
-def fetch_kernel(columns, flip, pieces, source_hbm, after_ref, out_ref, sems):
-    width = columns // pieces
+def fetch_kernel(columns, flip, source_hbm, after_ref, out_ref, pieces, sems):
+    width = pieces.shape[2]
     base = (lax.axis_index("tensor") ^ flip) * columns
     copies = [
         pltpu.make_async_copy(
             source_hbm.at[:, pl.ds(pl.multiple_of(base + i * width, LANES), width)],
-            out_ref.at[:, pl.ds(i * width, width)],
+            pieces.at[i],
             sems.at[i],
         )
-        for i in range(pieces)
+        for i in range(columns // width)
     ]
     for copy in copies:
         copy.start()
-    for copy in copies:
+    for i, copy in enumerate(copies):
         copy.wait()
+        out_ref[i * width : (i + 1) * width, :] = pieces[i].T
 
 
 def fetch(source, columns, flip, after):
-    pieces = 4 if columns // 4 % LANES == 0 else 1
+    width = block_width(columns)
     return pl.pallas_call(
-        functools.partial(fetch_kernel, columns, flip, pieces),
-        out_shape=pltpu.VMEM((source.shape[0], columns), source.dtype),
+        functools.partial(fetch_kernel, columns, flip),
+        out_shape=pltpu.VMEM((columns, source.shape[0]), source.dtype),
         in_specs=[ANY, ANY],
         out_specs=VMEM,
-        scratch_shapes=[pltpu.SemaphoreType.DMA((pieces,))],
+        scratch_shapes=[
+            pltpu.VMEM((columns // width, source.shape[0], width), source.dtype),
+            pltpu.SemaphoreType.DMA((columns // width,)),
+        ],
         name="fetch",
         cost_estimate=pl.CostEstimate(
             flops=0, bytes_accessed=2 * source.shape[0] * columns, transcendentals=0
@@ -244,15 +264,15 @@
     )(source, after)
 
 
-def project_kernel(block, features, *refs):
+def project_kernel(flip, block, carried, features, *refs):
     gain_ref, weight_ref, section_ref = refs[:3]
     refs = refs[3:]
     columns = section_ref.shape[1]
-    base = lax.axis_index("tensor")
+    base = lax.axis_index("tensor") ^ flip
     total = energy = None
-    if features:
-        base = base ^ 1
+    if carried:
         total, energy = refs[0][...], refs[1][...]
+        refs = refs[2:]
     for i in range(0, columns, block):
         wide = section_ref[:, i : i + block].astype(jnp.float32)
         square = jnp.sum(wide * wide, axis=1, keepdims=True)
@@ -260,36 +280,36 @@
         normed = (wide * gain_ref[:, pl.ds(begin, block)]).astype(jnp.bfloat16)
         product = lax.dot_general(
             normed,
-            weight_ref[:, i : i + block],
-            (((1,), (1,)), ((), ())),
+            weight_ref[i : i + block, :],
+            (((1,), (0,)), ((), ())),
             preferred_element_type=jnp.float32,
         )
         total = product if total is None else total + product
         energy = square if energy is None else energy + square
     if features:
         scale = lax.rsqrt(energy / features + epsilon)
-        refs[2][...] = (total * scale).astype(jnp.bfloat16)
+        refs[0][...] = (total * scale).astype(jnp.bfloat16)
     else:
         refs[0][...] = total
         refs[1][...] = energy
 
 
-def project(gain, weight, section, carried=(), features=0):
-    tokens, columns = section.shape
-    latents = weight.shape[0]
-    block = columns // 4 if columns // 4 % LANES == 0 else columns
+def project(gain, weight, section, flip=0, carried=(), features=0):
+    tokens, width = section.shape
+    latents = weight.shape[1]
+    block = width // 2 if width // 2 % LANES == 0 else width
     if features:
         out_shape = [shape_of((tokens, latents), jnp.bfloat16)]
     else:
         out_shape = [shape_of((tokens, latents), jnp.float32), shape_of((tokens, 1), jnp.float32)]
     return pl.pallas_call(
-        functools.partial(project_kernel, block, features),
+        functools.partial(project_kernel, flip, block, bool(carried), features),
         out_shape=out_shape,
         in_specs=[VMEM] * (3 + len(carried)),
         out_specs=[VMEM] * len(out_shape),
         name="project",
         cost_estimate=pl.CostEstimate(
-            flops=64 * tokens * latents * columns, bytes_accessed=0, transcendentals=0
+            flops=64 * tokens * latents * width, bytes_accessed=0, transcendentals=0
         ),
         compiler_params=pltpu.CompilerParams(vmem_limit_bytes=8 * MIB),
     )(gain, weight, section, *carried)
@@ -360,7 +380,7 @@
     other = lax.ppermute(stream, "tensor", [(i, i ^ 1) for i in range(tensors)])
     gain = norm_gain.reshape(1, features)
     carried = project(gain, held[0], stream)
-    (latents,) = project(gain, held[1], other, carried, features)
+    (latents,) = project(gain, held[1], other, 1, carried, features)
     return (stream, latents)
 
 

time: 42.3 us -> 41.1 us (0.972)
  local copies, waits for them, and re-layouts: 1.07 us -> 0.04 us
    ppermute x10, waiting for transfers between devices: 5.25 us -> 4.15 us  [swap(): lax.ppermute(value, 'expert', [(i, i ^ bits) for i in range(experts)])]
    unnamed x12 -> x10, local copies, waits for them, and re-layouts: 1.06 us -> 0.03 us
    ppermute x1, waiting for transfers between devices: 1.23 us -> 2.1 us  [on_device(): other = lax.ppermute(stream, 'tensor', [(i, i ^ 1) for i in range(tensors)])]
  transfers between devices with their start and end apart: 11 -> 11, of which waited for: 4 -> 4; matrix products, arithmetic and copies ran while one was open for 0% -> 0% of each run, Pallas kernels for 23% -> 24%
where the time goes in v3:
time: 41.1 us; the launch traced here: 41 us
  Pallas kernels  18.3 us (45%)
  starting transfers between devices  15.6 us (38%)
  waiting for transfers between devices  6.26 us (15%)
  between operations  0.76 us (2%)
    ppermute x10, starting transfers between devices, swap(): lax.ppermute(value, 'expert', [(i, i ^ bits) for i in range(experts)])  14 us
    pallas_call x2, Pallas kernels, fetch(): pl.pallas_call(functools.partial(fetch_kernel, columns, flip), out_shape=...  7.69 us
    pallas_call x1, Pallas kernels, down(): pl.pallas_call(functools.partial(down_kernel, experts, outputs), out_shap...  6.65 us
    ppermute x10, waiting for transfers between devices, swap(): lax.ppermute(value, 'expert', [(i, i ^ bits) for i in range(experts)])  4.15 us
    pallas_call x2, Pallas kernels, project(): pl.pallas_call(functools.partial(project_kernel, flip, block, bool(carrie...  2.97 us
    ppermute x1, waiting for transfers between devices, on_device(): other = lax.ppermute(stream, 'tensor', [(i, i ^ 1) for i in range(tensors)])  2.1 us
    ppermute x1, starting transfers between devices, on_device(): other = lax.ppermute(stream, 'tensor', [(i, i ^ 1) for i in range(tensors)])  1.58 us
    pallas_call x2, Pallas kernels, combine(): pl.pallas_call(functools.partial(combine_kernel, low, count, capacity, be...  0.93 us
  transfers between devices with their start and end apart: 11, of which 4 were waited for; matrix products, arithmetic and copies ran while one was open for 0% of the time, Pallas kernels for 24%

profile of v3, /device:TPU:0, one launch (start us, length us, event | category | flops | bytes accessed | tf_op | source)
XLA Modules:
  0.0 41.0 jit_solution(14154106682824630227)
XLA Ops:
  0.6 0.0 copy-start.3
  0.6 0.0 copy-start.4
  0.7 6.7 %down.1 = (bf16[32,3584]{1,0:T(8,128)(2,1)S(1)}, bf16[32,3584]{1,0:T(8,128)(2,1)S(1)}, bf16[32,3584]{1,0:T(8,128)(2,1)S(1)}, bf16[16,3584]{1,0:T(8,128)(2,1)S(1)}, bf16[16,3584]{1,0:T(8,128)(2,1)S(1)}) custom-call(bf16[1,128,2048]{2,1,0:T(8,128)(2,1)} %hidden_hbm.1, bf16[1,2048,3584]{2,1,0:T(8,128)(2,1)} %weight_hbm.1), custom_call_target="tpu_custom_call" | custom-call | flops 1879048192 | bytes 14680064 | tf_op jit(solution)/shard_map/down/pallas_call | solution.py:119
  7.3 3.0 %collective-permute-start.3 = (bf16[32,3584]{1,0:T(8,128)(2,1)S(1)}, bf16[32,3584]{1,0:T(8,128)(2,1)S(1)}, u32[]{:S(2)}, u32[]{:S(2)}) collective-permute-start(bf16[32,3584]{1,0:T(8,128)(2,1)S(1)} %get-tuple-element.32), channel_id=1, source_target_pairs={{0,4},{2,6},{4,0},{6,2},{8,12},{10,14},{12,8},{14,10},{16,20},{18,... | collective-permute-start | bytes 688136 | tf_op jit(solution)/shard_map/ppermute | solution.py:328
  10.3 0.0 copy-done.4
  10.3 0.0 copy-done.3
  10.3 1.6 %collective-permute-start = (f32[16,16]{1,0:T(8,128)S(1)}, f32[16,16]{1,0:T(8,128)S(1)}, u32[]{:S(2)}, u32[]{:S(2)}) collective-permute-start(f32[16,16]{1,0:T(8,128)S(1)} %pad_maximum_fusion.1.refs_0_), channel_id=1, source_target_pairs={{0,8},{2,10},{4,12},{6,14},{8,0},{10,2},{12,4},{14,6},{16,24},{18,... | collective-permute-start | bytes 3080 | tf_op jit(solution)/shard_map/ppermute | solution.py:328
  12.0 0.0 collective-permute-start.2
  12.0 2.1 %collective-permute-done.refs_1_ = f32[16,16]{1,0:T(8,128)S(1)} collective-permute-done((f32[16,16]{1,0:T(8,128)S(1)}, f32[16,16]{1,0:T(8,128)S(1)}, u32[]{:S(2)}, u32[]{:S(2)}) %collective-permute-start) | collective-permute-done | bytes 1056 | tf_op jit(solution)/shard_map/ppermute | solution.py:328
  14.1 2.6 %collective-permute-start.1 = (f32[32,16]{1,0:T(8,128)S(1)}, f32[32,16]{1,0:T(8,128)S(1)}, u32[]{:S(2)}, u32[]{:S(2)}) collective-permute-start(f32[32,16]{1,0:T(8,128)S(1)} %pad_maximum_fusion), channel_id=1, source_target_pairs={{0,16},{2,18},{4,20},{6,22},{8,24},{10,26},{12,28},{14,30},{16,0},... | collective-permute-start | bytes 6152 | tf_op jit(solution)/shard_map/ppermute | solution.py:328
  16.6 0.5 %collective-permute-start.7 = (bf16[16,3584]{1,0:T(8,128)(2,1)S(1)}, bf16[16,3584]{1,0:T(8,128)(2,1)S(1)}, u32[]{:S(2)}, u32[]{:S(2)}) collective-permute-start(bf16[16,3584]{1,0:T(8,128)(2,1)S(1)} %get-tuple-element.35), channel_id=1, source_target_pairs={{0,4},{2,6},{4,0},{6,2},{8,12},{10,14},{12,8},{14,10},{16,20},{18,... | collective-permute-start | bytes 344072 | tf_op jit(solution)/shard_map/ppermute | solution.py:328
  17.2 0.0 collective-permute-start.8
  17.2 0.0 collective-permute-done.3.refs_4_
  17.2 1.7 %collective-permute-start.4 = (bf16[16,3584]{1,0:T(8,128)(2,1)S(1)}, bf16[16,3584]{1,0:T(8,128)(2,1)S(1)}, u32[]{:S(2)}, u32[]{:S(2)}) collective-permute-start(bf16[16,3584]{1,0:T(8,128)(2,1)S(1)} %slice.4), channel_id=1, source_target_pairs={{0,2},{2,0},{4,6},{6,4},{8,10},{10,8},{12,14},{14,12},{16,18},{18,... | collective-permute-start | bytes 344072 | tf_op jit(solution)/shard_map/ppermute | solution.py:328
  18.9 0.0 collective-permute-done.1
  18.9 0.0 collective-permute-done.2.refs_3_
  18.9 1.0 %collective-permute-done.4.refs_5_ = bf16[16,3584]{1,0:T(8,128)(2,1)S(1)} collective-permute-done((bf16[16,3584]{1,0:T(8,128)(2,1)S(1)}, bf16[16,3584]{1,0:T(8,128)(2,1)S(1)}, u32[]{:S(2)}, u32[]{:S(2)}) %collective-permute-start.4) | collective-permute-done | bytes 114720 | tf_op jit(solution)/shard_map/ppermute | solution.py:328
  19.8 0.5 %combine.2 = (bf16[16,3584]{1,0:T(8,128)(2,1)S(1)}, bf16[16,3584]{1,0:T(8,128)(2,1)S(1)}) custom-call(f32[16,16]{1,0:T(8,128)S(1)} %get-tuple-element.45.refs_0_, f32[16,16]{1,0:T(8,128)S(1)} %get-tuple-element.44.refs_1_, bf16[32,3584]{1,0:T(8,128)(2,1)S(1)} %get-tuple-element.30.refs_2_, bf16[32,3584]{1,0:T(8,128)(2,1)S(1)} %collective-permute-done.2.refs_3_, ...), custom_call_target="tpu_custom_call" | custom-call | flops 58720256 | bytes 458752 | tf_op jit(solution)/shard_map/combine/pallas_call | solution.py:194
  20.3 2.6 %collective-permute-start.6 = (bf16[16,3584]{1,0:T(8,128)(2,1)S(1)}, bf16[16,3584]{1,0:T(8,128)(2,1)S(1)}, u32[]{:S(2)}, u32[]{:S(2)}) collective-permute-start(bf16[16,3584]{1,0:T(8,128)(2,1)S(1)} %get-tuple-element.34), channel_id=1, source_target_pairs={{0,24},{2,26},{4,28},{6,30},{8,16},{10,18},{12,20},{14,22},{16,8},... | collective-permute-start | bytes 344072 | tf_op jit(solution)/shard_map/ppermute | solution.py:328
  22.9 0.5 %collective-permute-start.5 = (bf16[16,3584]{1,0:T(8,128)(2,1)S(1)}, bf16[16,3584]{1,0:T(8,128)(2,1)S(1)}, u32[]{:S(2)}, u32[]{:S(2)}) collective-permute-start(bf16[16,3584]{1,0:T(8,128)(2,1)S(1)} %get-tuple-element.33.refs_6_), channel_id=1, source_target_pairs={{0,16},{2,18},{4,20},{6,22},{8,24},{10,26},{12,28},{14,30},{16,0},... | collective-permute-start | bytes 344072 | tf_op jit(solution)/shard_map/ppermute | solution.py:328
  23.4 0.0 collective-permute-done.7.refs_4_
  23.4 0.0 collective-permute-done.8.refs_5_
  23.4 0.5 %combine.3 = (bf16[16,3584]{1,0:T(8,128)(2,1)S(1)}, bf16[16,3584]{1,0:T(8,128)(2,1)S(1)}) custom-call(f32[16,16]{1,0:T(8,128)S(1)} %pad_maximum_fusion.1.refs_0_, f32[16,16]{1,0:T(8,128)S(1)} %collective-permute-done.refs_1_, bf16[32,3584]{1,0:T(8,128)(2,1)S(1)} %get-tuple-element.30.refs_2_, bf16[32,3584]{1,0:T(8,128)(2,1)S(1)} %collective-permute-done.2.refs_3_, ...), custom_call_target="tpu_custom_call" | custom-call | flops 58720256 | bytes 458752 | tf_op jit(solution)/shard_map/combine/pallas_call | solution.py:194
  23.9 1.4 %collective-permute-start.9 = (bf16[16,3584]{1,0:T(8,128)(2,1)S(1)}, bf16[16,3584]{1,0:T(8,128)(2,1)S(1)}, u32[]{:S(2)}, u32[]{:S(2)}) collective-permute-start(bf16[16,3584]{1,0:T(8,128)(2,1)S(1)} %get-tuple-element.38), channel_id=1, source_target_pairs={{0,8},{2,10},{4,12},{6,14},{8,0},{10,2},{12,4},{14,6},{16,24},{18,... | collective-permute-start | bytes 344072 | tf_op jit(solution)/shard_map/ppermute | solution.py:328
  25.3 3.8 %fetch.3.refs_1_ = bf16[3584,1056]{1,0:T(8,128)(2,1)S(1)} custom-call(bf16[1056,7168]{1,0:T(8,128)(2,1)} %bitcast.7, bf16[16,3584]{1,0:T(8,128)(2,1)S(1)} %get-tuple-element.37.after_ref), custom_call_target="tpu_custom_call" | custom-call | bytes 7569408 | tf_op jit(solution)/shard_map/fetch/pallas_call | solution.py:250
  29.1 0.0 copy-start
  29.2 0.0 copy-start.2
  29.2 3.9 %fetch.2.refs_1_ = bf16[3584,1056]{1,0:T(8,128)(2,1)S(1)} custom-call(bf16[1056,7168]{1,0:T(8,128)(2,1)} %bitcast.8, bf16[16,3584]{1,0:T(8,128)(2,1)S(1)} %get-tuple-element.37.after_ref), custom_call_target="tpu_custom_call" | custom-call | bytes 7569408 | tf_op jit(solution)/shard_map/fetch/pallas_call | solution.py:250
  33.0 0.0 collective-permute-done.6.refs_1_
  33.1 1.1 %collective-permute-done.5.refs_0_ = bf16[16,3584]{1,0:T(8,128)(2,1)S(1)} collective-permute-done((bf16[16,3584]{1,0:T(8,128)(2,1)S(1)}, bf16[16,3584]{1,0:T(8,128)(2,1)S(1)}, u32[]{:S(2)}, u32[]{:S(2)}) %collective-permute-start.5) | collective-permute-done | bytes 114720 | tf_op jit(solution)/shard_map/ppermute | solution.py:328
  34.2 0.0 copy-done
  34.2 0.0 collective-permute-done.9
  34.3 0.0 copy-start.1
  34.3 1.6 %collective-permute-start.10 = (bf16[16,3584]{1,0:T(8,128)(2,1)S(1)}, bf16[16,3584]{1,0:T(8,128)(2,1)S(1)}, u32[]{:S(2)}, u32[]{:S(2)}) collective-permute-start(bf16[16,3584]{1,0:T(8,128)(2,1)S(1)} %add_convert_fusion.refs_2_), channel_id=1, source_target_pairs={{0,1},{1,0},{2,3},{3,2},{4,5},{5,4},{6,7},{7,6},{8,9},{9,8},{10,11... | collective-permute-start | bytes 344072 | tf_op jit(solution)/shard_map/ppermute | solution.py:380
  35.9 0.0 copy-done.2
  35.9 1.2 %project.2 = (f32[16,1056]{1,0:T(8,128)S(1)}, f32[16,1]{1,0:T(8,128)S(1)}) custom-call(f32[1,7168]{1,0:T(1,128)S(1)} %bitcast.5, bf16[3584,1056]{1,0:T(8,128)(2,1)S(1)} %fetch.2.refs_1_, bf16[16,3584]{1,0:T(8,128)(2,1)S(1)} %add_convert_fusion.refs_2_), custom_call_target="tpu_custom_call" | custom-call | flops 3875536896 | tf_op jit(solution)/shard_map/project/pallas_call | solution.py:305
  37.0 2.1 %collective-permute-done.10.refs_2_ = bf16[16,3584]{1,0:T(8,128)(2,1)S(1)} collective-permute-done((bf16[16,3584]{1,0:T(8,128)(2,1)S(1)}, bf16[16,3584]{1,0:T(8,128)(2,1)S(1)}, u32[]{:S(2)}, u32[]{:S(2)}) %collective-permute-start.10) | collective-permute-done | bytes 114720 | tf_op jit(solution)/shard_map/ppermute | solution.py:380
  39.1 1.8 %project.3 = bf16[16,1056]{1,0:T(8,128)(2,1)} custom-call(f32[1,7168]{1,0:T(1,128)S(1)} %bitcast.6, bf16[3584,1056]{1,0:T(8,128)(2,1)S(1)} %fetch.3.refs_1_, bf16[16,3584]{1,0:T(8,128)(2,1)S(1)} %collective-permute-done.10.refs_2_, f32[16,1056]{1,0:T(8,128)S(1)} %get-tuple-element.42.refs_3_, f32[16,1]{1,0:T(8,128)S(1)} %get-tuple-element.43.refs_4_), custom_call_target="tpu_custom_call" | custom-call | flops 3875536896 | tf_op jit(solution)/shard_map/project/pallas_call | solution.py:305
  41.0 0.0 copy-done.1
  (7 shorter events, 0.1 us)
Async XLA Ops:
  0.6 9.7 %copy-start.3 = (f32[16,8]{0,1:T(8,128)S(1)}, f32[16,8]{0,1:T(8,128)}, u32[]{:S(2)}) copy-start(f32[16,8]{0,1:T(8,128)} %param.10) | copy-start | bytes 1540
  0.6 9.7 %copy-start.4 = (s32[16,8]{0,1:T(8,128)S(1)}, s32[16,8]{0,1:T(8,128)}, u32[]{:S(2)}) copy-start(s32[16,8]{0,1:T(8,128)} %param.9) | copy-start | bytes 1540
  7.3 9.9 %collective-permute-start.3 = (bf16[32,3584]{1,0:T(8,128)(2,1)S(1)}, bf16[32,3584]{1,0:T(8,128)(2,1)S(1)}, u32[]{:S(2)}, u32[]{:S(2)}) collective-permute-start(bf16[32,3584]{1,0:T(8,128)(2,1)S(1)} %get-tuple-element.32), channel_id=1, source_target_pairs={{0,4},{2,6},{4,0},{6,2},{8,12},{10,14},{12,8},{14,10},{16,20},{18,... | collective-permute-start | bytes 688136 | tf_op jit(solution)/shard_map/ppermute | solution.py:328
  10.3 3.7 %collective-permute-start = (f32[16,16]{1,0:T(8,128)S(1)}, f32[16,16]{1,0:T(8,128)S(1)}, u32[]{:S(2)}, u32[]{:S(2)}) collective-permute-start(f32[16,16]{1,0:T(8,128)S(1)} %pad_maximum_fusion.1.refs_0_), channel_id=1, source_target_pairs={{0,8},{2,10},{4,12},{6,14},{8,0},{10,2},{12,4},{14,6},{16,24},{18,... | collective-permute-start | bytes 3080 | tf_op jit(solution)/shard_map/ppermute | solution.py:328
  12.0 6.9 %collective-permute-start.2 = (bf16[32,3584]{1,0:T(8,128)(2,1)S(1)}, bf16[32,3584]{1,0:T(8,128)(2,1)S(1)}, u32[]{:S(2)}, u32[]{:S(2)}) collective-permute-start(bf16[32,3584]{1,0:T(8,128)(2,1)S(1)} %get-tuple-element.31), channel_id=1, source_target_pairs={{0,2},{2,0},{4,6},{6,4},{8,10},{10,8},{12,14},{14,12},{16,18},{18,... | collective-permute-start | bytes 688136 | tf_op jit(solution)/shard_map/ppermute | solution.py:328
  14.1 4.8 %collective-permute-start.1 = (f32[32,16]{1,0:T(8,128)S(1)}, f32[32,16]{1,0:T(8,128)S(1)}, u32[]{:S(2)}, u32[]{:S(2)}) collective-permute-start(f32[32,16]{1,0:T(8,128)S(1)} %pad_maximum_fusion), channel_id=1, source_target_pairs={{0,16},{2,18},{4,20},{6,22},{8,24},{10,26},{12,28},{14,30},{16,0},... | collective-permute-start | bytes 6152 | tf_op jit(solution)/shard_map/ppermute | solution.py:328
  16.6 6.8 %collective-permute-start.7 = (bf16[16,3584]{1,0:T(8,128)(2,1)S(1)}, bf16[16,3584]{1,0:T(8,128)(2,1)S(1)}, u32[]{:S(2)}, u32[]{:S(2)}) collective-permute-start(bf16[16,3584]{1,0:T(8,128)(2,1)S(1)} %get-tuple-element.35), channel_id=1, source_target_pairs={{0,4},{2,6},{4,0},{6,2},{8,12},{10,14},{12,8},{14,10},{16,20},{18,... | collective-permute-start | bytes 344072 | tf_op jit(solution)/shard_map/ppermute | solution.py:328
  17.2 6.2 %collective-permute-start.8 = (bf16[16,3584]{1,0:T(8,128)(2,1)S(1)}, bf16[16,3584]{1,0:T(8,128)(2,1)S(1)}, u32[]{:S(2)}, u32[]{:S(2)}) collective-permute-start(bf16[16,3584]{1,0:T(8,128)(2,1)S(1)} %get-tuple-element.36), channel_id=1, source_target_pairs={{0,6},{2,4},{4,2},{6,0},{8,14},{10,12},{12,10},{14,8},{16,22},{18,... | collective-permute-start | bytes 344072 | tf_op jit(solution)/shard_map/ppermute | solution.py:328
  17.2 2.6 %collective-permute-start.4 = (bf16[16,3584]{1,0:T(8,128)(2,1)S(1)}, bf16[16,3584]{1,0:T(8,128)(2,1)S(1)}, u32[]{:S(2)}, u32[]{:S(2)}) collective-permute-start(bf16[16,3584]{1,0:T(8,128)(2,1)S(1)} %slice.4), channel_id=1, source_target_pairs={{0,2},{2,0},{4,6},{6,4},{8,10},{10,8},{12,14},{14,12},{16,18},{18,... | collective-permute-start | bytes 344072 | tf_op jit(solution)/shard_map/ppermute | solution.py:328
  20.3 12.7 %collective-permute-start.6 = (bf16[16,3584]{1,0:T(8,128)(2,1)S(1)}, bf16[16,3584]{1,0:T(8,128)(2,1)S(1)}, u32[]{:S(2)}, u32[]{:S(2)}) collective-permute-start(bf16[16,3584]{1,0:T(8,128)(2,1)S(1)} %get-tuple-element.34), channel_id=1, source_target_pairs={{0,24},{2,26},{4,28},{6,30},{8,16},{10,18},{12,20},{14,22},{16,8},... | collective-permute-start | bytes 344072 | tf_op jit(solution)/shard_map/ppermute | solution.py:328
  22.9 11.3 %collective-permute-start.5 = (bf16[16,3584]{1,0:T(8,128)(2,1)S(1)}, bf16[16,3584]{1,0:T(8,128)(2,1)S(1)}, u32[]{:S(2)}, u32[]{:S(2)}) collective-permute-start(bf16[16,3584]{1,0:T(8,128)(2,1)S(1)} %get-tuple-element.33.refs_6_), channel_id=1, source_target_pairs={{0,16},{2,18},{4,20},{6,22},{8,24},{10,26},{12,28},{14,30},{16,0},... | collective-permute-start | bytes 344072 | tf_op jit(solution)/shard_map/ppermute | solution.py:328
  23.9 10.3 %collective-permute-start.9 = (bf16[16,3584]{1,0:T(8,128)(2,1)S(1)}, bf16[16,3584]{1,0:T(8,128)(2,1)S(1)}, u32[]{:S(2)}, u32[]{:S(2)}) collective-permute-start(bf16[16,3584]{1,0:T(8,128)(2,1)S(1)} %get-tuple-element.38), channel_id=1, source_target_pairs={{0,8},{2,10},{4,12},{6,14},{8,0},{10,2},{12,4},{14,6},{16,24},{18,... | collective-permute-start | bytes 344072 | tf_op jit(solution)/shard_map/ppermute | solution.py:328
  29.1 5.0 %copy-start = (bf16[16,3584]{1,0:T(8,128)(2,1)S(1)}, bf16[16,3584]{1,0:T(8,128)(2,1)}, u32[]{:S(2)}) copy-start(bf16[16,3584]{1,0:T(8,128)(2,1)} %base_ref.1) | copy-start | bytes 344068
  29.2 6.7 %copy-start.2 = (f32[7168]{0:T(1024)S(1)}, f32[7168]{0:T(1024)}, u32[]{:S(2)}) copy-start(f32[7168]{0:T(1024)} %param.12) | copy-start | bytes 86020
  34.3 6.7 %copy-start.1 = (bf16[16,3584]{1,0:T(8,128)(2,1)}, bf16[16,3584]{1,0:T(8,128)(2,1)S(1)}, u32[]{:S(2)}) copy-start(bf16[16,3584]{1,0:T(8,128)(2,1)S(1)} %add_convert_fusion.refs_2_) | copy-start | bytes 344068
  34.3 4.9 %collective-permute-start.10 = (bf16[16,3584]{1,0:T(8,128)(2,1)S(1)}, bf16[16,3584]{1,0:T(8,128)(2,1)S(1)}, u32[]{:S(2)}, u32[]{:S(2)}) collective-permute-start(bf16[16,3584]{1,0:T(8,128)(2,1)S(1)} %add_convert_fusion.refs_2_), channel_id=1, source_target_pairs={{0,1},{1,0},{2,3},{3,2},{4,5},{5,4},{6,7},{7,6},{8,9},{9,8},{10,11... | collective-permute-start | bytes 344072 | tf_op jit(solution)/shard_map/ppermute | solution.py:380

commit v4 on v3

--- a/solution.py
+++ b/solution.py
@@ -34,18 +34,23 @@
     return width
 
 
-def halves(groups):
-    if groups < 4 or groups % 4:
-        return [(0, groups)]
-    return [(groups // 2, groups // 2), (0, groups // 2)]
-
-
-def pieces_of(spans):
-    outputs = [[(j, low, count) for low, count in spans] for j in (0, 1)]
-    low, count = spans[0]
-    outputs.append([(2, low, count), (3, low, count)])
-    for low, count in spans[1:]:
-        outputs += [[(2, low, count)], [(3, low, count)]]
+def stages_of(groups):
+    if groups % 4:
+        return [list(range(groups))]
+    quarter = groups // 4
+    return [
+        list(range(3 * quarter, groups)),
+        list(range(2 * quarter, 3 * quarter)),
+        list(range(2 * quarter)),
+    ]
+
+
+def pieces_of(stages):
+    outputs = [[(j, d) for stage in stages for d in stage] for j in (0, 1)]
+    for stage in stages[:-1] or stages:
+        outputs.append([(j, d) for j in (2, 3) for d in stage])
+    if len(stages) > 1:
+        outputs += [[(j, d) for d in stages[-1]] for j in (2, 3)]
     return outputs
 
 
@@ -68,23 +73,15 @@
     capacity = rows // experts
     first_copy.wait()
     wide[...] = hidden[...].astype(jnp.float32)
-    start = 0
-    starts = []
-    for pieces in outputs:
-        starts.append(start)
-        for j, low, count in pieces:
-            for d in range(low, low + count, 2):
-                pair = []
-                for other in (d, d + 1):
-                    owner = index ^ (other * NODE_SIZE + j)
-                    pair.append(
-                        wide[pl.ds(pl.multiple_of(owner * capacity, capacity), capacity), :]
-                    )
-                ordered[start : start + 2 * capacity, :] = jnp.concatenate(pair, axis=0).astype(
-                    jnp.bfloat16
-                )
-                start += 2 * capacity
-    starts.append(start)
+    order = [piece for pieces in outputs for piece in pieces]
+    for n in range(0, len(order), 2):
+        pair = []
+        for j, d in order[n : n + 2]:
+            owner = index ^ (d * NODE_SIZE + j)
+            pair.append(wide[pl.ds(pl.multiple_of(owner * capacity, capacity), capacity), :])
+        ordered[n * capacity : (n + 2) * capacity, :] = jnp.concatenate(pair, axis=0).astype(
+            jnp.bfloat16
+        )
     columns = total.shape[1]
     block = block_width(columns)
     for i, copy in enumerate(copies):
@@ -102,20 +99,19 @@
             if i < steps - 1:
                 total[:, first : first + block] = product
             else:
-                rounded = product.astype(jnp.bfloat16)
-                for ref, begin, end in zip(out_refs, starts[:-1], starts[1:]):
-                    ref[:, first : first + block] = rounded[begin:end, :]
-
-
-def down(hidden, down_weight, experts, spans):
+                begin = 0
+                for ref in out_refs:
+                    end = begin + ref.shape[0]
+                    ref[:, first : first + block] = product[begin:end].astype(jnp.bfloat16)
+                    begin = end
+
+
+def down(hidden, down_weight, experts, stages):
     rows, depth = hidden.shape[1:]
     columns = down_weight.shape[2]
     capacity = rows // experts
-    outputs = pieces_of(spans)
-    out_shape = [
-        shape_of((sum(count for _, _, count in pieces) * capacity, columns), jnp.bfloat16)
-        for pieces in outputs
-    ]
+    outputs = pieces_of(stages)
+    out_shape = [shape_of((len(pieces) * capacity, columns), jnp.bfloat16) for pieces in outputs]
     return pl.pallas_call(
         functools.partial(down_kernel, experts, outputs),
         out_shape=out_shape,
@@ -170,9 +166,10 @@
     tokens = chosen_refs[0].shape[1]
     index = lax.axis_index("expert")
     found = gates_of(index, low, count, capacity, tokens, [ref[...] for ref in chosen_refs])
+    wide = [ref[...].astype(jnp.float32) for ref in row_refs]
     rows = jnp.concatenate(
-        [ref[begin : begin + count * capacity] for ref, begin in zip(row_refs, begins)], axis=0
-    )
+        [rows[begin : begin + count * capacity] for rows, begin in zip(wide, begins)], axis=0
+    ).astype(jnp.bfloat16)
     together = count if count * tokens <= LANES else 1
     for base in range(0, count, together):
         gate = jnp.concatenate(found[base : base + together], axis=0)
@@ -227,16 +224,13 @@
     )(base, *parts)
 
 
-def fetch_kernel(columns, flip, source_hbm, after_ref, out_ref, pieces, sems):
-    width = pieces.shape[2]
-    base = (lax.axis_index("tensor") ^ flip) * columns
+def fetch_kernel(source_hbm, after_ref, out_ref, pieces, sems):
+    count, _, width = pieces.shape
     copies = [
         pltpu.make_async_copy(
-            source_hbm.at[:, pl.ds(pl.multiple_of(base + i * width, LANES), width)],
-            pieces.at[i],
-            sems.at[i],
-        )
-        for i in range(columns // width)
+            source_hbm.at[:, pl.ds(i * width, width)], pieces.at[i], sems.at[i]
+        )
+        for i in range(count)
     ]
     for copy in copies:
         copy.start()
@@ -245,20 +239,21 @@
         out_ref[i * width : (i + 1) * width, :] = pieces[i].T
 
 
-def fetch(source, columns, flip, after):
+def fetch(source, after):
+    rows, columns = source.shape
     width = block_width(columns)
     return pl.pallas_call(
-        functools.partial(fetch_kernel, columns, flip),
-        out_shape=pltpu.VMEM((columns, source.shape[0]), source.dtype),
+        fetch_kernel,
+        out_shape=pltpu.VMEM((columns, rows), source.dtype),
         in_specs=[ANY, ANY],
         out_specs=VMEM,
         scratch_shapes=[
-            pltpu.VMEM((columns // width, source.shape[0], width), source.dtype),
+            pltpu.VMEM((columns // width, rows, width), source.dtype),
             pltpu.SemaphoreType.DMA((columns // width,)),
         ],
         name="fetch",
         cost_estimate=pl.CostEstimate(
-            flops=0, bytes_accessed=2 * source.shape[0] * columns, transcendentals=0
+            flops=0, bytes_accessed=2 * source.size, transcendentals=0
         ),
         compiler_params=pltpu.CompilerParams(vmem_limit_bytes=40 * MIB),
     )(source, after)
@@ -280,7 +275,7 @@
         normed = (wide * gain_ref[:, pl.ds(begin, block)]).astype(jnp.bfloat16)
         product = lax.dot_general(
             normed,
-            weight_ref[i : i + block, :],
+            weight_ref[pl.ds(begin, block), :],
             (((1,), (0,)), ((), ())),
             preferred_element_type=jnp.float32,
         )
@@ -322,19 +317,21 @@
     columns = down_weight.shape[2]
     capacity = hidden.shape[1] // experts
     features = columns * tensors
-    spans = halves(groups)
+    stages = stages_of(groups)
 
     def swap(value, bits):
         return lax.ppermute(value, "expert", [(i, i ^ bits) for i in range(experts)])
 
-    results = down(hidden, down_weight, experts, spans)
+    results = down(hidden, down_weight, experts, stages)
     results, expert_ids, gate_weights = lax.optimization_barrier(
         (results, expert_ids, gate_weights)
     )
-    own, near, first, *rest = results
-    first = swap(first, 2)
+    own, near, *far = results
+    early = max(len(stages) - 1, 1)
+    far[:early] = [swap(rows, 2) for rows in far[:early]]
     near = swap(near, 1)
-    rest = [swap(rows, 2 + n % 2) for n, rows in enumerate(rest)]
+    far[0], *far[early:] = lax.optimization_barrier((far[0], *far[early:]))
+    far[early:] = [swap(rows, 2 + n) for n, rows in enumerate(far[early:])]
     chosen = [jnp.concatenate([expert_ids.T.astype(jnp.float32), gate_weights.T], axis=0)]
     while len(chosen) < groups:
         sent = jnp.concatenate(chosen, axis=0)
@@ -344,25 +341,25 @@
     summed = residual
     begin = 0
     after = ()
-    paired = columns % LANES == 0 and tensors == 2 and len(spans) == 2
-    for n, (low, count) in enumerate(spans):
-        height = count * capacity
-        if n:
-            far = rest[2 * n - 2 : 2 * n]
+    paired = columns % LANES == 0 and tensors == 2
+    for n, stage in enumerate(stages):
+        height = len(stage) * capacity
+        if n < early:
+            rows = [far[n], swap(far[n][height:], 1)]
         else:
-            far = [first, swap(first[height:], 1)]
+            rows = far[early:]
         parts = combine(
-            chosen[low : low + count],
-            [own, near, *far],
+            [chosen[d] for d in stage],
+            [own, near, *rows],
             [begin, begin, 0, 0],
-            low,
+            stage[0],
             capacity,
             after,
         )
         begin += height
         after = parts[:1]
-        moved = [swap(part, d * NODE_SIZE) if d else part for d, part in enumerate(parts, low)]
-        if low:
+        moved = [swap(part, d * NODE_SIZE) if d else part for d, part in zip(stage, parts)]
+        if n < early and len(stages) > 1:
             summed = add(summed, moved)
         else:
             for part in moved:
@@ -375,12 +372,12 @@
         energy = jnp.sum(wide * wide, axis=1)
         inverse = lax.rsqrt(energy / features + epsilon)
         return (stream, (added * inverse[:, None]).astype(jnp.bfloat16))
-    held = [fetch(weight, columns, flip, *after) for flip in range(2)]
+    held = fetch(weight, *after)
     stream, held = lax.optimization_barrier((stream, held))
     other = lax.ppermute(stream, "tensor", [(i, i ^ 1) for i in range(tensors)])
     gain = norm_gain.reshape(1, features)
-    carried = project(gain, held[0], stream)
-    (latents,) = project(gain, held[1], other, 1, carried, features)
+    carried = project(gain, held, stream)
+    (latents,) = project(gain, held, other, 1, carried, features)
     return (stream, latents)
 
 

time: 41.1 us -> 39.9 us (0.971)
  waiting for transfers between devices: 6.26 us -> 4.8 us
  Pallas kernels: 18.3 us -> 17.3 us
  local copies, waits for them, and re-layouts: 0.04 us -> 0.69 us
  starting transfers between devices: 15.6 us -> 16.1 us
    ppermute x10 -> x12, waiting for transfers between devices: 4.15 us -> 2.7 us  [swap(): lax.ppermute(value, 'expert', [(i, i ^ bits) for i in range(experts)])]
    pallas_call x2 -> x1, Pallas kernels: 7.69 us -> 6.45 us  [fetch(): pl.pallas_call(fetch_kernel, out_shape=pltpu.VMEM((columns, rows), source...]
    unnamed x10 -> x14, local copies, waits for them, and re-layouts: 0.03 us -> 0.68 us
    ppermute x10 -> x12, starting transfers between devices: 14 us -> 14.5 us  [swap(): lax.ppermute(value, 'expert', [(i, i ^ bits) for i in range(experts)])]
    pallas_call x2 -> x3, Pallas kernels: 0.93 us -> 1.21 us  [combine(): pl.pallas_call(functools.partial(combine_kernel, low, count, capacity, be...]
  transfers between devices with their start and end apart: 11 -> 13, of which waited for: 4 -> 4; matrix products, arithmetic and copies ran while one was open for 0% -> 0% of each run, Pallas kernels for 24% -> 22%
where the time goes in v4:
time: 39.9 us; the launch traced here: 39.7 us
  Pallas kernels  17.3 us (43%)
  starting transfers between devices  16.1 us (40%)
  waiting for transfers between devices  4.8 us (12%)
  between operations  0.81 us (2%)
  local copies, waits for them, and re-layouts  0.69 us (2%)
    ppermute x12, starting transfers between devices, swap(): lax.ppermute(value, 'expert', [(i, i ^ bits) for i in range(experts)])  14.5 us
    pallas_call x1, Pallas kernels, down(): pl.pallas_call(functools.partial(down_kernel, experts, outputs), out_shap...  6.65 us
    pallas_call x1, Pallas kernels, fetch(): pl.pallas_call(fetch_kernel, out_shape=pltpu.VMEM((columns, rows), source...  6.45 us
    pallas_call x2, Pallas kernels, project(): pl.pallas_call(functools.partial(project_kernel, flip, block, bool(carrie...  2.98 us
    ppermute x12, waiting for transfers between devices, swap(): lax.ppermute(value, 'expert', [(i, i ^ bits) for i in range(experts)])  2.7 us
    ppermute x1, waiting for transfers between devices, on_device(): other = lax.ppermute(stream, 'tensor', [(i, i ^ 1) for i in range(tensors)])  2.1 us
    ppermute x1, starting transfers between devices, on_device(): other = lax.ppermute(stream, 'tensor', [(i, i ^ 1) for i in range(tensors)])  1.59 us
    pallas_call x3, Pallas kernels, combine(): pl.pallas_call(functools.partial(combine_kernel, low, count, capacity, be...  1.21 us
  transfers between devices with their start and end apart: 13, of which 4 were waited for; matrix products, arithmetic and copies ran while one was open for 0% of the time, Pallas kernels for 22%

profile of v4, /device:TPU:0, one launch (start us, length us, event | category | flops | bytes accessed | tf_op | source)
XLA Modules:
  0.0 39.7 jit_solution(13099418999498581917)
XLA Ops:
  0.6 0.0 copy-start.5
  0.6 0.0 copy-start.6
  0.7 6.7 %down.1 = (bf16[32,3584]{1,0:T(8,128)(2,1)S(1)}, bf16[32,3584]{1,0:T(8,128)(2,1)S(1)}, bf16[16,3584]{1,0:T(8,128)(2,1)S(1)}, bf16[16,3584]{1,0:T(8,128)(2,1)S(1)...) custom-call(bf16[1,128,2048]{2,1,0:T(8,128)(2,1)} %hidden_hbm.1, bf16[1,2048,3584]{2,1,0:T(8,128)(2,1)} %weight_hbm.1), custom_call_target="tpu_custom_call" | custom-call | flops 1879048192 | bytes 14680064 | tf_op jit(solution)/shard_map/down/pallas_call | solution.py:115
  7.3 0.0 copy-done.6
  7.3 0.0 copy-done.5
  7.4 3.1 %collective-permute-start = (f32[16,16]{1,0:T(8,128)S(1)}, f32[16,16]{1,0:T(8,128)S(1)}, u32[]{:S(2)}, u32[]{:S(2)}) collective-permute-start(f32[16,16]{1,0:T(8,128)S(1)} %pad_maximum_fusion.1.refs_0_), channel_id=1, source_target_pairs={{0,8},{2,10},{4,12},{6,14},{8,0},{10,2},{12,4},{14,6},{16,24},{18,... | collective-permute-start | bytes 3080 | tf_op jit(solution)/shard_map/ppermute | solution.py:323
  10.4 1.5 %collective-permute-start.3 = (bf16[16,3584]{1,0:T(8,128)(2,1)S(1)}, bf16[16,3584]{1,0:T(8,128)(2,1)S(1)}, u32[]{:S(2)}, u32[]{:S(2)}) collective-permute-start(bf16[16,3584]{1,0:T(8,128)(2,1)S(1)} %get-tuple-element.35), channel_id=1, source_target_pairs={{0,4},{2,6},{4,0},{6,2},{8,12},{10,14},{12,8},{14,10},{16,20},{18,... | collective-permute-start | bytes 344072 | tf_op jit(solution)/shard_map/ppermute | solution.py:323
  11.9 0.5 %collective-permute-start.6 = (bf16[16,3584]{1,0:T(8,128)(2,1)S(1)}, bf16[16,3584]{1,0:T(8,128)(2,1)S(1)}, u32[]{:S(2)}, u32[]{:S(2)}) collective-permute-start(bf16[16,3584]{1,0:T(8,128)(2,1)S(1)} %get-tuple-element.39), channel_id=1, source_target_pairs={{0,4},{2,6},{4,0},{6,2},{8,12},{10,14},{12,8},{14,10},{16,20},{18,... | collective-permute-start | bytes 344072 | tf_op jit(solution)/shard_map/ppermute | solution.py:323
  12.5 0.0 collective-permute-start.2
  12.5 0.0 collective-permute-done.refs_1_
  12.5 2.7 %collective-permute-start.1 = (f32[32,16]{1,0:T(8,128)S(1)}, f32[32,16]{1,0:T(8,128)S(1)}, u32[]{:S(2)}, u32[]{:S(2)}) collective-permute-start(f32[32,16]{1,0:T(8,128)S(1)} %pad_maximum_fusion), channel_id=1, source_target_pairs={{0,16},{2,18},{4,20},{6,22},{8,24},{10,26},{12,28},{14,30},{16,0},... | collective-permute-start | bytes 6152 | tf_op jit(solution)/shard_map/ppermute | solution.py:323
  15.1 1.1 %collective-permute-done.3.refs_3_ = bf16[16,3584]{1,0:T(8,128)(2,1)S(1)} collective-permute-done((bf16[16,3584]{1,0:T(8,128)(2,1)S(1)}, bf16[16,3584]{1,0:T(8,128)(2,1)S(1)}, u32[]{:S(2)}, u32[]{:S(2)}) %collective-permute-start.3) | collective-permute-done | bytes 114720 | tf_op jit(solution)/shard_map/ppermute | solution.py:323
  16.3 0.0 collective-permute-start.4
  16.3 1.6 %collective-permute-start.9 = (bf16[16,3584]{1,0:T(8,128)(2,1)S(1)}, bf16[16,3584]{1,0:T(8,128)(2,1)S(1)}, u32[]{:S(2)}, u32[]{:S(2)}) collective-permute-start(bf16[16,3584]{1,0:T(8,128)(2,1)S(1)} %get-tuple-element.40), channel_id=1, source_target_pairs={{0,4},{2,6},{4,0},{6,2},{8,12},{10,14},{12,8},{14,10},{16,20},{18,... | collective-permute-start | bytes 344072 | tf_op jit(solution)/shard_map/ppermute | solution.py:323
  17.8 0.0 collective-permute-done.6.refs_3_
  17.8 0.3 collective-permute-start.10
  18.2 0.0 collective-permute-done.1
  18.2 1.0 %collective-permute-start.7 = (bf16[8,3584]{1,0:T(8,128)(2,1)S(1)}, bf16[8,3584]{1,0:T(8,128)(2,1)S(1)}, u32[]{:S(2)}, u32[]{:S(2)}) collective-permute-start(bf16[8,3584]{1,0:T(8,128)(2,1)S(1)} %slice.8), channel_id=1, source_target_pairs={{0,2},{2,0},{4,6},{6,4},{8,10},{10,8},{12,14},{14,12},{16,18},{18,... | collective-permute-start | bytes 172040 | tf_op jit(solution)/shard_map/ppermute | solution.py:323
  19.2 0.0 collective-permute-done.4.refs_4_
  19.2 0.0 collective-permute-done.2.refs_2_.refs_3_
  19.2 0.4 combine.3.refs_5_
  19.6 2.5 %collective-permute-start.5 = (bf16[16,3584]{1,0:T(8,128)(2,1)S(1)}, bf16[16,3584]{1,0:T(8,128)(2,1)S(1)}, u32[]{:S(2)}, u32[]{:S(2)}) collective-permute-start(bf16[16,3584]{1,0:T(8,128)(2,1)S(1)} %combine.3.refs_5_), channel_id=1, source_target_pairs={{0,24},{2,26},{4,28},{6,30},{8,16},{10,18},{12,20},{14,22},{16,8},... | collective-permute-start | bytes 344072 | tf_op jit(solution)/shard_map/ppermute | solution.py:323
  22.1 0.0 collective-permute-done.7.refs_4_
  22.1 0.4 combine.4.refs_6_
  22.5 0.6 %collective-permute-start.8 = (bf16[16,3584]{1,0:T(8,128)(2,1)S(1)}, bf16[16,3584]{1,0:T(8,128)(2,1)S(1)}, u32[]{:S(2)}, u32[]{:S(2)}) collective-permute-start(bf16[16,3584]{1,0:T(8,128)(2,1)S(1)} %combine.4.refs_6_), channel_id=1, source_target_pairs={{0,16},{2,18},{4,20},{6,22},{8,24},{10,26},{12,28},{14,30},{16,0},... | collective-permute-start | bytes 344072 | tf_op jit(solution)/shard_map/ppermute | solution.py:323
  23.1 0.0 collective-permute-done.9.refs_4_
  23.1 0.7 %collective-permute-done.10.refs_5_ = bf16[16,3584]{1,0:T(8,128)(2,1)S(1)} collective-permute-done((bf16[16,3584]{1,0:T(8,128)(2,1)S(1)}, bf16[16,3584]{1,0:T(8,128)(2,1)S(1)}, u32[]{:S(2)}, u32[]{:S(2)}) %collective-permute-start.10) | collective-permute-done | bytes 114720 | tf_op jit(solution)/shard_map/ppermute | solution.py:323
  23.8 0.5 %combine.5 = (bf16[16,3584]{1,0:T(8,128)(2,1)S(1)}, bf16[16,3584]{1,0:T(8,128)(2,1)S(1)}) custom-call(f32[16,16]{1,0:T(8,128)S(1)} %pad_maximum_fusion.1.refs_0_, f32[16,16]{1,0:T(8,128)S(1)} %collective-permute-done.refs_1_, bf16[32,3584]{1,0:T(8,128)(2,1)S(1)} %get-tuple-element.33.refs_1_.refs_2_, ...), custom_call_target="tpu_custom_call" | custom-call | flops 58720256 | bytes 458752 | tf_op jit(solution)/shard_map/combine/pallas_call | solution.py:191
  24.3 0.0 copy-start
  24.3 0.6 %copy-done = bf16[16,3584]{1,0:T(8,128)(2,1)} copy-done((bf16[16,3584]{1,0:T(8,128)(2,1)}, bf16[16,3584]{1,0:T(8,128)(2,1)S(1)}, u32[]{:S(2)}) %copy-start) | copy-done | bytes 114712
  25.0 0.7 %collective-permute-start.11 = (bf16[16,3584]{1,0:T(8,128)(2,1)S(1)}, bf16[16,3584]{1,0:T(8,128)(2,1)S(1)}, u32[]{:S(2)}, u32[]{:S(2)}) collective-permute-start(bf16[16,3584]{1,0:T(8,128)(2,1)S(1)} %get-tuple-element.43), channel_id=1, source_target_pairs={{0,8},{2,10},{4,12},{6,14},{8,0},{10,2},{12,4},{14,6},{16,24},{18,... | collective-permute-start | bytes 344072 | tf_op jit(solution)/shard_map/ppermute | solution.py:323
  25.6 0.0 copy-start.4
  25.6 0.0 copy-start.1
  25.6 0.0 copy-start.3
  25.6 6.4 %fetch.1.refs_1_ = bf16[7168,1056]{1,0:T(8,128)(2,1)S(1)} custom-call(bf16[1056,7168]{1,0:T(8,128)(2,1)} %bitcast.7, bf16[16,3584]{1,0:T(8,128)(2,1)} %copy-done), custom_call_target="tpu_custom_call" | custom-call | bytes 15138816 | tf_op jit(solution)/shard_map/fetch/pallas_call | solution.py:245
  32.1 0.0 collective-permute-done.5.refs_0_
  32.1 0.0 copy-done.4
  32.1 0.8 %collective-permute-done.8.refs_0_ = bf16[16,3584]{1,0:T(8,128)(2,1)S(1)} collective-permute-done((bf16[16,3584]{1,0:T(8,128)(2,1)S(1)}, bf16[16,3584]{1,0:T(8,128)(2,1)S(1)}, u32[]{:S(2)}, u32[]{:S(2)}) %collective-permute-start.8) | collective-permute-done | bytes 114720 | tf_op jit(solution)/shard_map/ppermute | solution.py:323
  33.0 0.0 collective-permute-done.11
  33.0 0.0 copy-done.1
  33.1 0.0 copy-start.2
  33.1 1.6 %collective-permute-start.12 = (bf16[16,3584]{1,0:T(8,128)(2,1)S(1)}, bf16[16,3584]{1,0:T(8,128)(2,1)S(1)}, u32[]{:S(2)}, u32[]{:S(2)}) collective-permute-start(bf16[16,3584]{1,0:T(8,128)(2,1)S(1)} %add_convert_fusion.refs_2_), channel_id=1, source_target_pairs={{0,1},{1,0},{2,3},{3,2},{4,5},{5,4},{6,7},{7,6},{8,9},{9,8},{10,11... | collective-permute-start | bytes 344072 | tf_op jit(solution)/shard_map/ppermute | solution.py:377
  34.7 0.0 copy-done.3
  34.7 1.2 %project.2 = (f32[16,1056]{1,0:T(8,128)S(1)}, f32[16,1]{1,0:T(8,128)S(1)}) custom-call(f32[1,7168]{1,0:T(1,128)S(1)} %bitcast.5, bf16[7168,1056]{1,0:T(8,128)(2,1)S(1)} %fetch.1.refs_1_, bf16[16,3584]{1,0:T(8,128)(2,1)S(1)} %add_convert_fusion.refs_2_), custom_call_target="tpu_custom_call" | custom-call | flops 3875536896 | tf_op jit(solution)/shard_map/project/pallas_call | solution.py:300
  35.8 2.1 %collective-permute-done.12.refs_2_ = bf16[16,3584]{1,0:T(8,128)(2,1)S(1)} collective-permute-done((bf16[16,3584]{1,0:T(8,128)(2,1)S(1)}, bf16[16,3584]{1,0:T(8,128)(2,1)S(1)}, u32[]{:S(2)}, u32[]{:S(2)}) %collective-permute-start.12) | collective-permute-done | bytes 114720 | tf_op jit(solution)/shard_map/ppermute | solution.py:377
  37.9 1.8 %project.3 = bf16[16,1056]{1,0:T(8,128)(2,1)} custom-call(f32[1,7168]{1,0:T(1,128)S(1)} %bitcast.6, bf16[7168,1056]{1,0:T(8,128)(2,1)S(1)} %fetch.1.refs_1_, bf16[16,3584]{1,0:T(8,128)(2,1)S(1)} %collective-permute-done.12.refs_2_, f32[16,1056]{1,0:T(8,128)S(1)} %get-tuple-element.46.refs_3_, f32[16,1]{1,0:T(8,128)S(1)} %get-tuple-element.47.refs_4_), custom_call_target="tpu_custom_call" | custom-call | flops 3875536896 | tf_op jit(solution)/shard_map/project/pallas_call | solution.py:300
  39.7 0.0 copy-done.2
  (9 shorter events, 0.1 us)
Async XLA Ops:
  0.6 6.7 %copy-start.5 = (f32[16,8]{0,1:T(8,128)S(1)}, f32[16,8]{0,1:T(8,128)}, u32[]{:S(2)}) copy-start(f32[16,8]{0,1:T(8,128)} %param.10) | copy-start | bytes 1540
  0.6 6.7 %copy-start.6 = (s32[16,8]{0,1:T(8,128)S(1)}, s32[16,8]{0,1:T(8,128)}, u32[]{:S(2)}) copy-start(s32[16,8]{0,1:T(8,128)} %param.9) | copy-start | bytes 1540
  7.4 5.1 %collective-permute-start = (f32[16,16]{1,0:T(8,128)S(1)}, f32[16,16]{1,0:T(8,128)S(1)}, u32[]{:S(2)}, u32[]{:S(2)}) collective-permute-start(f32[16,16]{1,0:T(8,128)S(1)} %pad_maximum_fusion.1.refs_0_), channel_id=1, source_target_pairs={{0,8},{2,10},{4,12},{6,14},{8,0},{10,2},{12,4},{14,6},{16,24},{18,... | collective-permute-start | bytes 3080 | tf_op jit(solution)/shard_map/ppermute | solution.py:323
  10.4 5.8 %collective-permute-start.3 = (bf16[16,3584]{1,0:T(8,128)(2,1)S(1)}, bf16[16,3584]{1,0:T(8,128)(2,1)S(1)}, u32[]{:S(2)}, u32[]{:S(2)}) collective-permute-start(bf16[16,3584]{1,0:T(8,128)(2,1)S(1)} %get-tuple-element.35), channel_id=1, source_target_pairs={{0,4},{2,6},{4,0},{6,2},{8,12},{10,14},{12,8},{14,10},{16,20},{18,... | collective-permute-start | bytes 344072 | tf_op jit(solution)/shard_map/ppermute | solution.py:323
  11.9 5.9 %collective-permute-start.6 = (bf16[16,3584]{1,0:T(8,128)(2,1)S(1)}, bf16[16,3584]{1,0:T(8,128)(2,1)S(1)}, u32[]{:S(2)}, u32[]{:S(2)}) collective-permute-start(bf16[16,3584]{1,0:T(8,128)(2,1)S(1)} %get-tuple-element.39), channel_id=1, source_target_pairs={{0,4},{2,6},{4,0},{6,2},{8,12},{10,14},{12,8},{14,10},{16,20},{18,... | collective-permute-start | bytes 344072 | tf_op jit(solution)/shard_map/ppermute | solution.py:323
  12.5 6.7 %collective-permute-start.2 = (bf16[32,3584]{1,0:T(8,128)(2,1)S(1)}, bf16[32,3584]{1,0:T(8,128)(2,1)S(1)}, u32[]{:S(2)}, u32[]{:S(2)}) collective-permute-start(bf16[32,3584]{1,0:T(8,128)(2,1)S(1)} %get-tuple-element.34), channel_id=1, source_target_pairs={{0,2},{2,0},{4,6},{6,4},{8,10},{10,8},{12,14},{14,12},{16,18},{18,... | collective-permute-start | bytes 688136 | tf_op jit(solution)/shard_map/ppermute | solution.py:323
  12.5 5.7 %collective-permute-start.1 = (f32[32,16]{1,0:T(8,128)S(1)}, f32[32,16]{1,0:T(8,128)S(1)}, u32[]{:S(2)}, u32[]{:S(2)}) collective-permute-start(f32[32,16]{1,0:T(8,128)S(1)} %pad_maximum_fusion), channel_id=1, source_target_pairs={{0,16},{2,18},{4,20},{6,22},{8,24},{10,26},{12,28},{14,30},{16,0},... | collective-permute-start | bytes 6152 | tf_op jit(solution)/shard_map/ppermute | solution.py:323
  16.3 2.9 %collective-permute-start.4 = (bf16[8,3584]{1,0:T(8,128)(2,1)S(1)}, bf16[8,3584]{1,0:T(8,128)(2,1)S(1)}, u32[]{:S(2)}, u32[]{:S(2)}) collective-permute-start(bf16[8,3584]{1,0:T(8,128)(2,1)S(1)} %slice.6), channel_id=1, source_target_pairs={{0,2},{2,0},{4,6},{6,4},{8,10},{10,8},{12,14},{14,12},{16,18},{18,... | collective-permute-start | bytes 172040 | tf_op jit(solution)/shard_map/ppermute | solution.py:323
  16.3 6.8 %collective-permute-start.9 = (bf16[16,3584]{1,0:T(8,128)(2,1)S(1)}, bf16[16,3584]{1,0:T(8,128)(2,1)S(1)}, u32[]{:S(2)}, u32[]{:S(2)}) collective-permute-start(bf16[16,3584]{1,0:T(8,128)(2,1)S(1)} %get-tuple-element.40), channel_id=1, source_target_pairs={{0,4},{2,6},{4,0},{6,2},{8,12},{10,14},{12,8},{14,10},{16,20},{18,... | collective-permute-start | bytes 344072 | tf_op jit(solution)/shard_map/ppermute | solution.py:323
  17.8 6.0 %collective-permute-start.10 = (bf16[16,3584]{1,0:T(8,128)(2,1)S(1)}, bf16[16,3584]{1,0:T(8,128)(2,1)S(1)}, u32[]{:S(2)}, u32[]{:S(2)}) collective-permute-start(bf16[16,3584]{1,0:T(8,128)(2,1)S(1)} %get-tuple-element.41), channel_id=1, source_target_pairs={{0,6},{2,4},{4,2},{6,0},{8,14},{10,12},{12,10},{14,8},{16,22},{18,... | collective-permute-start | bytes 344072 | tf_op jit(solution)/shard_map/ppermute | solution.py:323
  18.2 4.0 %collective-permute-start.7 = (bf16[8,3584]{1,0:T(8,128)(2,1)S(1)}, bf16[8,3584]{1,0:T(8,128)(2,1)S(1)}, u32[]{:S(2)}, u32[]{:S(2)}) collective-permute-start(bf16[8,3584]{1,0:T(8,128)(2,1)S(1)} %slice.8), channel_id=1, source_target_pairs={{0,2},{2,0},{4,6},{6,4},{8,10},{10,8},{12,14},{14,12},{16,18},{18,... | collective-permute-start | bytes 172040 | tf_op jit(solution)/shard_map/ppermute | solution.py:323
  19.6 12.5 %collective-permute-start.5 = (bf16[16,3584]{1,0:T(8,128)(2,1)S(1)}, bf16[16,3584]{1,0:T(8,128)(2,1)S(1)}, u32[]{:S(2)}, u32[]{:S(2)}) collective-permute-start(bf16[16,3584]{1,0:T(8,128)(2,1)S(1)} %combine.3.refs_5_), channel_id=1, source_target_pairs={{0,24},{2,26},{4,28},{6,30},{8,16},{10,18},{12,20},{14,22},{16,8},... | collective-permute-start | bytes 344072 | tf_op jit(solution)/shard_map/ppermute | solution.py:323
  22.5 10.4 %collective-permute-start.8 = (bf16[16,3584]{1,0:T(8,128)(2,1)S(1)}, bf16[16,3584]{1,0:T(8,128)(2,1)S(1)}, u32[]{:S(2)}, u32[]{:S(2)}) collective-permute-start(bf16[16,3584]{1,0:T(8,128)(2,1)S(1)} %combine.4.refs_6_), channel_id=1, source_target_pairs={{0,16},{2,18},{4,20},{6,22},{8,24},{10,26},{12,28},{14,30},{16,0},... | collective-permute-start | bytes 344072 | tf_op jit(solution)/shard_map/ppermute | solution.py:323
  24.3 0.7 %copy-start = (bf16[16,3584]{1,0:T(8,128)(2,1)}, bf16[16,3584]{1,0:T(8,128)(2,1)S(1)}, u32[]{:S(2)}) copy-start(bf16[16,3584]{1,0:T(8,128)(2,1)S(1)} %get-tuple-element.42.after_ref) | copy-start | bytes 344068
  25.0 8.0 %collective-permute-start.11 = (bf16[16,3584]{1,0:T(8,128)(2,1)S(1)}, bf16[16,3584]{1,0:T(8,128)(2,1)S(1)}, u32[]{:S(2)}, u32[]{:S(2)}) collective-permute-start(bf16[16,3584]{1,0:T(8,128)(2,1)S(1)} %get-tuple-element.43), channel_id=1, source_target_pairs={{0,8},{2,10},{4,12},{6,14},{8,0},{10,2},{12,4},{14,6},{16,24},{18,... | collective-permute-start | bytes 344072 | tf_op jit(solution)/shard_map/ppermute | solution.py:323
  25.6 6.5 %copy-start.4 = (bf16[16,3584]{1,0:T(8,128)(2,1)S(1)}, bf16[16,3584]{1,0:T(8,128)(2,1)}, u32[]{:S(2)}) copy-start(bf16[16,3584]{1,0:T(8,128)(2,1)} %base_ref.1) | copy-start | bytes 344068
  25.6 7.4 %copy-start.1 = (bf16[16,3584]{1,0:T(8,128)(2,1)S(1)}, bf16[16,3584]{1,0:T(8,128)(2,1)}, u32[]{:S(2)}) copy-start(bf16[16,3584]{1,0:T(8,128)(2,1)} %copy-done) | copy-start | bytes 344068
  25.6 9.0 %copy-start.3 = (f32[7168]{0:T(1024)S(1)}, f32[7168]{0:T(1024)}, u32[]{:S(2)}) copy-start(f32[7168]{0:T(1024)} %param.12) | copy-start | bytes 86020
  33.1 6.7 %copy-start.2 = (bf16[16,3584]{1,0:T(8,128)(2,1)}, bf16[16,3584]{1,0:T(8,128)(2,1)S(1)}, u32[]{:S(2)}) copy-start(bf16[16,3584]{1,0:T(8,128)(2,1)S(1)} %add_convert_fusion.refs_2_) | copy-start | bytes 344068
  33.1 4.9 %collective-permute-start.12 = (bf16[16,3584]{1,0:T(8,128)(2,1)S(1)}, bf16[16,3584]{1,0:T(8,128)(2,1)S(1)}, u32[]{:S(2)}, u32[]{:S(2)}) collective-permute-start(bf16[16,3584]{1,0:T(8,128)(2,1)S(1)} %add_convert_fusion.refs_2_), channel_id=1, source_target_pairs={{0,1},{1,0},{2,3},{3,2},{4,5},{5,4},{6,7},{7,6},{8,9},{9,8},{10,11... | collective-permute-start | bytes 344072 | tf_op jit(solution)/shard_map/ppermute | solution.py:377

commit v5 on v4

--- a/solution.py
+++ b/solution.py
@@ -11,7 +11,7 @@
 LANES = 128
 MIB = 1 << 20
 AHEAD = 3
-DEPTH_STEPS = 8
+DEPTH_PARTS = (4, 4, 4, 2, 2)
 ADD_COST = 64 * MIB
 
 
@@ -58,11 +58,15 @@
     out_refs = refs[: len(outputs)]
     hidden, wide, ordered, weights, total, hidden_sem, weight_sems = refs[len(outputs) :]
     index = lax.axis_index("expert")
-    steps, depth = weights.shape[:2]
+    unit = weights.shape[0] // sum(DEPTH_PARTS)
+    bounds = [sum(DEPTH_PARTS[:n]) * unit for n in range(len(DEPTH_PARTS) + 1)]
+    steps = len(DEPTH_PARTS)
     first_copy = pltpu.make_async_copy(hidden_hbm.at[0], hidden, hidden_sem)
     copies = [
         pltpu.make_async_copy(
-            weight_hbm.at[0, pl.ds(i * depth, depth)], weights.at[i], weight_sems.at[i]
+            weight_hbm.at[0, pl.ds(bounds[i], bounds[i + 1] - bounds[i])],
+            weights.at[pl.ds(bounds[i], bounds[i + 1] - bounds[i])],
+            weight_sems.at[i],
         )
         for i in range(steps)
     ]
@@ -90,8 +94,8 @@
             copies[i + AHEAD].start()
         for first in range(0, columns, block):
             product = jnp.dot(
-                ordered[:, i * depth : (i + 1) * depth],
-                weights[i, :, first : first + block],
+                ordered[:, bounds[i] : bounds[i + 1]],
+                weights[bounds[i] : bounds[i + 1], first : first + block],
                 preferred_element_type=jnp.float32,
             )
             if i:
@@ -121,10 +125,10 @@
             pltpu.VMEM((rows, depth), jnp.bfloat16),
             pltpu.VMEM((rows, depth), jnp.float32),
             pltpu.VMEM((rows, depth), jnp.bfloat16),
-            pltpu.VMEM((DEPTH_STEPS, depth // DEPTH_STEPS, columns), jnp.bfloat16),
+            pltpu.VMEM((depth, columns), jnp.bfloat16),
             pltpu.VMEM((rows, columns), jnp.float32),
             pltpu.SemaphoreType.DMA(()),
-            pltpu.SemaphoreType.DMA((DEPTH_STEPS,)),
+            pltpu.SemaphoreType.DMA((len(DEPTH_PARTS),)),
         ],
         name="down",
         cost_estimate=pl.CostEstimate(
@@ -255,7 +259,7 @@
         cost_estimate=pl.CostEstimate(
             flops=0, bytes_accessed=2 * source.size, transcendentals=0
         ),
-        compiler_params=pltpu.CompilerParams(vmem_limit_bytes=40 * MIB),
+        compiler_params=pltpu.CompilerParams(vmem_limit_bytes=32 * MIB),
     )(source, after)
 
 

time: 39.9 us -> 39.3 us (0.985)
  local copies, waits for them, and re-layouts: 0.69 us -> 0.03 us
  Pallas kernels: 17.3 us -> 16.7 us
  waiting for transfers between devices: 4.8 us -> 5.4 us
    unnamed x14 -> x10, local copies, waits for them, and re-layouts: 0.68 us -> 0.02 us
    pallas_call x1, Pallas kernels: 6.65 us -> 6.05 us  [down(): pl.pallas_call(functools.partial(down_kernel, experts, outputs), out_shap...]
    ppermute x12, waiting for transfers between devices: 2.7 us -> 3.3 us  [swap(): lax.ppermute(value, 'expert', [(i, i ^ bits) for i in range(experts)])]
  transfers between devices with their start and end apart: 13 -> 13, of which waited for: 4 -> 4; matrix products, arithmetic and copies ran while one was open for 0% -> 0% of each run, Pallas kernels for 22% -> 23%
where the time goes in v5:
time: 39.3 us; the launch traced here: 39.1 us
  Pallas kernels  16.7 us (42%)
  starting transfers between devices  16.1 us (41%)
  waiting for transfers between devices  5.4 us (14%)
  between operations  0.79 us (2%)
    ppermute x12, starting transfers between devices, swap(): lax.ppermute(value, 'expert', [(i, i ^ bits) for i in range(experts)])  14.5 us
    pallas_call x1, Pallas kernels, fetch(): pl.pallas_call(fetch_kernel, out_shape=pltpu.VMEM((columns, rows), source...  6.44 us
    pallas_call x1, Pallas kernels, down(): pl.pallas_call(functools.partial(down_kernel, experts, outputs), out_shap...  6.05 us
    ppermute x12, waiting for transfers between devices, swap(): lax.ppermute(value, 'expert', [(i, i ^ bits) for i in range(experts)])  3.3 us
    pallas_call x2, Pallas kernels, project(): pl.pallas_call(functools.partial(project_kernel, flip, block, bool(carrie...  2.98 us
    ppermute x1, waiting for transfers between devices, on_device(): other = lax.ppermute(stream, 'tensor', [(i, i ^ 1) for i in range(tensors)])  2.1 us
    ppermute x1, starting transfers between devices, on_device(): other = lax.ppermute(stream, 'tensor', [(i, i ^ 1) for i in range(tensors)])  1.58 us
    pallas_call x3, Pallas kernels, combine(): pl.pallas_call(functools.partial(combine_kernel, low, count, capacity, be...  1.21 us
  transfers between devices with their start and end apart: 13, of which 4 were waited for; matrix products, arithmetic and copies ran while one was open for 0% of the time, Pallas kernels for 23%

profile of v5, /device:TPU:0, one launch (start us, length us, event | category | flops | bytes accessed | tf_op | source)
XLA Modules:
  0.0 39.1 jit_solution(2448289259576888602)
XLA Ops:
  0.6 0.0 copy-start.3
  0.6 0.0 copy-start.4
  0.7 6.1 %down.1 = (bf16[32,3584]{1,0:T(8,128)(2,1)S(1)}, bf16[32,3584]{1,0:T(8,128)(2,1)S(1)}, bf16[16,3584]{1,0:T(8,128)(2,1)S(1)}, bf16[16,3584]{1,0:T(8,128)(2,1)S(1)...) custom-call(bf16[1,128,2048]{2,1,0:T(8,128)(2,1)} %hidden_hbm.1, bf16[1,2048,3584]{2,1,0:T(8,128)(2,1)} %weight_hbm.1), custom_call_target="tpu_custom_call" | custom-call | flops 1879048192 | bytes 14680064 | tf_op jit(solution)/shard_map/down/pallas_call | solution.py:119
  6.7 0.0 copy-done.4
  6.7 0.0 copy-done.3
  6.8 3.1 %collective-permute-start = (f32[16,16]{1,0:T(8,128)S(1)}, f32[16,16]{1,0:T(8,128)S(1)}, u32[]{:S(2)}, u32[]{:S(2)}) collective-permute-start(f32[16,16]{1,0:T(8,128)S(1)} %pad_maximum_fusion.1.refs_0_), channel_id=1, source_target_pairs={{0,8},{2,10},{4,12},{6,14},{8,0},{10,2},{12,4},{14,6},{16,24},{18,... | collective-permute-start | bytes 3080 | tf_op jit(solution)/shard_map/ppermute | solution.py:327
  9.8 1.5 %collective-permute-start.3 = (bf16[16,3584]{1,0:T(8,128)(2,1)S(1)}, bf16[16,3584]{1,0:T(8,128)(2,1)S(1)}, u32[]{:S(2)}, u32[]{:S(2)}) collective-permute-start(bf16[16,3584]{1,0:T(8,128)(2,1)S(1)} %get-tuple-element.35), channel_id=1, source_target_pairs={{0,4},{2,6},{4,0},{6,2},{8,12},{10,14},{12,8},{14,10},{16,20},{18,... | collective-permute-start | bytes 344072 | tf_op jit(solution)/shard_map/ppermute | solution.py:327
  11.3 0.5 %collective-permute-start.6 = (bf16[16,3584]{1,0:T(8,128)(2,1)S(1)}, bf16[16,3584]{1,0:T(8,128)(2,1)S(1)}, u32[]{:S(2)}, u32[]{:S(2)}) collective-permute-start(bf16[16,3584]{1,0:T(8,128)(2,1)S(1)} %get-tuple-element.39), channel_id=1, source_target_pairs={{0,4},{2,6},{4,0},{6,2},{8,12},{10,14},{12,8},{14,10},{16,20},{18,... | collective-permute-start | bytes 344072 | tf_op jit(solution)/shard_map/ppermute | solution.py:327
  11.9 0.0 collective-permute-start.2
  11.9 0.0 collective-permute-done.refs_1_
  11.9 2.7 %collective-permute-start.1 = (f32[32,16]{1,0:T(8,128)S(1)}, f32[32,16]{1,0:T(8,128)S(1)}, u32[]{:S(2)}, u32[]{:S(2)}) collective-permute-start(f32[32,16]{1,0:T(8,128)S(1)} %pad_maximum_fusion), channel_id=1, source_target_pairs={{0,16},{2,18},{4,20},{6,22},{8,24},{10,26},{12,28},{14,30},{16,0},... | collective-permute-start | bytes 6152 | tf_op jit(solution)/shard_map/ppermute | solution.py:327
  14.5 1.1 %collective-permute-done.3.refs_3_ = bf16[16,3584]{1,0:T(8,128)(2,1)S(1)} collective-permute-done((bf16[16,3584]{1,0:T(8,128)(2,1)S(1)}, bf16[16,3584]{1,0:T(8,128)(2,1)S(1)}, u32[]{:S(2)}, u32[]{:S(2)}) %collective-permute-start.3) | collective-permute-done | bytes 114720 | tf_op jit(solution)/shard_map/ppermute | solution.py:327
  15.7 0.0 collective-permute-start.4
  15.7 1.6 %collective-permute-start.9 = (bf16[16,3584]{1,0:T(8,128)(2,1)S(1)}, bf16[16,3584]{1,0:T(8,128)(2,1)S(1)}, u32[]{:S(2)}, u32[]{:S(2)}) collective-permute-start(bf16[16,3584]{1,0:T(8,128)(2,1)S(1)} %get-tuple-element.40), channel_id=1, source_target_pairs={{0,4},{2,6},{4,0},{6,2},{8,12},{10,14},{12,8},{14,10},{16,20},{18,... | collective-permute-start | bytes 344072 | tf_op jit(solution)/shard_map/ppermute | solution.py:327
  17.2 0.0 collective-permute-done.6.refs_3_
  17.2 0.3 collective-permute-start.10
  17.6 0.0 collective-permute-done.1
  17.6 1.0 %collective-permute-start.7 = (bf16[8,3584]{1,0:T(8,128)(2,1)S(1)}, bf16[8,3584]{1,0:T(8,128)(2,1)S(1)}, u32[]{:S(2)}, u32[]{:S(2)}) collective-permute-start(bf16[8,3584]{1,0:T(8,128)(2,1)S(1)} %slice.8), channel_id=1, source_target_pairs={{0,2},{2,0},{4,6},{6,4},{8,10},{10,8},{12,14},{14,12},{16,18},{18,... | collective-permute-start | bytes 172040 | tf_op jit(solution)/shard_map/ppermute | solution.py:327
  18.6 0.0 collective-permute-done.4.refs_4_
  18.6 0.0 collective-permute-done.2.refs_2_.refs_3_
  18.6 0.4 combine.3.refs_5_
  19.0 2.5 %collective-permute-start.5 = (bf16[16,3584]{1,0:T(8,128)(2,1)S(1)}, bf16[16,3584]{1,0:T(8,128)(2,1)S(1)}, u32[]{:S(2)}, u32[]{:S(2)}) collective-permute-start(bf16[16,3584]{1,0:T(8,128)(2,1)S(1)} %combine.3.refs_5_), channel_id=1, source_target_pairs={{0,24},{2,26},{4,28},{6,30},{8,16},{10,18},{12,20},{14,22},{16,8},... | collective-permute-start | bytes 344072 | tf_op jit(solution)/shard_map/ppermute | solution.py:327
  21.5 0.0 collective-permute-done.7.refs_4_
  21.5 0.4 combine.4.refs_6_
  21.9 0.6 %collective-permute-start.8 = (bf16[16,3584]{1,0:T(8,128)(2,1)S(1)}, bf16[16,3584]{1,0:T(8,128)(2,1)S(1)}, u32[]{:S(2)}, u32[]{:S(2)}) collective-permute-start(bf16[16,3584]{1,0:T(8,128)(2,1)S(1)} %combine.4.refs_6_), channel_id=1, source_target_pairs={{0,16},{2,18},{4,20},{6,22},{8,24},{10,26},{12,28},{14,30},{16,0},... | collective-permute-start | bytes 344072 | tf_op jit(solution)/shard_map/ppermute | solution.py:327
  22.5 0.0 collective-permute-done.9.refs_4_
  22.5 0.7 %collective-permute-done.10.refs_5_ = bf16[16,3584]{1,0:T(8,128)(2,1)S(1)} collective-permute-done((bf16[16,3584]{1,0:T(8,128)(2,1)S(1)}, bf16[16,3584]{1,0:T(8,128)(2,1)S(1)}, u32[]{:S(2)}, u32[]{:S(2)}) %collective-permute-start.10) | collective-permute-done | bytes 114720 | tf_op jit(solution)/shard_map/ppermute | solution.py:327
  23.2 0.5 %combine.5 = (bf16[16,3584]{1,0:T(8,128)(2,1)S(1)}, bf16[16,3584]{1,0:T(8,128)(2,1)S(1)}) custom-call(f32[16,16]{1,0:T(8,128)S(1)} %pad_maximum_fusion.1.refs_0_, f32[16,16]{1,0:T(8,128)S(1)} %collective-permute-done.refs_1_, bf16[32,3584]{1,0:T(8,128)(2,1)S(1)} %get-tuple-element.33.refs_1_.refs_2_, ...), custom_call_target="tpu_custom_call" | custom-call | flops 58720256 | bytes 458752 | tf_op jit(solution)/shard_map/combine/pallas_call | solution.py:195
  23.7 0.7 %collective-permute-start.11 = (bf16[16,3584]{1,0:T(8,128)(2,1)S(1)}, bf16[16,3584]{1,0:T(8,128)(2,1)S(1)}, u32[]{:S(2)}, u32[]{:S(2)}) collective-permute-start(bf16[16,3584]{1,0:T(8,128)(2,1)S(1)} %get-tuple-element.43), channel_id=1, source_target_pairs={{0,8},{2,10},{4,12},{6,14},{8,0},{10,2},{12,4},{14,6},{16,24},{18,... | collective-permute-start | bytes 344072 | tf_op jit(solution)/shard_map/ppermute | solution.py:327
  24.4 0.0 copy-start.2
  24.4 0.0 copy-start.1
  24.4 6.4 %fetch.1.refs_1_ = bf16[7168,1056]{1,0:T(8,128)(2,1)S(1)} custom-call(bf16[1056,7168]{1,0:T(8,128)(2,1)} %bitcast.7, bf16[16,3584]{1,0:T(8,128)(2,1)S(1)} %get-tuple-element.42.after_ref), custom_call_target="tpu_custom_call" | custom-call | bytes 15138816 | tf_op jit(solution)/shard_map/fetch/pallas_call | solution.py:249
  30.9 0.0 collective-permute-done.5.refs_0_
  30.9 0.0 copy-done.2
  30.9 1.4 %collective-permute-done.8.refs_0_ = bf16[16,3584]{1,0:T(8,128)(2,1)S(1)} collective-permute-done((bf16[16,3584]{1,0:T(8,128)(2,1)S(1)}, bf16[16,3584]{1,0:T(8,128)(2,1)S(1)}, u32[]{:S(2)}, u32[]{:S(2)}) %collective-permute-start.8) | collective-permute-done | bytes 114720 | tf_op jit(solution)/shard_map/ppermute | solution.py:327
  32.4 0.0 collective-permute-done.11
  32.4 0.0 copy-start
  32.5 1.6 %collective-permute-start.12 = (bf16[16,3584]{1,0:T(8,128)(2,1)S(1)}, bf16[16,3584]{1,0:T(8,128)(2,1)S(1)}, u32[]{:S(2)}, u32[]{:S(2)}) collective-permute-start(bf16[16,3584]{1,0:T(8,128)(2,1)S(1)} %add_convert_fusion.refs_2_), channel_id=1, source_target_pairs={{0,1},{1,0},{2,3},{3,2},{4,5},{5,4},{6,7},{7,6},{8,9},{9,8},{10,11... | collective-permute-start | bytes 344072 | tf_op jit(solution)/shard_map/ppermute | solution.py:381
  34.0 0.0 copy-done.1
  34.0 1.2 %project.2 = (f32[16,1056]{1,0:T(8,128)S(1)}, f32[16,1]{1,0:T(8,128)S(1)}) custom-call(f32[1,7168]{1,0:T(1,128)S(1)} %bitcast.5, bf16[7168,1056]{1,0:T(8,128)(2,1)S(1)} %fetch.1.refs_1_, bf16[16,3584]{1,0:T(8,128)(2,1)S(1)} %add_convert_fusion.refs_2_), custom_call_target="tpu_custom_call" | custom-call | flops 3875536896 | tf_op jit(solution)/shard_map/project/pallas_call | solution.py:304
  35.2 2.1 %collective-permute-done.12.refs_2_ = bf16[16,3584]{1,0:T(8,128)(2,1)S(1)} collective-permute-done((bf16[16,3584]{1,0:T(8,128)(2,1)S(1)}, bf16[16,3584]{1,0:T(8,128)(2,1)S(1)}, u32[]{:S(2)}, u32[]{:S(2)}) %collective-permute-start.12) | collective-permute-done | bytes 114720 | tf_op jit(solution)/shard_map/ppermute | solution.py:381
  37.3 1.8 %project.3 = bf16[16,1056]{1,0:T(8,128)(2,1)} custom-call(f32[1,7168]{1,0:T(1,128)S(1)} %bitcast.6, bf16[7168,1056]{1,0:T(8,128)(2,1)S(1)} %fetch.1.refs_1_, bf16[16,3584]{1,0:T(8,128)(2,1)S(1)} %collective-permute-done.12.refs_2_, f32[16,1056]{1,0:T(8,128)S(1)} %get-tuple-element.46.refs_3_, f32[16,1]{1,0:T(8,128)S(1)} %get-tuple-element.47.refs_4_), custom_call_target="tpu_custom_call" | custom-call | flops 3875536896 | tf_op jit(solution)/shard_map/project/pallas_call | solution.py:304
  39.1 0.0 copy-done
  (9 shorter events, 0.1 us)
Async XLA Ops:
  0.6 6.1 %copy-start.3 = (f32[16,8]{0,1:T(8,128)S(1)}, f32[16,8]{0,1:T(8,128)}, u32[]{:S(2)}) copy-start(f32[16,8]{0,1:T(8,128)} %param.10) | copy-start | bytes 1540
  0.6 6.1 %copy-start.4 = (s32[16,8]{0,1:T(8,128)S(1)}, s32[16,8]{0,1:T(8,128)}, u32[]{:S(2)}) copy-start(s32[16,8]{0,1:T(8,128)} %param.9) | copy-start | bytes 1540
  6.8 5.1 %collective-permute-start = (f32[16,16]{1,0:T(8,128)S(1)}, f32[16,16]{1,0:T(8,128)S(1)}, u32[]{:S(2)}, u32[]{:S(2)}) collective-permute-start(f32[16,16]{1,0:T(8,128)S(1)} %pad_maximum_fusion.1.refs_0_), channel_id=1, source_target_pairs={{0,8},{2,10},{4,12},{6,14},{8,0},{10,2},{12,4},{14,6},{16,24},{18,... | collective-permute-start | bytes 3080 | tf_op jit(solution)/shard_map/ppermute | solution.py:327
  9.8 5.8 %collective-permute-start.3 = (bf16[16,3584]{1,0:T(8,128)(2,1)S(1)}, bf16[16,3584]{1,0:T(8,128)(2,1)S(1)}, u32[]{:S(2)}, u32[]{:S(2)}) collective-permute-start(bf16[16,3584]{1,0:T(8,128)(2,1)S(1)} %get-tuple-element.35), channel_id=1, source_target_pairs={{0,4},{2,6},{4,0},{6,2},{8,12},{10,14},{12,8},{14,10},{16,20},{18,... | collective-permute-start | bytes 344072 | tf_op jit(solution)/shard_map/ppermute | solution.py:327
  11.3 5.9 %collective-permute-start.6 = (bf16[16,3584]{1,0:T(8,128)(2,1)S(1)}, bf16[16,3584]{1,0:T(8,128)(2,1)S(1)}, u32[]{:S(2)}, u32[]{:S(2)}) collective-permute-start(bf16[16,3584]{1,0:T(8,128)(2,1)S(1)} %get-tuple-element.39), channel_id=1, source_target_pairs={{0,4},{2,6},{4,0},{6,2},{8,12},{10,14},{12,8},{14,10},{16,20},{18,... | collective-permute-start | bytes 344072 | tf_op jit(solution)/shard_map/ppermute | solution.py:327
  11.9 6.7 %collective-permute-start.2 = (bf16[32,3584]{1,0:T(8,128)(2,1)S(1)}, bf16[32,3584]{1,0:T(8,128)(2,1)S(1)}, u32[]{:S(2)}, u32[]{:S(2)}) collective-permute-start(bf16[32,3584]{1,0:T(8,128)(2,1)S(1)} %get-tuple-element.34), channel_id=1, source_target_pairs={{0,2},{2,0},{4,6},{6,4},{8,10},{10,8},{12,14},{14,12},{16,18},{18,... | collective-permute-start | bytes 688136 | tf_op jit(solution)/shard_map/ppermute | solution.py:327
  11.9 5.7 %collective-permute-start.1 = (f32[32,16]{1,0:T(8,128)S(1)}, f32[32,16]{1,0:T(8,128)S(1)}, u32[]{:S(2)}, u32[]{:S(2)}) collective-permute-start(f32[32,16]{1,0:T(8,128)S(1)} %pad_maximum_fusion), channel_id=1, source_target_pairs={{0,16},{2,18},{4,20},{6,22},{8,24},{10,26},{12,28},{14,30},{16,0},... | collective-permute-start | bytes 6152 | tf_op jit(solution)/shard_map/ppermute | solution.py:327
  15.7 2.9 %collective-permute-start.4 = (bf16[8,3584]{1,0:T(8,128)(2,1)S(1)}, bf16[8,3584]{1,0:T(8,128)(2,1)S(1)}, u32[]{:S(2)}, u32[]{:S(2)}) collective-permute-start(bf16[8,3584]{1,0:T(8,128)(2,1)S(1)} %slice.6), channel_id=1, source_target_pairs={{0,2},{2,0},{4,6},{6,4},{8,10},{10,8},{12,14},{14,12},{16,18},{18,... | collective-permute-start | bytes 172040 | tf_op jit(solution)/shard_map/ppermute | solution.py:327
  15.7 6.8 %collective-permute-start.9 = (bf16[16,3584]{1,0:T(8,128)(2,1)S(1)}, bf16[16,3584]{1,0:T(8,128)(2,1)S(1)}, u32[]{:S(2)}, u32[]{:S(2)}) collective-permute-start(bf16[16,3584]{1,0:T(8,128)(2,1)S(1)} %get-tuple-element.40), channel_id=1, source_target_pairs={{0,4},{2,6},{4,0},{6,2},{8,12},{10,14},{12,8},{14,10},{16,20},{18,... | collective-permute-start | bytes 344072 | tf_op jit(solution)/shard_map/ppermute | solution.py:327
  17.2 6.0 %collective-permute-start.10 = (bf16[16,3584]{1,0:T(8,128)(2,1)S(1)}, bf16[16,3584]{1,0:T(8,128)(2,1)S(1)}, u32[]{:S(2)}, u32[]{:S(2)}) collective-permute-start(bf16[16,3584]{1,0:T(8,128)(2,1)S(1)} %get-tuple-element.41), channel_id=1, source_target_pairs={{0,6},{2,4},{4,2},{6,0},{8,14},{10,12},{12,10},{14,8},{16,22},{18,... | collective-permute-start | bytes 344072 | tf_op jit(solution)/shard_map/ppermute | solution.py:327
  17.6 4.0 %collective-permute-start.7 = (bf16[8,3584]{1,0:T(8,128)(2,1)S(1)}, bf16[8,3584]{1,0:T(8,128)(2,1)S(1)}, u32[]{:S(2)}, u32[]{:S(2)}) collective-permute-start(bf16[8,3584]{1,0:T(8,128)(2,1)S(1)} %slice.8), channel_id=1, source_target_pairs={{0,2},{2,0},{4,6},{6,4},{8,10},{10,8},{12,14},{14,12},{16,18},{18,... | collective-permute-start | bytes 172040 | tf_op jit(solution)/shard_map/ppermute | solution.py:327
  19.0 11.9 %collective-permute-start.5 = (bf16[16,3584]{1,0:T(8,128)(2,1)S(1)}, bf16[16,3584]{1,0:T(8,128)(2,1)S(1)}, u32[]{:S(2)}, u32[]{:S(2)}) collective-permute-start(bf16[16,3584]{1,0:T(8,128)(2,1)S(1)} %combine.3.refs_5_), channel_id=1, source_target_pairs={{0,24},{2,26},{4,28},{6,30},{8,16},{10,18},{12,20},{14,22},{16,8},... | collective-permute-start | bytes 344072 | tf_op jit(solution)/shard_map/ppermute | solution.py:327
  21.9 10.5 %collective-permute-start.8 = (bf16[16,3584]{1,0:T(8,128)(2,1)S(1)}, bf16[16,3584]{1,0:T(8,128)(2,1)S(1)}, u32[]{:S(2)}, u32[]{:S(2)}) collective-permute-start(bf16[16,3584]{1,0:T(8,128)(2,1)S(1)} %combine.4.refs_6_), channel_id=1, source_target_pairs={{0,16},{2,18},{4,20},{6,22},{8,24},{10,26},{12,28},{14,30},{16,0},... | collective-permute-start | bytes 344072 | tf_op jit(solution)/shard_map/ppermute | solution.py:327
  23.7 8.7 %collective-permute-start.11 = (bf16[16,3584]{1,0:T(8,128)(2,1)S(1)}, bf16[16,3584]{1,0:T(8,128)(2,1)S(1)}, u32[]{:S(2)}, u32[]{:S(2)}) collective-permute-start(bf16[16,3584]{1,0:T(8,128)(2,1)S(1)} %get-tuple-element.43), channel_id=1, source_target_pairs={{0,8},{2,10},{4,12},{6,14},{8,0},{10,2},{12,4},{14,6},{16,24},{18,... | collective-permute-start | bytes 344072 | tf_op jit(solution)/shard_map/ppermute | solution.py:327
  24.4 6.5 %copy-start.2 = (bf16[16,3584]{1,0:T(8,128)(2,1)S(1)}, bf16[16,3584]{1,0:T(8,128)(2,1)}, u32[]{:S(2)}) copy-start(bf16[16,3584]{1,0:T(8,128)(2,1)} %base_ref.1) | copy-start | bytes 344068
  24.4 9.6 %copy-start.1 = (f32[7168]{0:T(1024)S(1)}, f32[7168]{0:T(1024)}, u32[]{:S(2)}) copy-start(f32[7168]{0:T(1024)} %param.12) | copy-start | bytes 86020
  32.4 6.7 %copy-start = (bf16[16,3584]{1,0:T(8,128)(2,1)}, bf16[16,3584]{1,0:T(8,128)(2,1)S(1)}, u32[]{:S(2)}) copy-start(bf16[16,3584]{1,0:T(8,128)(2,1)S(1)} %add_convert_fusion.refs_2_) | copy-start | bytes 344068
  32.5 4.9 %collective-permute-start.12 = (bf16[16,3584]{1,0:T(8,128)(2,1)S(1)}, bf16[16,3584]{1,0:T(8,128)(2,1)S(1)}, u32[]{:S(2)}, u32[]{:S(2)}) collective-permute-start(bf16[16,3584]{1,0:T(8,128)(2,1)S(1)} %add_convert_fusion.refs_2_), channel_id=1, source_target_pairs={{0,1},{1,0},{2,3},{3,2},{4,5},{5,4},{6,7},{7,6},{8,9},{9,8},{10,11... | collective-permute-start | bytes 344072 | tf_op jit(solution)/shard_map/ppermute | solution.py:381

commit v6 on v5

--- a/solution.py
+++ b/solution.py
@@ -87,7 +87,7 @@
             jnp.bfloat16
         )
     columns = total.shape[1]
-    block = block_width(columns)
+    block = columns // 2 if columns % (2 * LANES) == 0 else block_width(columns)
     for i, copy in enumerate(copies):
         copy.wait()
         if i + AHEAD < steps:
@@ -170,10 +170,13 @@
     tokens = chosen_refs[0].shape[1]
     index = lax.axis_index("expert")
     found = gates_of(index, low, count, capacity, tokens, [ref[...] for ref in chosen_refs])
-    wide = [ref[...].astype(jnp.float32) for ref in row_refs]
-    rows = jnp.concatenate(
-        [rows[begin : begin + count * capacity] for rows, begin in zip(wide, begins)], axis=0
-    ).astype(jnp.bfloat16)
+    picked = []
+    for ref, begin in zip(row_refs, begins):
+        end = begin + count * capacity
+        low_row, high_row = begin // 16 * 16, min(-(-end // 16) * 16, ref.shape[0])
+        wide = ref[low_row:high_row].astype(jnp.float32)
+        picked.append(wide[begin - low_row : end - low_row])
+    rows = jnp.concatenate(picked, axis=0).astype(jnp.bfloat16)
     together = count if count * tokens <= LANES else 1
     for base in range(0, count, together):
         gate = jnp.concatenate(found[base : base + together], axis=0)

time: 39.3 us -> 39.3 us (level)
  no operation moved by 1% of the time
where the time goes in v6:
time: 39.3 us; the launch traced here: 39.1 us
  Pallas kernels  16.7 us (42%)
  starting transfers between devices  16.1 us (41%)
  waiting for transfers between devices  5.4 us (14%)
  between operations  0.79 us (2%)
    ppermute x12, starting transfers between devices, swap(): lax.ppermute(value, 'expert', [(i, i ^ bits) for i in range(experts)])  14.5 us
    pallas_call x1, Pallas kernels, fetch(): pl.pallas_call(fetch_kernel, out_shape=pltpu.VMEM((columns, rows), source...  6.44 us
    pallas_call x1, Pallas kernels, down(): pl.pallas_call(functools.partial(down_kernel, experts, outputs), out_shap...  6.05 us
    ppermute x12, waiting for transfers between devices, swap(): lax.ppermute(value, 'expert', [(i, i ^ bits) for i in range(experts)])  3.3 us
    pallas_call x2, Pallas kernels, project(): pl.pallas_call(functools.partial(project_kernel, flip, block, bool(carrie...  2.98 us
    ppermute x1, waiting for transfers between devices, on_device(): other = lax.ppermute(stream, 'tensor', [(i, i ^ 1) for i in range(tensors)])  2.1 us
    ppermute x1, starting transfers between devices, on_device(): other = lax.ppermute(stream, 'tensor', [(i, i ^ 1) for i in range(tensors)])  1.58 us
    pallas_call x3, Pallas kernels, combine(): pl.pallas_call(functools.partial(combine_kernel, low, count, capacity, be...  1.21 us
  transfers between devices with their start and end apart: 13, of which 4 were waited for; matrix products, arithmetic and copies ran while one was open for 0% of the time, Pallas kernels for 23%

profile of v6, /device:TPU:0, one launch (start us, length us, event | category | flops | bytes accessed | tf_op | source)
XLA Modules:
  0.0 39.1 jit_solution(2448289259576888602)
XLA Ops:
  0.6 0.0 copy-start.3
  0.6 0.0 copy-start.4
  0.7 6.1 %down.1 = (bf16[32,3584]{1,0:T(8,128)(2,1)S(1)}, bf16[32,3584]{1,0:T(8,128)(2,1)S(1)}, bf16[16,3584]{1,0:T(8,128)(2,1)S(1)}, bf16[16,3584]{1,0:T(8,128)(2,1)S(1)...) custom-call(bf16[1,128,2048]{2,1,0:T(8,128)(2,1)} %hidden_hbm.1, bf16[1,2048,3584]{2,1,0:T(8,128)(2,1)} %weight_hbm.1), custom_call_target="tpu_custom_call" | custom-call | flops 1879048192 | bytes 14680064 | tf_op jit(solution)/shard_map/down/pallas_call | solution.py:119
  6.7 0.0 copy-done.4
  6.7 0.0 copy-done.3
  6.8 3.1 %collective-permute-start = (f32[16,16]{1,0:T(8,128)S(1)}, f32[16,16]{1,0:T(8,128)S(1)}, u32[]{:S(2)}, u32[]{:S(2)}) collective-permute-start(f32[16,16]{1,0:T(8,128)S(1)} %pad_maximum_fusion.1.refs_0_), channel_id=1, source_target_pairs={{0,8},{2,10},{4,12},{6,14},{8,0},{10,2},{12,4},{14,6},{16,24},{18,... | collective-permute-start | bytes 3080 | tf_op jit(solution)/shard_map/ppermute | solution.py:330
  9.8 1.5 %collective-permute-start.3 = (bf16[16,3584]{1,0:T(8,128)(2,1)S(1)}, bf16[16,3584]{1,0:T(8,128)(2,1)S(1)}, u32[]{:S(2)}, u32[]{:S(2)}) collective-permute-start(bf16[16,3584]{1,0:T(8,128)(2,1)S(1)} %get-tuple-element.35), channel_id=1, source_target_pairs={{0,4},{2,6},{4,0},{6,2},{8,12},{10,14},{12,8},{14,10},{16,20},{18,... | collective-permute-start | bytes 344072 | tf_op jit(solution)/shard_map/ppermute | solution.py:330
  11.3 0.5 %collective-permute-start.6 = (bf16[16,3584]{1,0:T(8,128)(2,1)S(1)}, bf16[16,3584]{1,0:T(8,128)(2,1)S(1)}, u32[]{:S(2)}, u32[]{:S(2)}) collective-permute-start(bf16[16,3584]{1,0:T(8,128)(2,1)S(1)} %get-tuple-element.39), channel_id=1, source_target_pairs={{0,4},{2,6},{4,0},{6,2},{8,12},{10,14},{12,8},{14,10},{16,20},{18,... | collective-permute-start | bytes 344072 | tf_op jit(solution)/shard_map/ppermute | solution.py:330
  11.9 0.0 collective-permute-start.2
  11.9 0.0 collective-permute-done.refs_1_
  11.9 2.7 %collective-permute-start.1 = (f32[32,16]{1,0:T(8,128)S(1)}, f32[32,16]{1,0:T(8,128)S(1)}, u32[]{:S(2)}, u32[]{:S(2)}) collective-permute-start(f32[32,16]{1,0:T(8,128)S(1)} %pad_maximum_fusion), channel_id=1, source_target_pairs={{0,16},{2,18},{4,20},{6,22},{8,24},{10,26},{12,28},{14,30},{16,0},... | collective-permute-start | bytes 6152 | tf_op jit(solution)/shard_map/ppermute | solution.py:330
  14.5 1.1 %collective-permute-done.3.refs_3_ = bf16[16,3584]{1,0:T(8,128)(2,1)S(1)} collective-permute-done((bf16[16,3584]{1,0:T(8,128)(2,1)S(1)}, bf16[16,3584]{1,0:T(8,128)(2,1)S(1)}, u32[]{:S(2)}, u32[]{:S(2)}) %collective-permute-start.3) | collective-permute-done | bytes 114720 | tf_op jit(solution)/shard_map/ppermute | solution.py:330
  15.7 0.0 collective-permute-start.4
  15.7 1.6 %collective-permute-start.9 = (bf16[16,3584]{1,0:T(8,128)(2,1)S(1)}, bf16[16,3584]{1,0:T(8,128)(2,1)S(1)}, u32[]{:S(2)}, u32[]{:S(2)}) collective-permute-start(bf16[16,3584]{1,0:T(8,128)(2,1)S(1)} %get-tuple-element.40), channel_id=1, source_target_pairs={{0,4},{2,6},{4,0},{6,2},{8,12},{10,14},{12,8},{14,10},{16,20},{18,... | collective-permute-start | bytes 344072 | tf_op jit(solution)/shard_map/ppermute | solution.py:330
  17.2 0.0 collective-permute-done.6.refs_3_
  17.2 0.3 collective-permute-start.10
  17.6 0.0 collective-permute-done.1
  17.6 1.0 %collective-permute-start.7 = (bf16[8,3584]{1,0:T(8,128)(2,1)S(1)}, bf16[8,3584]{1,0:T(8,128)(2,1)S(1)}, u32[]{:S(2)}, u32[]{:S(2)}) collective-permute-start(bf16[8,3584]{1,0:T(8,128)(2,1)S(1)} %slice.8), channel_id=1, source_target_pairs={{0,2},{2,0},{4,6},{6,4},{8,10},{10,8},{12,14},{14,12},{16,18},{18,... | collective-permute-start | bytes 172040 | tf_op jit(solution)/shard_map/ppermute | solution.py:330
  18.6 0.0 collective-permute-done.4.refs_4_
  18.6 0.0 collective-permute-done.2.refs_2_.refs_3_
  18.6 0.4 combine.3.refs_5_
  19.0 2.5 %collective-permute-start.5 = (bf16[16,3584]{1,0:T(8,128)(2,1)S(1)}, bf16[16,3584]{1,0:T(8,128)(2,1)S(1)}, u32[]{:S(2)}, u32[]{:S(2)}) collective-permute-start(bf16[16,3584]{1,0:T(8,128)(2,1)S(1)} %combine.3.refs_5_), channel_id=1, source_target_pairs={{0,24},{2,26},{4,28},{6,30},{8,16},{10,18},{12,20},{14,22},{16,8},... | collective-permute-start | bytes 344072 | tf_op jit(solution)/shard_map/ppermute | solution.py:330
  21.5 0.0 collective-permute-done.7.refs_4_
  21.5 0.4 combine.4.refs_6_
  21.9 0.6 %collective-permute-start.8 = (bf16[16,3584]{1,0:T(8,128)(2,1)S(1)}, bf16[16,3584]{1,0:T(8,128)(2,1)S(1)}, u32[]{:S(2)}, u32[]{:S(2)}) collective-permute-start(bf16[16,3584]{1,0:T(8,128)(2,1)S(1)} %combine.4.refs_6_), channel_id=1, source_target_pairs={{0,16},{2,18},{4,20},{6,22},{8,24},{10,26},{12,28},{14,30},{16,0},... | collective-permute-start | bytes 344072 | tf_op jit(solution)/shard_map/ppermute | solution.py:330
  22.5 0.0 collective-permute-done.9.refs_4_
  22.5 0.7 %collective-permute-done.10.refs_5_ = bf16[16,3584]{1,0:T(8,128)(2,1)S(1)} collective-permute-done((bf16[16,3584]{1,0:T(8,128)(2,1)S(1)}, bf16[16,3584]{1,0:T(8,128)(2,1)S(1)}, u32[]{:S(2)}, u32[]{:S(2)}) %collective-permute-start.10) | collective-permute-done | bytes 114720 | tf_op jit(solution)/shard_map/ppermute | solution.py:330
  23.2 0.5 %combine.5 = (bf16[16,3584]{1,0:T(8,128)(2,1)S(1)}, bf16[16,3584]{1,0:T(8,128)(2,1)S(1)}) custom-call(f32[16,16]{1,0:T(8,128)S(1)} %pad_maximum_fusion.1.refs_0_, f32[16,16]{1,0:T(8,128)S(1)} %collective-permute-done.refs_1_, bf16[32,3584]{1,0:T(8,128)(2,1)S(1)} %get-tuple-element.33.refs_1_.refs_2_, ...), custom_call_target="tpu_custom_call" | custom-call | flops 58720256 | bytes 458752 | tf_op jit(solution)/shard_map/combine/pallas_call | solution.py:198
  23.7 0.7 %collective-permute-start.11 = (bf16[16,3584]{1,0:T(8,128)(2,1)S(1)}, bf16[16,3584]{1,0:T(8,128)(2,1)S(1)}, u32[]{:S(2)}, u32[]{:S(2)}) collective-permute-start(bf16[16,3584]{1,0:T(8,128)(2,1)S(1)} %get-tuple-element.43), channel_id=1, source_target_pairs={{0,8},{2,10},{4,12},{6,14},{8,0},{10,2},{12,4},{14,6},{16,24},{18,... | collective-permute-start | bytes 344072 | tf_op jit(solution)/shard_map/ppermute | solution.py:330
  24.4 0.0 copy-start.2
  24.4 0.0 copy-start.1
  24.4 6.4 %fetch.1.refs_1_ = bf16[7168,1056]{1,0:T(8,128)(2,1)S(1)} custom-call(bf16[1056,7168]{1,0:T(8,128)(2,1)} %bitcast.7, bf16[16,3584]{1,0:T(8,128)(2,1)S(1)} %get-tuple-element.42.after_ref), custom_call_target="tpu_custom_call" | custom-call | bytes 15138816 | tf_op jit(solution)/shard_map/fetch/pallas_call | solution.py:252
  30.9 0.0 collective-permute-done.5.refs_0_
  30.9 0.0 copy-done.2
  30.9 1.4 %collective-permute-done.8.refs_0_ = bf16[16,3584]{1,0:T(8,128)(2,1)S(1)} collective-permute-done((bf16[16,3584]{1,0:T(8,128)(2,1)S(1)}, bf16[16,3584]{1,0:T(8,128)(2,1)S(1)}, u32[]{:S(2)}, u32[]{:S(2)}) %collective-permute-start.8) | collective-permute-done | bytes 114720 | tf_op jit(solution)/shard_map/ppermute | solution.py:330
  32.4 0.0 collective-permute-done.11
  32.4 0.0 copy-start
  32.5 1.6 %collective-permute-start.12 = (bf16[16,3584]{1,0:T(8,128)(2,1)S(1)}, bf16[16,3584]{1,0:T(8,128)(2,1)S(1)}, u32[]{:S(2)}, u32[]{:S(2)}) collective-permute-start(bf16[16,3584]{1,0:T(8,128)(2,1)S(1)} %add_convert_fusion.refs_2_), channel_id=1, source_target_pairs={{0,1},{1,0},{2,3},{3,2},{4,5},{5,4},{6,7},{7,6},{8,9},{9,8},{10,11... | collective-permute-start | bytes 344072 | tf_op jit(solution)/shard_map/ppermute | solution.py:384
  34.0 0.0 copy-done.1
  34.0 1.2 %project.2 = (f32[16,1056]{1,0:T(8,128)S(1)}, f32[16,1]{1,0:T(8,128)S(1)}) custom-call(f32[1,7168]{1,0:T(1,128)S(1)} %bitcast.5, bf16[7168,1056]{1,0:T(8,128)(2,1)S(1)} %fetch.1.refs_1_, bf16[16,3584]{1,0:T(8,128)(2,1)S(1)} %add_convert_fusion.refs_2_), custom_call_target="tpu_custom_call" | custom-call | flops 3875536896 | tf_op jit(solution)/shard_map/project/pallas_call | solution.py:307
  35.2 2.1 %collective-permute-done.12.refs_2_ = bf16[16,3584]{1,0:T(8,128)(2,1)S(1)} collective-permute-done((bf16[16,3584]{1,0:T(8,128)(2,1)S(1)}, bf16[16,3584]{1,0:T(8,128)(2,1)S(1)}, u32[]{:S(2)}, u32[]{:S(2)}) %collective-permute-start.12) | collective-permute-done | bytes 114720 | tf_op jit(solution)/shard_map/ppermute | solution.py:384
  37.3 1.8 %project.3 = bf16[16,1056]{1,0:T(8,128)(2,1)} custom-call(f32[1,7168]{1,0:T(1,128)S(1)} %bitcast.6, bf16[7168,1056]{1,0:T(8,128)(2,1)S(1)} %fetch.1.refs_1_, bf16[16,3584]{1,0:T(8,128)(2,1)S(1)} %collective-permute-done.12.refs_2_, f32[16,1056]{1,0:T(8,128)S(1)} %get-tuple-element.46.refs_3_, f32[16,1]{1,0:T(8,128)S(1)} %get-tuple-element.47.refs_4_), custom_call_target="tpu_custom_call" | custom-call | flops 3875536896 | tf_op jit(solution)/shard_map/project/pallas_call | solution.py:307
  39.1 0.0 copy-done
  (9 shorter events, 0.1 us)
Async XLA Ops:
  0.6 6.1 %copy-start.3 = (f32[16,8]{0,1:T(8,128)S(1)}, f32[16,8]{0,1:T(8,128)}, u32[]{:S(2)}) copy-start(f32[16,8]{0,1:T(8,128)} %param.10) | copy-start | bytes 1540
  0.6 6.1 %copy-start.4 = (s32[16,8]{0,1:T(8,128)S(1)}, s32[16,8]{0,1:T(8,128)}, u32[]{:S(2)}) copy-start(s32[16,8]{0,1:T(8,128)} %param.9) | copy-start | bytes 1540
  6.8 5.1 %collective-permute-start = (f32[16,16]{1,0:T(8,128)S(1)}, f32[16,16]{1,0:T(8,128)S(1)}, u32[]{:S(2)}, u32[]{:S(2)}) collective-permute-start(f32[16,16]{1,0:T(8,128)S(1)} %pad_maximum_fusion.1.refs_0_), channel_id=1, source_target_pairs={{0,8},{2,10},{4,12},{6,14},{8,0},{10,2},{12,4},{14,6},{16,24},{18,... | collective-permute-start | bytes 3080 | tf_op jit(solution)/shard_map/ppermute | solution.py:330
  9.8 5.8 %collective-permute-start.3 = (bf16[16,3584]{1,0:T(8,128)(2,1)S(1)}, bf16[16,3584]{1,0:T(8,128)(2,1)S(1)}, u32[]{:S(2)}, u32[]{:S(2)}) collective-permute-start(bf16[16,3584]{1,0:T(8,128)(2,1)S(1)} %get-tuple-element.35), channel_id=1, source_target_pairs={{0,4},{2,6},{4,0},{6,2},{8,12},{10,14},{12,8},{14,10},{16,20},{18,... | collective-permute-start | bytes 344072 | tf_op jit(solution)/shard_map/ppermute | solution.py:330
  11.3 5.9 %collective-permute-start.6 = (bf16[16,3584]{1,0:T(8,128)(2,1)S(1)}, bf16[16,3584]{1,0:T(8,128)(2,1)S(1)}, u32[]{:S(2)}, u32[]{:S(2)}) collective-permute-start(bf16[16,3584]{1,0:T(8,128)(2,1)S(1)} %get-tuple-element.39), channel_id=1, source_target_pairs={{0,4},{2,6},{4,0},{6,2},{8,12},{10,14},{12,8},{14,10},{16,20},{18,... | collective-permute-start | bytes 344072 | tf_op jit(solution)/shard_map/ppermute | solution.py:330
  11.9 6.7 %collective-permute-start.2 = (bf16[32,3584]{1,0:T(8,128)(2,1)S(1)}, bf16[32,3584]{1,0:T(8,128)(2,1)S(1)}, u32[]{:S(2)}, u32[]{:S(2)}) collective-permute-start(bf16[32,3584]{1,0:T(8,128)(2,1)S(1)} %get-tuple-element.34), channel_id=1, source_target_pairs={{0,2},{2,0},{4,6},{6,4},{8,10},{10,8},{12,14},{14,12},{16,18},{18,... | collective-permute-start | bytes 688136 | tf_op jit(solution)/shard_map/ppermute | solution.py:330
  11.9 5.7 %collective-permute-start.1 = (f32[32,16]{1,0:T(8,128)S(1)}, f32[32,16]{1,0:T(8,128)S(1)}, u32[]{:S(2)}, u32[]{:S(2)}) collective-permute-start(f32[32,16]{1,0:T(8,128)S(1)} %pad_maximum_fusion), channel_id=1, source_target_pairs={{0,16},{2,18},{4,20},{6,22},{8,24},{10,26},{12,28},{14,30},{16,0},... | collective-permute-start | bytes 6152 | tf_op jit(solution)/shard_map/ppermute | solution.py:330
  15.7 2.9 %collective-permute-start.4 = (bf16[8,3584]{1,0:T(8,128)(2,1)S(1)}, bf16[8,3584]{1,0:T(8,128)(2,1)S(1)}, u32[]{:S(2)}, u32[]{:S(2)}) collective-permute-start(bf16[8,3584]{1,0:T(8,128)(2,1)S(1)} %slice.6), channel_id=1, source_target_pairs={{0,2},{2,0},{4,6},{6,4},{8,10},{10,8},{12,14},{14,12},{16,18},{18,... | collective-permute-start | bytes 172040 | tf_op jit(solution)/shard_map/ppermute | solution.py:330
  15.7 6.8 %collective-permute-start.9 = (bf16[16,3584]{1,0:T(8,128)(2,1)S(1)}, bf16[16,3584]{1,0:T(8,128)(2,1)S(1)}, u32[]{:S(2)}, u32[]{:S(2)}) collective-permute-start(bf16[16,3584]{1,0:T(8,128)(2,1)S(1)} %get-tuple-element.40), channel_id=1, source_target_pairs={{0,4},{2,6},{4,0},{6,2},{8,12},{10,14},{12,8},{14,10},{16,20},{18,... | collective-permute-start | bytes 344072 | tf_op jit(solution)/shard_map/ppermute | solution.py:330
  17.2 6.0 %collective-permute-start.10 = (bf16[16,3584]{1,0:T(8,128)(2,1)S(1)}, bf16[16,3584]{1,0:T(8,128)(2,1)S(1)}, u32[]{:S(2)}, u32[]{:S(2)}) collective-permute-start(bf16[16,3584]{1,0:T(8,128)(2,1)S(1)} %get-tuple-element.41), channel_id=1, source_target_pairs={{0,6},{2,4},{4,2},{6,0},{8,14},{10,12},{12,10},{14,8},{16,22},{18,... | collective-permute-start | bytes 344072 | tf_op jit(solution)/shard_map/ppermute | solution.py:330
  17.6 4.0 %collective-permute-start.7 = (bf16[8,3584]{1,0:T(8,128)(2,1)S(1)}, bf16[8,3584]{1,0:T(8,128)(2,1)S(1)}, u32[]{:S(2)}, u32[]{:S(2)}) collective-permute-start(bf16[8,3584]{1,0:T(8,128)(2,1)S(1)} %slice.8), channel_id=1, source_target_pairs={{0,2},{2,0},{4,6},{6,4},{8,10},{10,8},{12,14},{14,12},{16,18},{18,... | collective-permute-start | bytes 172040 | tf_op jit(solution)/shard_map/ppermute | solution.py:330
  19.0 11.9 %collective-permute-start.5 = (bf16[16,3584]{1,0:T(8,128)(2,1)S(1)}, bf16[16,3584]{1,0:T(8,128)(2,1)S(1)}, u32[]{:S(2)}, u32[]{:S(2)}) collective-permute-start(bf16[16,3584]{1,0:T(8,128)(2,1)S(1)} %combine.3.refs_5_), channel_id=1, source_target_pairs={{0,24},{2,26},{4,28},{6,30},{8,16},{10,18},{12,20},{14,22},{16,8},... | collective-permute-start | bytes 344072 | tf_op jit(solution)/shard_map/ppermute | solution.py:330
  21.9 10.5 %collective-permute-start.8 = (bf16[16,3584]{1,0:T(8,128)(2,1)S(1)}, bf16[16,3584]{1,0:T(8,128)(2,1)S(1)}, u32[]{:S(2)}, u32[]{:S(2)}) collective-permute-start(bf16[16,3584]{1,0:T(8,128)(2,1)S(1)} %combine.4.refs_6_), channel_id=1, source_target_pairs={{0,16},{2,18},{4,20},{6,22},{8,24},{10,26},{12,28},{14,30},{16,0},... | collective-permute-start | bytes 344072 | tf_op jit(solution)/shard_map/ppermute | solution.py:330
  23.7 8.7 %collective-permute-start.11 = (bf16[16,3584]{1,0:T(8,128)(2,1)S(1)}, bf16[16,3584]{1,0:T(8,128)(2,1)S(1)}, u32[]{:S(2)}, u32[]{:S(2)}) collective-permute-start(bf16[16,3584]{1,0:T(8,128)(2,1)S(1)} %get-tuple-element.43), channel_id=1, source_target_pairs={{0,8},{2,10},{4,12},{6,14},{8,0},{10,2},{12,4},{14,6},{16,24},{18,... | collective-permute-start | bytes 344072 | tf_op jit(solution)/shard_map/ppermute | solution.py:330
  24.4 6.5 %copy-start.2 = (bf16[16,3584]{1,0:T(8,128)(2,1)S(1)}, bf16[16,3584]{1,0:T(8,128)(2,1)}, u32[]{:S(2)}) copy-start(bf16[16,3584]{1,0:T(8,128)(2,1)} %base_ref.1) | copy-start | bytes 344068
  24.4 9.6 %copy-start.1 = (f32[7168]{0:T(1024)S(1)}, f32[7168]{0:T(1024)}, u32[]{:S(2)}) copy-start(f32[7168]{0:T(1024)} %param.12) | copy-start | bytes 86020
  32.4 6.7 %copy-start = (bf16[16,3584]{1,0:T(8,128)(2,1)}, bf16[16,3584]{1,0:T(8,128)(2,1)S(1)}, u32[]{:S(2)}) copy-start(bf16[16,3584]{1,0:T(8,128)(2,1)S(1)} %add_convert_fusion.refs_2_) | copy-start | bytes 344068
  32.5 4.9 %collective-permute-start.12 = (bf16[16,3584]{1,0:T(8,128)(2,1)S(1)}, bf16[16,3584]{1,0:T(8,128)(2,1)S(1)}, u32[]{:S(2)}, u32[]{:S(2)}) collective-permute-start(bf16[16,3584]{1,0:T(8,128)(2,1)S(1)} %add_convert_fusion.refs_2_), channel_id=1, source_target_pairs={{0,1},{1,0},{2,3},{3,2},{4,5},{5,4},{6,7},{7,6},{8,9},{9,8},{10,11... | collective-permute-start | bytes 344072 | tf_op jit(solution)/shard_map/ppermute | solution.py:384
